TPU v7x, 32 devices: a whole 2x2x4 slice. The times are simulated.
32 devices in a mesh: lat: 4 (over y, x), lon: 8 (over z, core).
Axes of the slice: x: 2, y: 2, z: 4, core: 2. Of those that a mesh axis runs over, the one named last changes fastest.
Arguments:
- queries: float32 [16, 256, 512], P('lat', 'lon'), may hold values from -80 to 80
- key_rows: float32 [32, 512], P(('lat', 'lon')), may hold values from -8 to 8
- value_rows: float32 [32, 512], P(('lat', 'lon')), may hold values from -6 to 6
- cotangent: float32 [16, 256, 512], P('lat', 'lon'), may hold values from -25 to 25
- conv_taps: float32 [9, 512], replicated, may hold values from -1.75 to 1.75
Outputs:
- query_grad: float32 [16, 256, 512], P('lat', 'lon')
- key_grad: float32 [32, 512], P(('lat', 'lon'))
- value_grad: float32 [32, 512], P(('lat', 'lon'))
- tap_update: float32 [9, 512], replicated
All inputs are finite; a program needn't handle non-finite values.
Results may differ from a plain program's by a relative error of at most 0.0003.
Values sent between devices are 32-bit elements; how exact they have to be, the bound alone decides.
No kernel may reach another device: no remote copies, remote signals or barrier semaphores. Data moves between devices by JAX's collectives and lax.ppermute only.
A program may use at most 64 MiB of HBM per device.

v0:
```python
import jax
import jax.numpy as jnp
from jax import lax
from jax.sharding import PartitionSpec as P

HD = 64


HIGH = lax.Precision.HIGHEST
OFFSETS = ((-1, -1), (-1, 0), (-1, 1), (0, -1), (0, 0), (0, 1), (1, -1), (1, 0), (1, 1))


def extended(value, sides, width):
    for axis, dim in sides:
        peers, length = (lax.axis_size(axis), value.shape[dim])
        up = [(i, (i + 1) % peers) for i in range(peers)]
        down = [(j, i) for i, j in up]
        last = lax.slice_in_dim(value, length - width, length, axis=dim)
        initial = lax.slice_in_dim(value, 0, width, axis=dim)
        before = lax.ppermute(last, axis, up)
        after = lax.ppermute(initial, axis, down)
        value = jnp.concatenate([before, value, after], axis=dim)
    return value


def split_heads(matrix):
    return matrix.reshape(matrix.shape[0], -1, HD)


def latitude_weights(row_count, band_index, band_count):
    line_total = row_count * band_count
    centres = (jnp.arange(line_total, dtype=jnp.float32) + 0.5) * (jnp.pi / line_total)
    mean_cosine = jnp.sum(jnp.sin(centres)) / line_total
    mine = (band_index * row_count + jnp.arange(row_count, dtype=jnp.int32)).astype(jnp.float32)
    return jnp.sin((mine + 0.5) * (jnp.pi / line_total)) / mean_cosine


def close_poles(padded, row_dim, band_index, band_count):
    height = padded.shape[row_dim]
    positions = jnp.arange(height)
    outside = (positions == 0) & (band_index == 0) | (positions == height - 1) & (
        band_index == band_count - 1
    )
    shape_mask = [1] * padded.ndim
    shape_mask[row_dim] = height
    return jnp.where(outside.reshape(shape_mask), 0.0, padded)


def spread_taps(weighted, grad_padded, conv_taps):
    row_count, col_count = (weighted.shape[0], weighted.shape[1])
    result = weighted
    for tap_index, (shift_row, shift_col) in enumerate(OFFSETS):
        result = (
            result
            + conv_taps[tap_index]
            * grad_padded[
                1 - shift_row : 1 - shift_row + row_count, 1 - shift_col : 1 - shift_col + col_count
            ]
        )
    return result


def tap_terms(weighted, out_padded):
    row_count, col_count = (weighted.shape[0], weighted.shape[1])
    term_list = []
    for shift_row, shift_col in OFFSETS:
        term_list.append(
            jnp.sum(
                out_padded[
                    1 + shift_row : 1 + shift_row + row_count,
                    1 + shift_col : 1 + shift_col + col_count,
                ]
                * weighted,
                axis=(0, 1),
            )
        )
    return jnp.stack(term_list)


def group_logits(query_part, key_part):
    return jnp.einsum(
        "qhd,khd->hqk", split_heads(query_part), split_heads(key_part), precision=HIGH
    ) * HD ** (-0.5)


def body(queries, key_rows, value_rows, cotangent, conv_taps):
    row_count, col_count, channels = queries.shape
    band_count = lax.axis_size("lat")
    band_index = lax.axis_index("lat")
    weighted = cotangent * latitude_weights(row_count, band_index, band_count)[:, None, None]
    paired_rows = jnp.concatenate([key_rows, value_rows], 1)
    paired_all = lax.all_gather(paired_rows, ("lat", "lon"), axis=0, tiled=True)
    key_all = paired_all[:, :channels]
    value_all = paired_all[:, channels:]
    token_count = row_count * col_count
    key_count = key_all.shape[0]
    query_flat = queries.reshape(token_count, channels)
    group_width = 2 * HD
    group_count = channels // group_width
    outputs = []
    peaks = []
    sums_soft = []
    for group_index in range(group_count):
        col_start = group_index * group_width
        col_stop = col_start + group_width
        logits = group_logits(query_flat[:, col_start:col_stop], key_all[:, col_start:col_stop])
        row_peak = jnp.max(logits, -1, keepdims=True)
        raised = jnp.exp(logits - row_peak)
        normaliser = jnp.sum(raised, -1, keepdims=True)
        soft_weights = raised / normaliser
        outputs.append(
            jnp.einsum(
                "hqk,khd->qhd",
                soft_weights,
                split_heads(value_all[:, col_start:col_stop]),
                precision=HIGH,
            ).reshape(token_count, group_width)
        )
        peaks.append(row_peak)
        sums_soft.append(normaliser)
    out_flat = jnp.concatenate(outputs, 1)
    out_grid = out_flat.reshape(row_count, col_count, channels)
    both_padded = close_poles(
        extended(jnp.stack([weighted, out_grid]), (("lat", 1), ("lon", 2)), 1),
        1,
        band_index,
        band_count,
    )
    grad_padded = both_padded[0]
    out_padded = both_padded[1]
    out_grad = spread_taps(weighted, grad_padded, conv_taps)
    tap_sum = lax.psum(tap_terms(weighted, out_padded), ("lat", "lon"))
    tap_update = tap_sum / jnp.sqrt(jnp.mean(tap_sum * tap_sum) + 1e-06)
    grad_flat = out_grad.reshape(token_count, channels)
    query_parts = []
    key_parts = []
    value_parts = []
    for group_index in range(group_count):
        col_start = group_index * group_width
        col_stop = col_start + group_width
        query_heads = split_heads(query_flat[:, col_start:col_stop])
        key_heads = split_heads(key_all[:, col_start:col_stop])
        logits = jnp.einsum("qhd,khd->hqk", query_heads, key_heads, precision=HIGH) * HD ** (-0.5)
        soft_weights = jnp.exp(logits - peaks[group_index]) / sums_soft[group_index]
        grad_heads = split_heads(grad_flat[:, col_start:col_stop])
        value_parts.append(
            jnp.einsum("hqk,qhd->khd", soft_weights, grad_heads, precision=HIGH).reshape(
                key_count, group_width
            )
        )
        prob_grad = jnp.einsum(
            "qhd,khd->hqk",
            grad_heads,
            split_heads(value_all[:, col_start:col_stop]),
            precision=HIGH,
        )
        row_dot = jnp.transpose(
            jnp.sum(grad_heads * split_heads(out_flat[:, col_start:col_stop]), -1)
        )[:, :, None]
        logit_grad = soft_weights * (prob_grad - row_dot)
        query_parts.append(
            (
                jnp.einsum("hqk,khd->qhd", logit_grad, key_heads, precision=HIGH) * HD ** (-0.5)
            ).reshape(token_count, group_width)
        )
        key_parts.append(
            (
                jnp.einsum("hqk,qhd->khd", logit_grad, query_heads, precision=HIGH) * HD ** (-0.5)
            ).reshape(key_count, group_width)
        )
    paired_terms = jnp.concatenate(key_parts + value_parts, 1)
    paired_band = lax.psum_scatter(paired_terms, "lat", scatter_dimension=0, tiled=True)
    paired_grad = lax.psum_scatter(paired_band, "lon", scatter_dimension=0, tiled=True)
    key_grad = paired_grad[:, :channels]
    value_grad = paired_grad[:, channels:]
    query_grad = jnp.concatenate(query_parts, 1).reshape(row_count, col_count, channels)
    return (query_grad, key_grad, value_grad, tap_update)


def solution(mesh):
    placed = (
        P("lat", "lon", None),
        P(("lat", "lon"), None),
        P(("lat", "lon"), None),
        P("lat", "lon", None),
        P(),
    )
    return jax.shard_map(
        body,
        mesh=mesh,
        in_specs=placed,
        out_specs=(P("lat", "lon", None), P(("lat", "lon"), None), P(("lat", "lon"), None), P()),
        check_vma=False,
    )
```

profile of v0, /device:TPU:0, one launch (start us, length us, event | category | flops | bytes accessed | tf_op | source)
XLA Modules:
  0.0 199.0 jit_solution(11398560798238135702)
XLA Ops:
  7.2 0.7 sine_reduce_fusion
  7.9 0.7 maximum_bitcast_fusion
  8.6 43.7 %all-gather = f32[32,1,1024]{2,1,0:T(1,128)S(1)} all-gather(f32[1,1,1024]{2,1,0:T(1,128)S(1)} %maximum_bitcast_fusion), channel_id=1, replica_groups=mesh['lat'=4,'lon'=8] {'lat','lon'}, dimensions={0}, use_global_device_ids=true | all-gather | bytes 135168 | tf_op jit(solution)/shard_map/all_gather | solution.py:92
  52.4 0.8 copy-done.1
  58.4 2.9 %collective-permute-start.1 = (f32[2,1,32,512]{3,2,1,0:T(8,128)S(1)}, f32[2,1,32,512]{3,2,1,0:T(8,128)S(1)}, u32[]{:S(2)}, u32[]{:S(2)}) collective-permute-start(f32[2,1,32,512]{3,2,1,0:T(8,128)S(1)} %get-tuple-element.18), channel_id=1, source_target_pairs={{8,0},{16,8},{24,16},{0,24},{9,1},{17,9},{25,17},{1,25},{10,2},{18... | collective-permute-start | bytes 393224 | tf_op jit(solution)/shard_map/ppermute | solution.py:21
  61.3 4.3 %collective-permute-done = f32[2,1,32,512]{3,2,1,0:T(8,128)S(1)} collective-permute-done((f32[2,1,32,512]{3,2,1,0:T(8,128)S(1)}, f32[2,1,32,512]{3,2,1,0:T(8,128)S(1)}, u32[]{:S(2)}, u32[]{:S(2)}) %collective-permute-start) | collective-permute-done | bytes 131104 | tf_op jit(solution)/shard_map/ppermute | solution.py:20
  65.6 1.3 collective-permute-done.1
  66.9 3.5 %collective-permute-start.3 = (f32[2,6,1,512]{3,2,1,0:T(1,128)S(1)}, f32[2,6,1,512]{3,2,1,0:T(1,128)S(1)}, u32[]{:S(2)}, u32[]{:S(2)}) collective-permute-start(f32[2,6,1,512]{3,2,1,0:T(1,128)S(1)} %get-tuple-element.16), channel_id=1, source_target_pairs={{1,0},{2,1},{3,2},{4,3},{5,4},{6,5},{7,6},{0,7},{9,8},{10,9},{11,1... | collective-permute-start | bytes 73736 | tf_op jit(solution)/shard_map/ppermute | solution.py:21
  70.5 0.7 copy-done.6
  71.1 0.6 dynamic-slice
  71.8 0.6 dynamic-slice.2
  74.5 0.3 fusion.3
  75.5 0.3 fusion.2
  76.6 0.3 fusion.1
  78.0 0.3 fusion.16
  78.4 37.8 %psum.7 = f32[9,512]{1,0:T(8,128)S(1)} all-reduce(f32[9,512]{1,0:T(8,128)S(1)} %stack.47), channel_id=1, replica_groups=mesh['lat'=4,'lon'=8] {'lat','lon'}, use_global_device_ids=true, to_apply=%region_24.25 | all-reduce | flops 4608 | bytes 36864 | tf_op jit(solution)/shard_map/psum | solution.py:132
  116.1 0.6 multiply_reduce_fusion.4
  118.5 0.6 copy-done.2
  119.1 0.6 broadcast_divide_fusion
  120.8 0.7 pad_maximum_fusion
  121.5 40.5 %all-reduce.4.cloned.1.call-done = f32[32,1024]{1,0:T(8,128)} async-done(((f32[32,1024]{1,0:T(8,128)}), f32[32,1024]{1,0:T(8,128)}) %all-reduce.4.cloned.1.call-update) | async-done | bytes 131088
  162.0 0.8 constant_dynamic-slice_fusion.1
  162.8 28.1 %all-reduce.1 = f32[8,1024]{1,0:T(8,128)S(1)} all-reduce(f32[8,1024]{1,0:T(8,128)S(1)} %constant_dynamic-slice_fusion.1), channel_id=3, replica_groups=mesh['lat'=4,'lon'=8] {'lon'}, use_global_device_ids=true, to_apply=%region_14.15.clone | all-reduce | flops 8192 | bytes 65536
  190.9 1.3 fusion.70
  (116 shorter events, 10.4 us)
Async XLA Ops:
  7.2 0.7 copy-start.4
  7.2 154.9 %all-reduce.4.cloned.1.call-start = ((), (), s32[]{:S(2)}) async-start(), calls=%async_computation | async-start | bytes 262144
  52.3 0.9 copy-start.1
  56.9 1.3 copy-start
  58.2 3.0 %copy-start.3 = (f32[9,512]{1,0:T(8,128)S(1)}, f32[9,512]{1,0:T(8,128)}, u32[]{:S(2)}) copy-start(f32[9,512]{1,0:T(8,128)} %param.9) | copy-start | bytes 55300
  58.3 7.3 %collective-permute-start = (f32[2,1,32,512]{3,2,1,0:T(8,128)S(1)}, f32[2,1,32,512]{3,2,1,0:T(8,128)S(1)}, u32[]{:S(2)}, u32[]{:S(2)}) collective-permute-start(f32[2,1,32,512]{3,2,1,0:T(8,128)S(1)} %get-tuple-element.17), channel_id=1, source_target_pairs={{0,8},{8,16},{16,24},{24,0},{1,9},{9,17},{17,25},{25,1},{2,10},{10... | collective-permute-start | bytes 393224 | tf_op jit(solution)/shard_map/ppermute | solution.py:20
  58.4 8.5 %collective-permute-start.1 = (f32[2,1,32,512]{3,2,1,0:T(8,128)S(1)}, f32[2,1,32,512]{3,2,1,0:T(8,128)S(1)}, u32[]{:S(2)}, u32[]{:S(2)}) collective-permute-start(f32[2,1,32,512]{3,2,1,0:T(8,128)S(1)} %get-tuple-element.18), channel_id=1, source_target_pairs={{8,0},{16,8},{24,16},{0,24},{9,1},{17,9},{25,17},{1,25},{10,2},{18... | collective-permute-start | bytes 393224 | tf_op jit(solution)/shard_map/ppermute | solution.py:21
  66.9 6.2 %collective-permute-start.2 = (f32[2,6,1,512]{3,2,1,0:T(1,128)S(1)}, f32[2,6,1,512]{3,2,1,0:T(1,128)S(1)}, u32[]{:S(2)}, u32[]{:S(2)}) collective-permute-start(f32[2,6,1,512]{3,2,1,0:T(1,128)S(1)} %get-tuple-element.15), channel_id=1, source_target_pairs={{0,1},{1,2},{2,3},{3,4},{4,5},{5,6},{6,7},{7,0},{8,9},{9,10},{10,1... | collective-permute-start | bytes 73736 | tf_op jit(solution)/shard_map/ppermute | solution.py:20
  66.9 6.2 %collective-permute-start.3 = (f32[2,6,1,512]{3,2,1,0:T(1,128)S(1)}, f32[2,6,1,512]{3,2,1,0:T(1,128)S(1)}, u32[]{:S(2)}, u32[]{:S(2)}) collective-permute-start(f32[2,6,1,512]{3,2,1,0:T(1,128)S(1)} %get-tuple-element.16), channel_id=1, source_target_pairs={{1,0},{2,1},{3,2},{4,3},{5,4},{6,5},{7,6},{0,7},{9,8},{10,9},{11,1... | collective-permute-start | bytes 73736 | tf_op jit(solution)/shard_map/ppermute | solution.py:21
  70.5 0.7 copy-start.6
  71.1 0.7 copy-start.5
  118.5 0.7 copy-start.2
Sparse Core Ops, SparseCore 0:
  119.3 42.7 all-reduce.3
where the time goes:
time: 199 us
  blocking collectives  110 us (55%)
  waiting for transfers between devices  46.1 us (23%)
  between operations  16.6 us (8%)
  local copies, waits for them, and re-layouts  9.97 us (5%)
  starting transfers between devices  6.6 us (3%)
  matrix products  5.64 us (3%)
  other arithmetic  4.54 us (2%)
    all_gather x1, blocking collectives, body(): paired_all = lax.all_gather(paired_rows, ('lat', 'lon'), axis=0, tiled=True)  43.7 us
    unnamed x2, waiting for transfers between devices  40.6 us
    psum x1, blocking collectives, body(): tap_sum = lax.psum(tap_terms(weighted, out_padded), ('lat', 'lon'))  37.8 us
    unnamed x1, blocking collectives  28.1 us
    ppermute x2, starting transfers between devices, extended(): after = lax.ppermute(initial, axis, down)  6.44 us
    unnamed x33, local copies, waits for them, and re-layouts  4.94 us
    ppermute x2, waiting for transfers between devices, extended(): before = lax.ppermute(last, axis, up)  4.27 us
  transfers between devices with their start and end apart: 5, of which 3 were waited for; matrix products, arithmetic and copies ran while one was open for 2% of the time, Pallas kernels for 0%

commit v1 on v0

--- a/solution.py
+++ b/solution.py
@@ -1,13 +1,272 @@
+import functools
+
 import jax
 import jax.numpy as jnp
+import numpy as np
 from jax import lax
+from jax.experimental import pallas as pl
+from jax.experimental.pallas import tpu as pltpu
 from jax.sharding import PartitionSpec as P
 
 HD = 64
-
+LANES = 128
+SUBLANES = 8
+VMEM_LIMIT = 16 * 1024 * 1024
 
 HIGH = lax.Precision.HIGHEST
 OFFSETS = ((-1, -1), (-1, 0), (-1, 1), (0, -1), (0, 0), (0, 1), (1, -1), (1, 0), (1, 1))
+
+
+def partner(index, step, peers):
+    if peers & (peers - 1) == 0:
+        return index ^ step
+    return lax.rem(index + step, peers) if not isinstance(index, int) else (index + step) % peers
+
+
+def source(index, step, peers):
+    if peers & (peers - 1) == 0:
+        return index ^ step
+    return lax.rem(index + (peers - step), peers)
+
+
+def exchange(value, step, peers):
+    return lax.ppermute(value, "lat", [(i, partner(i, step, peers)) for i in range(peers)])
+
+
+def round_up(value, multiple):
+    return -(-value // multiple) * multiple
+
+
+def row_weights(line_total):
+    cosine = np.sin((np.arange(line_total, dtype=np.float64) + 0.5) * (np.pi / line_total))
+    return [float(w) for w in cosine / np.mean(cosine)]
+
+
+def vmem_call(kernel, out_shapes, scratch=()):
+    return pl.pallas_call(
+        kernel,
+        out_shape=[jax.ShapeDtypeStruct(s, jnp.float32) for s in out_shapes],
+        scratch_shapes=[pltpu.VMEM(s, jnp.float32) for s in scratch],
+        compiler_params=pltpu.CompilerParams(vmem_limit_bytes=VMEM_LIMIT),
+    )
+
+
+def rows_kernel(bands, sectors, width, key_ref, value_ref, first_ref, last_ref, out_ref):
+    sector = lax.axis_index("lon")
+    rows = first_ref.shape[0]
+    keys = key_ref.shape[0]
+    for band in range(bands):
+        lanes = slice(band * width, (band + 1) * width)
+        key = key_ref[:, lanes]
+        value = value_ref[:, lanes]
+        first = first_ref[:, lanes]
+        last = last_ref[:, lanes]
+        for other in range(sectors):
+            device = band * sectors + other
+            is_next = lax.rem(other - sector + sectors, sectors) == 1
+            out_ref[device, 0:keys, :] = key
+            out_ref[device, keys : 2 * keys, :] = value
+            out_ref[device, 2 * keys : 2 * keys + rows, :] = jnp.where(is_next, last, first)
+
+
+def tokens_kernel(bands, width, query_ref, cotangent_ref, *out_refs):
+    band = lax.axis_index("lat")
+    for step, out_ref in enumerate(out_refs):
+        lanes = pl.ds(pl.multiple_of(partner(band, step, bands) * width, width), width)
+        out_ref[0] = query_ref[:, :, lanes]
+        out_ref[1] = cotangent_ref[:, :, lanes]
+
+
+def heads_of(matrix, width):
+    lane = lax.broadcasted_iota(jnp.int32, matrix.shape, 1)
+    return jnp.concatenate(
+        [
+            jnp.where((lane >= h * HD) & (lane < (h + 1) * HD), matrix, 0.0)
+            for h in range(width // HD)
+        ],
+        0,
+    )
+
+
+def own_heads(matrix, width, keys):
+    lane = lax.broadcasted_iota(jnp.int32, (keys, width), 1)
+    result = matrix[0:keys]
+    for h in range(1, width // HD):
+        result = jnp.where(lane >= h * HD, matrix[h * keys : (h + 1) * keys], result)
+    return result
+
+
+def dot(left, right, left_dim, right_dim):
+    return lax.dot_general(
+        left,
+        right,
+        (((left_dim,), (right_dim,)), ((), ())),
+        precision=HIGH,
+        preferred_element_type=jnp.float32,
+    )
+
+
+def attention_kernel(bands, sectors, width, keys, *refs):
+    part_refs = refs[:bands]
+    rows_ref, taps_ref, terms_ref = refs[bands : bands + 3]
+    query_grad_refs = refs[bands + 3 : 2 * bands + 3]
+    query_ref, weighted_ref, grad_ref, out_ref = refs[2 * bands + 3 :]
+    band = lax.axis_index("lat")
+    sector = lax.axis_index("lon")
+    rows, columns = part_refs[0].shape[1:3]
+    lines = rows * bands
+    tokens = lines * columns
+    edge = SUBLANES
+    scale = HD ** (-0.5)
+    weights = row_weights(lines)
+    heads = width // HD
+    key_total = bands * sectors * keys
+
+    for step, part_ref in enumerate(part_refs):
+        start = source(band, step, bands) * rows
+        query_ref[pl.ds(start, rows)] = part_ref[0]
+        weighted_ref[pl.ds(start + 1, rows), edge : edge + columns, :] = part_ref[1]
+    before = lax.rem(sector + sectors - 1, sectors)
+    after = lax.rem(sector + 1, sectors)
+    for line in range(lines):
+        b, r = divmod(line, rows)
+        r = 2 * keys + r
+        inner = weighted_ref[1 + line, edge : edge + columns, :]
+        weighted_ref[1 + line, edge : edge + columns, :] = inner * weights[line]
+        left = rows_ref[b * sectors + before, r : r + 1, :]
+        right = rows_ref[b * sectors + after, r : r + 1, :]
+        weighted_ref[1 + line, edge - 1 : edge, :] = left * weights[line]
+        weighted_ref[1 + line, edge + columns : edge + columns + 1, :] = right * weights[line]
+    zeros = jnp.zeros(weighted_ref.shape[1:], jnp.float32)
+    weighted_ref[0] = zeros
+    weighted_ref[lines + 1] = zeros
+
+    own_lanes = pl.ds(pl.multiple_of(band * width, width), width)
+    taps = [taps_ref[t : t + 1, own_lanes] for t in range(len(OFFSETS))]
+
+    def shifted(line, offset):
+        a, b = offset
+        return weighted_ref[1 + line - a, edge - b : edge - b + columns, :]
+
+    for line in range(lines):
+        total = shifted(line, (0, 0))
+        for tap, offset in zip(taps, OFFSETS):
+            total = total + tap * shifted(line, offset)
+        grad_ref[line] = total
+
+    key_all = rows_ref[:, 0:keys, :].reshape(key_total, width)
+    value_all = rows_ref[:, keys : 2 * keys, :].reshape(key_total, width)
+    key_heads = heads_of(key_all, width)
+    value_heads = heads_of(value_all, width)
+    query = query_ref[...].reshape(tokens, width)
+    grad = grad_ref[...].reshape(tokens, width)
+
+    logits = dot(key_heads, query, 1, 1) * scale
+    prob_list = []
+    for h in range(heads):
+        part = logits[h * key_total : (h + 1) * key_total]
+        raised = jnp.exp(part - jnp.max(part, 0, keepdims=True))
+        prob_list.append(raised / jnp.sum(raised, 0, keepdims=True))
+    probs = jnp.concatenate(prob_list, 0)
+    out_ref[...] = dot(probs, value_heads, 0, 0).reshape(lines, columns, width)
+    prob_grad = dot(value_heads, grad, 1, 1)
+    logit_grad_list = []
+    for h in range(heads):
+        part = prob_grad[h * key_total : (h + 1) * key_total]
+        row_dot = jnp.sum(prob_list[h] * part, 0, keepdims=True)
+        logit_grad_list.append(prob_list[h] * (part - row_dot))
+    logit_grad = jnp.concatenate(logit_grad_list, 0)
+
+    key_grad = own_heads(dot(logit_grad, query, 1, 0), width, key_total) * scale
+    value_grad = own_heads(dot(probs, grad, 1, 0), width, key_total)
+
+    sums = [jnp.zeros((SUBLANES, width), jnp.float32) for _ in OFFSETS]
+    for line in range(lines):
+        out_line = out_ref[line]
+        for t, offset in enumerate(OFFSETS):
+            product = out_line * shifted(line, offset)
+            for c in range(0, columns, SUBLANES):
+                sums[t] = sums[t] + product[c : c + SUBLANES]
+    tap_sum = jnp.concatenate([jnp.sum(s, 0, keepdims=True) for s in sums], 0)
+    used = 2 * keys + len(OFFSETS)
+    filler = jnp.zeros((terms_ref.shape[1] - used, width), jnp.float32)
+    for device in range(bands * sectors):
+        mine = slice(device * keys, (device + 1) * keys)
+        terms_ref[device, 0:keys, :] = key_grad[mine]
+        terms_ref[device, keys : 2 * keys, :] = value_grad[mine]
+        terms_ref[device, 2 * keys : used, :] = tap_sum
+        if terms_ref.shape[1] > used:
+            terms_ref[device, used:, :] = filler
+
+    query_grad = (dot(logit_grad, key_heads, 0, 0) * scale).reshape(lines, columns, width)
+    out_ref[...] = query_grad
+    for step, query_grad_ref in enumerate(query_grad_refs):
+        query_grad_ref[...] = out_ref[pl.ds(partner(band, step, bands) * rows, rows)]
+
+
+def join_kernel(bands, width, *refs):
+    band = lax.axis_index("lat")
+    out_ref = refs[-1]
+    for step, part_ref in enumerate(refs[:-1]):
+        lanes = pl.ds(pl.multiple_of(source(band, step, bands) * width, width), width)
+        out_ref[:, :, lanes] = part_ref[...]
+
+
+def sums_kernel(bands, sectors, width, keys, terms_ref, key_ref, value_ref, taps_ref):
+    used = 2 * keys + len(OFFSETS)
+    total = jnp.zeros((), jnp.float32)
+    parts = []
+    for band in range(bands):
+        lanes = slice(band * width, (band + 1) * width)
+        part = terms_ref[band * sectors]
+        for sector in range(1, sectors):
+            part = part + terms_ref[band * sectors + sector]
+        key_ref[:, lanes] = part[0:keys]
+        value_ref[:, lanes] = part[keys : 2 * keys]
+        parts.append(part[2 * keys : used])
+    tap_sum = jnp.concatenate(parts, 1)
+    mean = jnp.sum(tap_sum * tap_sum, keepdims=True) / (len(OFFSETS) * width * bands)
+    taps_ref[...] = tap_sum / jnp.sqrt(mean + 1e-06)
+
+
+def split_heads_body(queries, key_rows, value_rows, cotangent, conv_taps):
+    rows, columns, channels = queries.shape
+    bands = lax.axis_size("lat")
+    sectors = lax.axis_size("lon")
+    devices = bands * sectors
+    keys = key_rows.shape[0]
+    width = channels // bands
+    lines = rows * bands
+
+    sent_rows = round_up(2 * keys + rows, SUBLANES)
+    (row_blocks,) = vmem_call(
+        functools.partial(rows_kernel, bands, sectors, width), [(devices, sent_rows, width)]
+    )(key_rows, value_rows, cotangent[:, 0, :], cotangent[:, columns - 1, :])
+    row_blocks = lax.all_to_all(row_blocks, ("lat", "lon"), 0, 0, tiled=True)
+
+    parts = vmem_call(
+        functools.partial(tokens_kernel, bands, width), [(2, rows, columns, width)] * bands
+    )(queries, cotangent)
+    parts = [parts[0]] + [exchange(parts[s], s, bands) for s in range(1, bands)]
+
+    sent_terms = round_up(2 * keys + len(OFFSETS), SUBLANES)
+    grid = (lines, columns, width)
+    terms, *grad_parts = vmem_call(
+        functools.partial(attention_kernel, bands, sectors, width, keys),
+        [(devices, sent_terms, width)] + [(rows, columns, width)] * bands,
+        [grid, (lines + 2, columns + 2 * SUBLANES, width), grid, grid],
+    )(*parts, row_blocks, conv_taps)
+
+    terms = lax.all_to_all(terms, ("lat", "lon"), 0, 0, tiled=True)
+    grad_parts = [grad_parts[0]] + [exchange(grad_parts[s], s, bands) for s in range(1, bands)]
+    (query_grad,) = vmem_call(
+        functools.partial(join_kernel, bands, width), [(rows, columns, channels)]
+    )(*grad_parts)
+    key_grad, value_grad, tap_update = vmem_call(
+        functools.partial(sums_kernel, bands, sectors, width, keys),
+        [(keys, channels), (keys, channels), (len(OFFSETS), channels)],
+    )(terms)
+    return (query_grad, key_grad, value_grad, tap_update)
 
 
 def extended(value, sides, width):
@@ -83,7 +342,7 @@
     ) * HD ** (-0.5)
 
 
-def body(queries, key_rows, value_rows, cotangent, conv_taps):
+def whole_rows_body(queries, key_rows, value_rows, cotangent, conv_taps):
     row_count, col_count, channels = queries.shape
     band_count = lax.axis_size("lat")
     band_index = lax.axis_index("lat")
@@ -177,6 +436,15 @@
     return (query_grad, key_grad, value_grad, tap_update)
 
 
+def body(queries, key_rows, value_rows, cotangent, conv_taps):
+    bands = lax.axis_size("lat")
+    sectors = lax.axis_size("lon")
+    columns, channels = queries.shape[1:]
+    if channels % (bands * LANES) == 0 and sectors > 2 and columns % SUBLANES == 0:
+        return split_heads_body(queries, key_rows, value_rows, cotangent, conv_taps)
+    return whole_rows_body(queries, key_rows, value_rows, cotangent, conv_taps)
+
+
 def solution(mesh):
     placed = (
         P("lat", "lon", None),

time: 199 us -> 40.4 us (0.20)
  blocking collectives: 110 us -> 0 us
  waiting for transfers between devices: 46.1 us -> 13.1 us
  between operations: 16.6 us -> 0.71 us
  starting transfers between devices: 6.6 us -> 18.4 us
  local copies, waits for them, and re-layouts: 9.97 us -> 3.25 us
  matrix products: 5.64 us -> 0 us
  Pallas kernels: 0 us -> 4.59 us
  other arithmetic: 4.54 us -> 0 us
    all_gather x1 -> x0, blocking collectives: 43.7 us -> none  [body(): paired_all = lax.all_gather(paired_rows, ('lat', 'lon'), axis=0, tiled=True)]
    unnamed x2 -> x0, waiting for transfers between devices: 40.6 us -> none
    psum x1 -> x0, blocking collectives: 37.8 us -> none  [body(): tap_sum = lax.psum(tap_terms(weighted, out_padded), ('lat', 'lon'))]
    unnamed x1 -> x0, blocking collectives: 28.1 us -> none
    all_to_all x0 -> x2, starting transfers between devices: none -> 11.3 us  [the longest x1 7.3 us: split_heads_body(): row_blocks = lax.all_to_all(row_blocks, ('lat', 'lon'), 0, 0, tiled=True)]
    ppermute x4 -> x6, waiting for transfers between devices: 5.56 us -> 12.2 us  [exchange(): lax.ppermute(value, 'lat', [(i, partner(i, step, peers)) for i in range(p...]
    dot_general x24 -> x0, matrix products: 5.64 us -> none  [the longest x4 1.21 us: body(): jnp.einsum('hqk,khd->qhd', logit_grad, key_heads, precision=HIGH)]
    pallas_call x0 -> x5, Pallas kernels: none -> 4.59 us  [the longest x1 2.33 us: split_heads_body(): vmem_call(functools.partial(attention_kernel, bands, sectors, width, keys...]
  transfers between devices with their start and end apart: 5 -> 8, of which waited for: 3 -> 6; matrix products, arithmetic and copies ran while one was open for 2% -> 0% of each run, Pallas kernels for 0% -> 2%
where the time goes in v1:
time: 40.4 us; the launch traced here: 40.1 us
  starting transfers between devices  18.4 us (46%)
  waiting for transfers between devices  13.1 us (32%)
  Pallas kernels  4.59 us (11%)
  local copies, waits for them, and re-layouts  3.25 us (8%)
  between operations  0.71 us (2%)
    ppermute x6, waiting for transfers between devices, exchange(): lax.ppermute(value, 'lat', [(i, partner(i, step, peers)) for i in range(p...  12.2 us
    all_to_all x1, starting transfers between devices, split_heads_body(): row_blocks = lax.all_to_all(row_blocks, ('lat', 'lon'), 0, 0, tiled=True)  7.3 us
    ppermute x6, starting transfers between devices, exchange(): lax.ppermute(value, 'lat', [(i, partner(i, step, peers)) for i in range(p...  7.11 us
    all_to_all x1, starting transfers between devices, split_heads_body(): terms = lax.all_to_all(terms, ('lat', 'lon'), 0, 0, tiled=True)  4.01 us
    pallas_call x1, Pallas kernels, split_heads_body(): vmem_call(functools.partial(attention_kernel, bands, sectors, width, keys...  2.33 us
    unnamed x10, local copies, waits for them, and re-layouts  2.31 us
    all_to_all x1, waiting for transfers between devices, split_heads_body(): terms = lax.all_to_all(terms, ('lat', 'lon'), 0, 0, tiled=True)  0.97 us
    slice x1, local copies, waits for them, and re-layouts, split_heads_body(): cotangent[:, columns - 1, :]  0.93 us
  transfers between devices with their start and end apart: 8, of which 6 were waited for; matrix products, arithmetic and copies ran while one was open for 0% of the time, Pallas kernels for 2%

profile of v1, /device:TPU:0, one launch (start us, length us, event | category | flops | bytes accessed | tf_op | source)
XLA Modules:
  0.0 40.1 jit_solution(2793058058359626614)
XLA Ops:
  0.6 0.9 %fusion = (f32[4,1,512]{2,1,0:T(1,128)S(1)}, f32[4,1,512]{2,1,0:T(1,128)S(1)}) fusion(f32[4,32,512]{2,1,0:T(8,128)} %cotangent_ref.1), kind=kLoop, calls=%fused_computation.2 | loop fusion | bytes 32768 | tf_op jit(solution)/shard_map/slice | solution.py:244
  1.6 0.0 copy-start.3
  1.6 0.7 %copy-done.3 = f32[1,512]{1,0:T(1,128)S(1)} copy-done((f32[1,512]{1,0:T(1,128)S(1)}, f32[1,512]{1,0:T(1,128)}, u32[]{:S(2)}) %copy-start.3) | copy-done | bytes 2072
  2.3 0.7 %copy-done.4 = f32[1,512]{1,0:T(1,128)S(1)} copy-done((f32[1,512]{1,0:T(1,128)S(1)}, f32[1,512]{1,0:T(1,128)}, u32[]{:S(2)}) %copy-start.4) | copy-done | bytes 2072
  3.0 0.7 %shard_map.85 = f32[32,8,128]{2,1,0:T(8,128)} custom-call(f32[1,512]{1,0:T(1,128)S(1)} %copy-done.3, f32[1,512]{1,0:T(1,128)S(1)} %copy-done.4, f32[4,512]{1,0:T(4,128)S(1)} %get-tuple-element.31.first_ref, f32[4,512]{1,0:T(4,128)S(1)} %get-tuple-element.30.last_ref), custom_call_target="tpu_custom_call" | custom-call | tf_op jit(solution)/shard_map/pallas_call | solution.py:242
  3.6 7.3 %all-to-all-start = ((f32[32,8,128]{2,1,0:T(8,128)}), f32[32,8,128]{2,1,0:T(8,128)S(1)}, u32[]{:S(2)}, u32[]{:S(2)}) async-start(f32[32,8,128]{2,1,0:T(8,128)} %shard_map.85), calls=%async_computation | async-start | bytes 262144 | tf_op jit(solution)/shard_map/all_to_all | solution.py:245
  11.0 0.9 %copy-done.1 = f32[4,32,512]{2,1,0:T(8,128)S(1)} copy-done((f32[4,32,512]{2,1,0:T(8,128)S(1)}, f32[4,32,512]{2,1,0:T(8,128)}, u32[]{:S(2)}) %copy-start.1) | copy-done | bytes 262168
  11.9 0.1 shard_map.84
  12.0 1.8 %collective-permute-start = (f32[2,4,32,128]{3,2,1,0:T(8,128)S(1)}, f32[2,4,32,128]{3,2,1,0:T(8,128)S(1)}, u32[]{:S(2)}, u32[]{:S(2)}) collective-permute-start(f32[2,4,32,128]{3,2,1,0:T(8,128)S(1)} %get-tuple-element.17), channel_id=1, source_target_pairs={{0,8},{8,0},{16,24},{24,16},{1,9},{9,1},{17,25},{25,17},{2,10},{10... | collective-permute-start | bytes 393224 | tf_op jit(solution)/shard_map/ppermute | solution.py:33
  13.8 1.5 %collective-permute-start.1 = (f32[2,4,32,128]{3,2,1,0:T(8,128)S(1)}, f32[2,4,32,128]{3,2,1,0:T(8,128)S(1)}, u32[]{:S(2)}, u32[]{:S(2)}) collective-permute-start(f32[2,4,32,128]{3,2,1,0:T(8,128)S(1)} %get-tuple-element.18), channel_id=1, source_target_pairs={{0,16},{8,24},{16,0},{24,8},{1,17},{9,25},{17,1},{25,9},{2,18},{10... | collective-permute-start | bytes 393224 | tf_op jit(solution)/shard_map/ppermute | solution.py:33
  15.3 0.3 collective-permute-start.2
  15.5 3.5 %collective-permute-done.refs_1_ = f32[2,4,32,128]{3,2,1,0:T(8,128)S(1)} collective-permute-done((f32[2,4,32,128]{3,2,1,0:T(8,128)S(1)}, f32[2,4,32,128]{3,2,1,0:T(8,128)S(1)}, u32[]{:S(2)}, u32[]{:S(2)}) %collective-permute-start) | collective-permute-done | bytes 131104 | tf_op jit(solution)/shard_map/ppermute | solution.py:33
  19.1 3.5 %collective-permute-done.1.refs_2_ = f32[2,4,32,128]{3,2,1,0:T(8,128)S(1)} collective-permute-done((f32[2,4,32,128]{3,2,1,0:T(8,128)S(1)}, f32[2,4,32,128]{3,2,1,0:T(8,128)S(1)}, u32[]{:S(2)}, u32[]{:S(2)}) %collective-permute-start.1) | collective-permute-done | bytes 131104 | tf_op jit(solution)/shard_map/ppermute | solution.py:33
  22.6 2.3 %shard_map.86 = (f32[32,16,128]{2,1,0:T(8,128)}, f32[4,32,128]{2,1,0:T(8,128)S(1)}, f32[4,32,128]{2,1,0:T(8,128)S(1)}, f32[4,32,128]{2,1,0:T(8,128)S(1)}, f32[4,32,128]{2,1,0:T(8,128)S(1)}) custom-call(f32[2,4,32,128]{3,2,1,0:T(8,128)S(1)} %get-tuple-element.16.refs_0_, f32[2,4,32,128]{3,2,1,0:T(8,128)S(1)} %collective-permute-done.refs_1_, ...), custom_call_target="tpu_custom_call" | custom-call | tf_op jit(solution)/shard_map/pallas_call | solution.py:254
  24.9 4.0 %all-to-all-start.1 = ((f32[32,16,128]{2,1,0:T(8,128)}), f32[32,16,128]{2,1,0:T(8,128)S(1)}, u32[]{:S(2)}, u32[]{:S(2)}) async-start(f32[32,16,128]{2,1,0:T(8,128)} %get-tuple-element.24), calls=%async_computation.1 | async-start | bytes 524288 | tf_op jit(solution)/shard_map/all_to_all | solution.py:260
  28.9 1.8 %collective-permute-start.3 = (f32[4,32,128]{2,1,0:T(8,128)S(1)}, f32[4,32,128]{2,1,0:T(8,128)S(1)}, u32[]{:S(2)}, u32[]{:S(2)}) collective-permute-start(f32[4,32,128]{2,1,0:T(8,128)S(1)} %get-tuple-element.21), channel_id=1, source_target_pairs={{0,8},{8,0},{16,24},{24,16},{1,9},{9,1},{17,25},{25,17},{2,10},{10... | collective-permute-start | bytes 196616 | tf_op jit(solution)/shard_map/ppermute | solution.py:33
  30.8 1.5 %collective-permute-start.4 = (f32[4,32,128]{2,1,0:T(8,128)S(1)}, f32[4,32,128]{2,1,0:T(8,128)S(1)}, u32[]{:S(2)}, u32[]{:S(2)}) collective-permute-start(f32[4,32,128]{2,1,0:T(8,128)S(1)} %get-tuple-element.22), channel_id=1, source_target_pairs={{0,16},{8,24},{16,0},{24,8},{1,17},{9,25},{17,1},{25,9},{2,18},{10... | collective-permute-start | bytes 196616 | tf_op jit(solution)/shard_map/ppermute | solution.py:33
  32.2 0.3 collective-permute-start.5
  32.5 2.6 %collective-permute-done.3.refs_1_ = f32[4,32,128]{2,1,0:T(8,128)S(1)} collective-permute-done((f32[4,32,128]{2,1,0:T(8,128)S(1)}, f32[4,32,128]{2,1,0:T(8,128)S(1)}, u32[]{:S(2)}, u32[]{:S(2)}) %collective-permute-start.3) | collective-permute-done | bytes 65568 | tf_op jit(solution)/shard_map/ppermute | solution.py:33
  35.1 1.8 %collective-permute-done.4.refs_2_ = f32[4,32,128]{2,1,0:T(8,128)S(1)} collective-permute-done((f32[4,32,128]{2,1,0:T(8,128)S(1)}, f32[4,32,128]{2,1,0:T(8,128)S(1)}, u32[]{:S(2)}, u32[]{:S(2)}) %collective-permute-start.4) | collective-permute-done | bytes 65568 | tf_op jit(solution)/shard_map/ppermute | solution.py:33
  37.0 0.7 %collective-permute-done.5.refs_3_ = f32[4,32,128]{2,1,0:T(8,128)S(1)} collective-permute-done((f32[4,32,128]{2,1,0:T(8,128)S(1)}, f32[4,32,128]{2,1,0:T(8,128)S(1)}, u32[]{:S(2)}, u32[]{:S(2)}) %collective-permute-start.5) | collective-permute-done | bytes 65568 | tf_op jit(solution)/shard_map/ppermute | solution.py:33
  37.6 0.7 %shard_map.87 = f32[4,32,512]{2,1,0:T(8,128)} custom-call(f32[4,32,128]{2,1,0:T(8,128)S(1)} %get-tuple-element.20.refs_0_, f32[4,32,128]{2,1,0:T(8,128)S(1)} %collective-permute-done.3.refs_1_, f32[4,32,128]{2,1,0:T(8,128)S(1)} %collective-permute-done.4.refs_2_, f32[4,32,128]{2,1,0:T(8,128)S(1)} %collective-permute-done.5.refs_3_), custom_call_target="tpu_custom_call" | custom-call | tf_op jit(solution)/shard_map/pallas_call | solution.py:262
  38.4 1.0 %all-to-all-done.1.terms_ref = f32[32,16,128]{2,1,0:T(8,128)S(1)} async-done(((f32[32,16,128]{2,1,0:T(8,128)}), f32[32,16,128]{2,1,0:T(8,128)S(1)}, u32[]{:S(2)}, u32[]{:S(2)}) %all-to-all-start.1) | async-done | bytes 262176 | tf_op jit(solution)/shard_map/all_to_all | solution.py:260
  39.3 0.8 %shard_map.88 = (f32[1,512]{1,0:T(1,128)}, f32[1,512]{1,0:T(1,128)}, f32[9,512]{1,0:T(8,128)}) custom-call(f32[32,16,128]{2,1,0:T(8,128)S(1)} %all-to-all-done.1.terms_ref), custom_call_target="tpu_custom_call" | custom-call | tf_op jit(solution)/shard_map/pallas_call | solution.py:265
  (9 shorter events, 0.0 us)
Async XLA Ops:
  0.6 10.3 %copy-start = (f32[4,32,512]{2,1,0:T(8,128)S(1)}, f32[4,32,512]{2,1,0:T(8,128)}, u32[]{:S(2)}) copy-start(f32[4,32,512]{2,1,0:T(8,128)} %cotangent_ref.1) | copy-start | bytes 786436
  1.6 0.7 %copy-start.3 = (f32[1,512]{1,0:T(1,128)S(1)}, f32[1,512]{1,0:T(1,128)}, u32[]{:S(2)}) copy-start(f32[1,512]{1,0:T(1,128)} %key_ref.1) | copy-start | bytes 6148
  2.3 0.7 %copy-start.4 = (f32[1,512]{1,0:T(1,128)S(1)}, f32[1,512]{1,0:T(1,128)}, u32[]{:S(2)}) copy-start(f32[1,512]{1,0:T(1,128)} %value_ref.1) | copy-start | bytes 6148
  3.6 18.9 %all-to-all-start = ((f32[32,8,128]{2,1,0:T(8,128)}), f32[32,8,128]{2,1,0:T(8,128)S(1)}, u32[]{:S(2)}, u32[]{:S(2)}) async-start(f32[32,8,128]{2,1,0:T(8,128)} %shard_map.85), calls=%async_computation | async-start | bytes 262144 | tf_op jit(solution)/shard_map/all_to_all | solution.py:245
  11.0 1.0 %copy-start.1 = (f32[4,32,512]{2,1,0:T(8,128)S(1)}, f32[4,32,512]{2,1,0:T(8,128)}, u32[]{:S(2)}) copy-start(f32[4,32,512]{2,1,0:T(8,128)} %query_ref.1) | copy-start | bytes 786436
  11.9 10.7 %copy-start.2 = (f32[9,512]{1,0:T(8,128)S(1)}, f32[9,512]{1,0:T(8,128)}, u32[]{:S(2)}) copy-start(f32[9,512]{1,0:T(8,128)} %refs_5_.1) | copy-start | bytes 55300
  12.0 7.1 %collective-permute-start = (f32[2,4,32,128]{3,2,1,0:T(8,128)S(1)}, f32[2,4,32,128]{3,2,1,0:T(8,128)S(1)}, u32[]{:S(2)}, u32[]{:S(2)}) collective-permute-start(f32[2,4,32,128]{3,2,1,0:T(8,128)S(1)} %get-tuple-element.17), channel_id=1, source_target_pairs={{0,8},{8,0},{16,24},{24,16},{1,9},{9,1},{17,25},{25,17},{2,10},{10... | collective-permute-start | bytes 393224 | tf_op jit(solution)/shard_map/ppermute | solution.py:33
  13.8 8.8 %collective-permute-start.1 = (f32[2,4,32,128]{3,2,1,0:T(8,128)S(1)}, f32[2,4,32,128]{3,2,1,0:T(8,128)S(1)}, u32[]{:S(2)}, u32[]{:S(2)}) collective-permute-start(f32[2,4,32,128]{3,2,1,0:T(8,128)S(1)} %get-tuple-element.18), channel_id=1, source_target_pairs={{0,16},{8,24},{16,0},{24,8},{1,17},{9,25},{17,1},{25,9},{2,18},{10... | collective-permute-start | bytes 393224 | tf_op jit(solution)/shard_map/ppermute | solution.py:33
  15.3 7.3 %collective-permute-start.2 = (f32[2,4,32,128]{3,2,1,0:T(8,128)S(1)}, f32[2,4,32,128]{3,2,1,0:T(8,128)S(1)}, u32[]{:S(2)}, u32[]{:S(2)}) collective-permute-start(f32[2,4,32,128]{3,2,1,0:T(8,128)S(1)} %get-tuple-element.19), channel_id=1, source_target_pairs={{0,24},{8,16},{16,8},{24,0},{1,25},{9,17},{17,9},{25,1},{2,26},{10... | collective-permute-start | bytes 393224 | tf_op jit(solution)/shard_map/ppermute | solution.py:33
  24.9 14.4 %all-to-all-start.1 = ((f32[32,16,128]{2,1,0:T(8,128)}), f32[32,16,128]{2,1,0:T(8,128)S(1)}, u32[]{:S(2)}, u32[]{:S(2)}) async-start(f32[32,16,128]{2,1,0:T(8,128)} %get-tuple-element.24), calls=%async_computation.1 | async-start | bytes 524288 | tf_op jit(solution)/shard_map/all_to_all | solution.py:260
  28.9 6.2 %collective-permute-start.3 = (f32[4,32,128]{2,1,0:T(8,128)S(1)}, f32[4,32,128]{2,1,0:T(8,128)S(1)}, u32[]{:S(2)}, u32[]{:S(2)}) collective-permute-start(f32[4,32,128]{2,1,0:T(8,128)S(1)} %get-tuple-element.21), channel_id=1, source_target_pairs={{0,8},{8,0},{16,24},{24,16},{1,9},{9,1},{17,25},{25,17},{2,10},{10... | collective-permute-start | bytes 196616 | tf_op jit(solution)/shard_map/ppermute | solution.py:33
  30.8 6.2 %collective-permute-start.4 = (f32[4,32,128]{2,1,0:T(8,128)S(1)}, f32[4,32,128]{2,1,0:T(8,128)S(1)}, u32[]{:S(2)}, u32[]{:S(2)}) collective-permute-start(f32[4,32,128]{2,1,0:T(8,128)S(1)} %get-tuple-element.22), channel_id=1, source_target_pairs={{0,16},{8,24},{16,0},{24,8},{1,17},{9,25},{17,1},{25,9},{2,18},{10... | collective-permute-start | bytes 196616 | tf_op jit(solution)/shard_map/ppermute | solution.py:33
  32.2 5.4 %collective-permute-start.5 = (f32[4,32,128]{2,1,0:T(8,128)S(1)}, f32[4,32,128]{2,1,0:T(8,128)S(1)}, u32[]{:S(2)}, u32[]{:S(2)}) collective-permute-start(f32[4,32,128]{2,1,0:T(8,128)S(1)} %get-tuple-element.23), channel_id=1, source_target_pairs={{0,24},{8,16},{16,8},{24,0},{1,25},{9,17},{17,9},{25,1},{2,26},{10... | collective-permute-start | bytes 196616 | tf_op jit(solution)/shard_map/ppermute | solution.py:33

commit v2 on v1

--- a/solution.py
+++ b/solution.py
@@ -51,30 +51,58 @@
     )
 
 
-def rows_kernel(bands, sectors, width, key_ref, value_ref, first_ref, last_ref, out_ref):
+def in_hbm(array):
+    return pltpu.with_memory_space_constraint(array, pltpu.HBM)
+
+
+def pack_kernel(bands, sectors, width, keys, *refs):
+    key_ref, value_ref, query_ref, cotangent_ref, block_ref = refs[:5]
+    part_refs = refs[5 : 5 + bands]
+    key_own, value_own, first_own, last_own, sems = refs[5 + bands :]
+    band = lax.axis_index("lat")
     sector = lax.axis_index("lon")
-    rows = first_ref.shape[0]
-    keys = key_ref.shape[0]
-    for band in range(bands):
-        lanes = slice(band * width, (band + 1) * width)
-        key = key_ref[:, lanes]
-        value = value_ref[:, lanes]
-        first = first_ref[:, lanes]
-        last = last_ref[:, lanes]
-        for other in range(sectors):
-            device = band * sectors + other
-            is_next = lax.rem(other - sector + sectors, sectors) == 1
-            out_ref[device, 0:keys, :] = key
-            out_ref[device, keys : 2 * keys, :] = value
-            out_ref[device, 2 * keys : 2 * keys + rows, :] = jnp.where(is_next, last, first)
-
-
-def tokens_kernel(bands, width, query_ref, cotangent_ref, *out_refs):
-    band = lax.axis_index("lat")
-    for step, out_ref in enumerate(out_refs):
+    rows, columns = query_ref.shape[:2]
+
+    small = [
+        pltpu.make_async_copy(source_ref, target_ref, sems.at[i])
+        for i, (source_ref, target_ref) in enumerate(
+            (
+                (key_ref, key_own),
+                (value_ref, value_own),
+                (cotangent_ref.at[:, 0:SUBLANES, :], first_own),
+                (cotangent_ref.at[:, columns - SUBLANES : columns, :], last_own),
+            )
+        )
+    ]
+    for copy in small:
+        copy.start()
+    large = []
+    for step, part_ref in enumerate(part_refs):
         lanes = pl.ds(pl.multiple_of(partner(band, step, bands) * width, width), width)
-        out_ref[0] = query_ref[:, :, lanes]
-        out_ref[1] = cotangent_ref[:, :, lanes]
+        for i, array_ref in enumerate((query_ref, cotangent_ref)):
+            large.append(
+                pltpu.make_async_copy(
+                    array_ref.at[:, :, lanes], part_ref.at[i], sems.at[len(small) + len(large)]
+                )
+            )
+    for copy in large:
+        copy.start()
+    for copy in small:
+        copy.wait()
+    for to_band in range(bands):
+        lanes = slice(to_band * width, (to_band + 1) * width)
+        key = key_own[:, lanes]
+        value = value_own[:, lanes]
+        first = first_own[:, 0, lanes]
+        last = last_own[:, SUBLANES - 1, lanes]
+        for to_sector in range(sectors):
+            device = to_band * sectors + to_sector
+            is_next = lax.rem(to_sector - sector + sectors, sectors) == 1
+            block_ref[device, 0:keys, :] = key
+            block_ref[device, keys : 2 * keys, :] = value
+            block_ref[device, 2 * keys : 2 * keys + rows, :] = jnp.where(is_next, last, first)
+    for copy in large:
+        copy.wait()
 
 
 def heads_of(matrix, width):
@@ -239,14 +267,25 @@
     lines = rows * bands
 
     sent_rows = round_up(2 * keys + rows, SUBLANES)
-    (row_blocks,) = vmem_call(
-        functools.partial(rows_kernel, bands, sectors, width), [(devices, sent_rows, width)]
-    )(key_rows, value_rows, cotangent[:, 0, :], cotangent[:, columns - 1, :])
+    part_shape = (2, rows, columns, width)
+    anywhere = pl.BlockSpec(memory_space=pl.ANY)
+    row_blocks, *parts = pl.pallas_call(
+        functools.partial(pack_kernel, bands, sectors, width, keys),
+        out_shape=[
+            jax.ShapeDtypeStruct(s, jnp.float32)
+            for s in [(devices, sent_rows, width)] + [part_shape] * bands
+        ],
+        in_specs=[anywhere] * 4,
+        scratch_shapes=[
+            pltpu.VMEM((keys, channels), jnp.float32),
+            pltpu.VMEM((keys, channels), jnp.float32),
+            pltpu.VMEM((rows, SUBLANES, channels), jnp.float32),
+            pltpu.VMEM((rows, SUBLANES, channels), jnp.float32),
+            pltpu.SemaphoreType.DMA((4 + 2 * bands,)),
+        ],
+        compiler_params=pltpu.CompilerParams(vmem_limit_bytes=VMEM_LIMIT),
+    )(*[in_hbm(x) for x in (key_rows, value_rows, queries, cotangent)])
     row_blocks = lax.all_to_all(row_blocks, ("lat", "lon"), 0, 0, tiled=True)
-
-    parts = vmem_call(
-        functools.partial(tokens_kernel, bands, width), [(2, rows, columns, width)] * bands
-    )(queries, cotangent)
     parts = [parts[0]] + [exchange(parts[s], s, bands) for s in range(1, bands)]
 
     sent_terms = round_up(2 * keys + len(OFFSETS), SUBLANES)

time: 40.4 us -> 38.6 us (0.955)
  local copies, waits for them, and re-layouts: 3.25 us -> 0.01 us
  Pallas kernels: 4.59 us -> 5.76 us
    unnamed x10 -> x2, local copies, waits for them, and re-layouts: 2.31 us -> 0.01 us
    pallas_call x2 -> x1, Pallas kernels: 0.76 us -> 1.91 us  [split_heads_body(): pl.pallas_call(functools.partial(pack_kernel, bands, sectors, width, keys...]
    slice x1 -> x0, local copies, waits for them, and re-layouts: 0.93 us -> none  [split_heads_body(): cotangent[:, columns - 1, :]]
where the time goes in v2:
time: 38.6 us; the launch traced here: 38.2 us
  starting transfers between devices  18.3 us (47%)
  waiting for transfers between devices  13.5 us (35%)
  Pallas kernels  5.76 us (15%)
  between operations  0.68 us (2%)
    ppermute x6, waiting for transfers between devices, exchange(): lax.ppermute(value, 'lat', [(i, partner(i, step, peers)) for i in range(p...  12.5 us
    all_to_all x1, starting transfers between devices, split_heads_body(): row_blocks = lax.all_to_all(row_blocks, ('lat', 'lon'), 0, 0, tiled=True)  7.3 us
    ppermute x6, starting transfers between devices, exchange(): lax.ppermute(value, 'lat', [(i, partner(i, step, peers)) for i in range(p...  7.11 us
    all_to_all x1, starting transfers between devices, split_heads_body(): terms = lax.all_to_all(terms, ('lat', 'lon'), 0, 0, tiled=True)  3.88 us
    pallas_call x1, Pallas kernels, split_heads_body(): vmem_call(functools.partial(attention_kernel, bands, sectors, width, keys...  2.34 us
    pallas_call x1, Pallas kernels, split_heads_body(): pl.pallas_call(functools.partial(pack_kernel, bands, sectors, width, keys...  1.91 us
    all_to_all x1, waiting for transfers between devices, split_heads_body(): terms = lax.all_to_all(terms, ('lat', 'lon'), 0, 0, tiled=True)  0.97 us
    pallas_call x1, Pallas kernels, split_heads_body(): vmem_call(functools.partial(sums_kernel, bands, sectors, width, keys), [(...  0.78 us
  transfers between devices with their start and end apart: 8, of which 6 were waited for; matrix products, arithmetic and copies ran while one was open for 0% of the time, Pallas kernels for 2%

profile of v2, /device:TPU:0, one launch (start us, length us, event | category | flops | bytes accessed | tf_op | source)
XLA Modules:
  0.0 38.2 jit_solution(3876063696860811797)
XLA Ops:
  0.6 1.9 %shard_map.84 = (f32[32,8,128]{2,1,0:T(8,128)}, f32[2,4,32,128]{3,2,1,0:T(8,128)S(1)}, f32[2,4,32,128]{3,2,1,0:T(8,128)S(1)}, f32[2,4,32,128]{3,2,1,0:T(8,128)S(1)}, f32[2,4,32,128]{3,2,1,0:T(8,128)S(1)}) custom-call(f32[1,512]{1,0:T(1,128)} %refs_0_.1, f32[1,512]{1,0:T(1,128)} %refs_1_.1, f32[4,32,512]{2,1,0:T(8,128)} %refs_2_.1, f32[4,32,512]{2,1,0:T(8,128)} %refs_3_.1), custom_call_target="tpu_custom_call" | custom-call | tf_op jit(solution)/shard_map/pallas_call | solution.py:272
  2.5 0.0 copy-start
  2.6 7.3 %all-to-all-start = ((f32[32,8,128]{2,1,0:T(8,128)}), f32[32,8,128]{2,1,0:T(8,128)S(1)}, u32[]{:S(2)}, u32[]{:S(2)}) async-start(f32[32,8,128]{2,1,0:T(8,128)} %get-tuple-element.21), calls=%async_computation | async-start | bytes 262144 | tf_op jit(solution)/shard_map/all_to_all | solution.py:288
  9.9 1.8 %collective-permute-start = (f32[2,4,32,128]{3,2,1,0:T(8,128)S(1)}, f32[2,4,32,128]{3,2,1,0:T(8,128)S(1)}, u32[]{:S(2)}, u32[]{:S(2)}) collective-permute-start(f32[2,4,32,128]{3,2,1,0:T(8,128)S(1)} %get-tuple-element.18), channel_id=1, source_target_pairs={{0,8},{8,0},{16,24},{24,16},{1,9},{9,1},{17,25},{25,17},{2,10},{10... | collective-permute-start | bytes 393224 | tf_op jit(solution)/shard_map/ppermute | solution.py:33
  11.7 1.5 %collective-permute-start.1 = (f32[2,4,32,128]{3,2,1,0:T(8,128)S(1)}, f32[2,4,32,128]{3,2,1,0:T(8,128)S(1)}, u32[]{:S(2)}, u32[]{:S(2)}) collective-permute-start(f32[2,4,32,128]{3,2,1,0:T(8,128)S(1)} %get-tuple-element.19), channel_id=1, source_target_pairs={{0,16},{8,24},{16,0},{24,8},{1,17},{9,25},{17,1},{25,9},{2,18},{10... | collective-permute-start | bytes 393224 | tf_op jit(solution)/shard_map/ppermute | solution.py:33
  13.2 0.3 collective-permute-start.2
  13.4 3.9 %collective-permute-done.refs_1_ = f32[2,4,32,128]{3,2,1,0:T(8,128)S(1)} collective-permute-done((f32[2,4,32,128]{3,2,1,0:T(8,128)S(1)}, f32[2,4,32,128]{3,2,1,0:T(8,128)S(1)}, u32[]{:S(2)}, u32[]{:S(2)}) %collective-permute-start) | collective-permute-done | bytes 131104 | tf_op jit(solution)/shard_map/ppermute | solution.py:33
  17.3 3.5 %collective-permute-done.1.refs_2_ = f32[2,4,32,128]{3,2,1,0:T(8,128)S(1)} collective-permute-done((f32[2,4,32,128]{3,2,1,0:T(8,128)S(1)}, f32[2,4,32,128]{3,2,1,0:T(8,128)S(1)}, u32[]{:S(2)}, u32[]{:S(2)}) %collective-permute-start.1) | collective-permute-done | bytes 131104 | tf_op jit(solution)/shard_map/ppermute | solution.py:33
  20.8 0.0 collective-permute-done.2.refs_3_
  20.8 0.0 all-to-all-done.refs_4_
  20.8 0.0 copy-done
  20.9 2.3 %shard_map.85 = (f32[32,16,128]{2,1,0:T(8,128)}, f32[4,32,128]{2,1,0:T(8,128)S(1)}, f32[4,32,128]{2,1,0:T(8,128)S(1)}, f32[4,32,128]{2,1,0:T(8,128)S(1)}, f32[4,32,128]{2,1,0:T(8,128)S(1)}) custom-call(f32[2,4,32,128]{3,2,1,0:T(8,128)S(1)} %get-tuple-element.17.refs_0_, f32[2,4,32,128]{3,2,1,0:T(8,128)S(1)} %collective-permute-done.refs_1_, ...), custom_call_target="tpu_custom_call" | custom-call | tf_op jit(solution)/shard_map/pallas_call | solution.py:293
  23.2 3.9 %all-to-all-start.1 = ((f32[32,16,128]{2,1,0:T(8,128)}), f32[32,16,128]{2,1,0:T(8,128)S(1)}, u32[]{:S(2)}, u32[]{:S(2)}) async-start(f32[32,16,128]{2,1,0:T(8,128)} %get-tuple-element.26), calls=%async_computation.1 | async-start | bytes 524288 | tf_op jit(solution)/shard_map/all_to_all | solution.py:299
  27.1 1.8 %collective-permute-start.3 = (f32[4,32,128]{2,1,0:T(8,128)S(1)}, f32[4,32,128]{2,1,0:T(8,128)S(1)}, u32[]{:S(2)}, u32[]{:S(2)}) collective-permute-start(f32[4,32,128]{2,1,0:T(8,128)S(1)} %get-tuple-element.23), channel_id=1, source_target_pairs={{0,8},{8,0},{16,24},{24,16},{1,9},{9,1},{17,25},{25,17},{2,10},{10... | collective-permute-start | bytes 196616 | tf_op jit(solution)/shard_map/ppermute | solution.py:33
  28.9 1.5 %collective-permute-start.4 = (f32[4,32,128]{2,1,0:T(8,128)S(1)}, f32[4,32,128]{2,1,0:T(8,128)S(1)}, u32[]{:S(2)}, u32[]{:S(2)}) collective-permute-start(f32[4,32,128]{2,1,0:T(8,128)S(1)} %get-tuple-element.24), channel_id=1, source_target_pairs={{0,16},{8,24},{16,0},{24,8},{1,17},{9,25},{17,1},{25,9},{2,18},{10... | collective-permute-start | bytes 196616 | tf_op jit(solution)/shard_map/ppermute | solution.py:33
  30.4 0.3 collective-permute-start.5
  30.6 2.6 %collective-permute-done.3.refs_1_ = f32[4,32,128]{2,1,0:T(8,128)S(1)} collective-permute-done((f32[4,32,128]{2,1,0:T(8,128)S(1)}, f32[4,32,128]{2,1,0:T(8,128)S(1)}, u32[]{:S(2)}, u32[]{:S(2)}) %collective-permute-start.3) | collective-permute-done | bytes 65568 | tf_op jit(solution)/shard_map/ppermute | solution.py:33
  33.3 1.8 %collective-permute-done.4.refs_2_ = f32[4,32,128]{2,1,0:T(8,128)S(1)} collective-permute-done((f32[4,32,128]{2,1,0:T(8,128)S(1)}, f32[4,32,128]{2,1,0:T(8,128)S(1)}, u32[]{:S(2)}, u32[]{:S(2)}) %collective-permute-start.4) | collective-permute-done | bytes 65568 | tf_op jit(solution)/shard_map/ppermute | solution.py:33
  35.1 0.7 %collective-permute-done.5.refs_3_ = f32[4,32,128]{2,1,0:T(8,128)S(1)} collective-permute-done((f32[4,32,128]{2,1,0:T(8,128)S(1)}, f32[4,32,128]{2,1,0:T(8,128)S(1)}, u32[]{:S(2)}, u32[]{:S(2)}) %collective-permute-start.5) | collective-permute-done | bytes 65568 | tf_op jit(solution)/shard_map/ppermute | solution.py:33
  35.8 0.7 %shard_map.86 = f32[4,32,512]{2,1,0:T(8,128)} custom-call(f32[4,32,128]{2,1,0:T(8,128)S(1)} %get-tuple-element.22.refs_0_, f32[4,32,128]{2,1,0:T(8,128)S(1)} %collective-permute-done.3.refs_1_, f32[4,32,128]{2,1,0:T(8,128)S(1)} %collective-permute-done.4.refs_2_, f32[4,32,128]{2,1,0:T(8,128)S(1)} %collective-permute-done.5.refs_3_), custom_call_target="tpu_custom_call" | custom-call | tf_op jit(solution)/shard_map/pallas_call | solution.py:301
  36.5 1.0 %all-to-all-done.1.terms_ref = f32[32,16,128]{2,1,0:T(8,128)S(1)} async-done(((f32[32,16,128]{2,1,0:T(8,128)}), f32[32,16,128]{2,1,0:T(8,128)S(1)}, u32[]{:S(2)}, u32[]{:S(2)}) %all-to-all-start.1) | async-done | bytes 262176 | tf_op jit(solution)/shard_map/all_to_all | solution.py:299
  37.5 0.8 %shard_map.87 = (f32[1,512]{1,0:T(1,128)}, f32[1,512]{1,0:T(1,128)}, f32[9,512]{1,0:T(8,128)}) custom-call(f32[32,16,128]{2,1,0:T(8,128)S(1)} %all-to-all-done.1.terms_ref), custom_call_target="tpu_custom_call" | custom-call | tf_op jit(solution)/shard_map/pallas_call | solution.py:304
Async XLA Ops:
  2.5 18.3 %copy-start = (f32[9,512]{1,0:T(8,128)S(1)}, f32[9,512]{1,0:T(8,128)}, u32[]{:S(2)}) copy-start(f32[9,512]{1,0:T(8,128)} %refs_5_.1) | copy-start | bytes 55300
  2.6 18.3 %all-to-all-start = ((f32[32,8,128]{2,1,0:T(8,128)}), f32[32,8,128]{2,1,0:T(8,128)S(1)}, u32[]{:S(2)}, u32[]{:S(2)}) async-start(f32[32,8,128]{2,1,0:T(8,128)} %get-tuple-element.21), calls=%async_computation | async-start | bytes 262144 | tf_op jit(solution)/shard_map/all_to_all | solution.py:288
  9.9 7.5 %collective-permute-start = (f32[2,4,32,128]{3,2,1,0:T(8,128)S(1)}, f32[2,4,32,128]{3,2,1,0:T(8,128)S(1)}, u32[]{:S(2)}, u32[]{:S(2)}) collective-permute-start(f32[2,4,32,128]{3,2,1,0:T(8,128)S(1)} %get-tuple-element.18), channel_id=1, source_target_pairs={{0,8},{8,0},{16,24},{24,16},{1,9},{9,1},{17,25},{25,17},{2,10},{10... | collective-permute-start | bytes 393224 | tf_op jit(solution)/shard_map/ppermute | solution.py:33
  11.7 9.1 %collective-permute-start.1 = (f32[2,4,32,128]{3,2,1,0:T(8,128)S(1)}, f32[2,4,32,128]{3,2,1,0:T(8,128)S(1)}, u32[]{:S(2)}, u32[]{:S(2)}) collective-permute-start(f32[2,4,32,128]{3,2,1,0:T(8,128)S(1)} %get-tuple-element.19), channel_id=1, source_target_pairs={{0,16},{8,24},{16,0},{24,8},{1,17},{9,25},{17,1},{25,9},{2,18},{10... | collective-permute-start | bytes 393224 | tf_op jit(solution)/shard_map/ppermute | solution.py:33
  13.2 7.7 %collective-permute-start.2 = (f32[2,4,32,128]{3,2,1,0:T(8,128)S(1)}, f32[2,4,32,128]{3,2,1,0:T(8,128)S(1)}, u32[]{:S(2)}, u32[]{:S(2)}) collective-permute-start(f32[2,4,32,128]{3,2,1,0:T(8,128)S(1)} %get-tuple-element.20), channel_id=1, source_target_pairs={{0,24},{8,16},{16,8},{24,0},{1,25},{9,17},{17,9},{25,1},{2,26},{10... | collective-permute-start | bytes 393224 | tf_op jit(solution)/shard_map/ppermute | solution.py:33
  23.2 14.3 %all-to-all-start.1 = ((f32[32,16,128]{2,1,0:T(8,128)}), f32[32,16,128]{2,1,0:T(8,128)S(1)}, u32[]{:S(2)}, u32[]{:S(2)}) async-start(f32[32,16,128]{2,1,0:T(8,128)} %get-tuple-element.26), calls=%async_computation.1 | async-start | bytes 524288 | tf_op jit(solution)/shard_map/all_to_all | solution.py:299
  27.1 6.2 %collective-permute-start.3 = (f32[4,32,128]{2,1,0:T(8,128)S(1)}, f32[4,32,128]{2,1,0:T(8,128)S(1)}, u32[]{:S(2)}, u32[]{:S(2)}) collective-permute-start(f32[4,32,128]{2,1,0:T(8,128)S(1)} %get-tuple-element.23), channel_id=1, source_target_pairs={{0,8},{8,0},{16,24},{24,16},{1,9},{9,1},{17,25},{25,17},{2,10},{10... | collective-permute-start | bytes 196616 | tf_op jit(solution)/shard_map/ppermute | solution.py:33
  28.9 6.2 %collective-permute-start.4 = (f32[4,32,128]{2,1,0:T(8,128)S(1)}, f32[4,32,128]{2,1,0:T(8,128)S(1)}, u32[]{:S(2)}, u32[]{:S(2)}) collective-permute-start(f32[4,32,128]{2,1,0:T(8,128)S(1)} %get-tuple-element.24), channel_id=1, source_target_pairs={{0,16},{8,24},{16,0},{24,8},{1,17},{9,25},{17,1},{25,9},{2,18},{10... | collective-permute-start | bytes 196616 | tf_op jit(solution)/shard_map/ppermute | solution.py:33
  30.4 5.4 %collective-permute-start.5 = (f32[4,32,128]{2,1,0:T(8,128)S(1)}, f32[4,32,128]{2,1,0:T(8,128)S(1)}, u32[]{:S(2)}, u32[]{:S(2)}) collective-permute-start(f32[4,32,128]{2,1,0:T(8,128)S(1)} %get-tuple-element.25), channel_id=1, source_target_pairs={{0,24},{8,16},{16,8},{24,0},{1,25},{9,17},{17,9},{25,1},{2,26},{10... | collective-permute-start | bytes 196616 | tf_op jit(solution)/shard_map/ppermute | solution.py:33

commit v3 on v2

--- a/solution.py
+++ b/solution.py
@@ -217,14 +217,12 @@
                 sums[t] = sums[t] + product[c : c + SUBLANES]
     tap_sum = jnp.concatenate([jnp.sum(s, 0, keepdims=True) for s in sums], 0)
     used = 2 * keys + len(OFFSETS)
-    filler = jnp.zeros((terms_ref.shape[1] - used, width), jnp.float32)
     for device in range(bands * sectors):
         mine = slice(device * keys, (device + 1) * keys)
-        terms_ref[device, 0:keys, :] = key_grad[mine]
-        terms_ref[device, keys : 2 * keys, :] = value_grad[mine]
-        terms_ref[device, 2 * keys : used, :] = tap_sum
-        if terms_ref.shape[1] > used:
-            terms_ref[device, used:, :] = filler
+        start = device * used
+        terms_ref[start : start + keys, :] = key_grad[mine]
+        terms_ref[start + keys : start + 2 * keys, :] = value_grad[mine]
+        terms_ref[start + 2 * keys : start + used, :] = tap_sum
 
     query_grad = (dot(logit_grad, key_heads, 0, 0) * scale).reshape(lines, columns, width)
     out_ref[...] = query_grad
@@ -232,23 +230,21 @@
         query_grad_ref[...] = out_ref[pl.ds(partner(band, step, bands) * rows, rows)]
 
 
-def join_kernel(bands, width, *refs):
+def finish_kernel(bands, sectors, width, keys, *refs):
+    part_refs = refs[:bands]
+    terms_ref, query_ref, key_ref, value_ref, taps_ref = refs[bands:]
     band = lax.axis_index("lat")
-    out_ref = refs[-1]
-    for step, part_ref in enumerate(refs[:-1]):
+    for step, part_ref in enumerate(part_refs):
         lanes = pl.ds(pl.multiple_of(source(band, step, bands) * width, width), width)
-        out_ref[:, :, lanes] = part_ref[...]
-
-
-def sums_kernel(bands, sectors, width, keys, terms_ref, key_ref, value_ref, taps_ref):
+        query_ref[:, :, lanes] = part_ref[...]
     used = 2 * keys + len(OFFSETS)
-    total = jnp.zeros((), jnp.float32)
     parts = []
-    for band in range(bands):
-        lanes = slice(band * width, (band + 1) * width)
-        part = terms_ref[band * sectors]
-        for sector in range(1, sectors):
-            part = part + terms_ref[band * sectors + sector]
+    for to_band in range(bands):
+        lanes = slice(to_band * width, (to_band + 1) * width)
+        part = jnp.zeros((used, width), jnp.float32)
+        for sector in range(sectors):
+            start = (to_band * sectors + sector) * used
+            part = part + terms_ref[start : start + used, :]
         key_ref[:, lanes] = part[0:keys]
         value_ref[:, lanes] = part[keys : 2 * keys]
         parts.append(part[2 * keys : used])
@@ -288,23 +284,26 @@
     row_blocks = lax.all_to_all(row_blocks, ("lat", "lon"), 0, 0, tiled=True)
     parts = [parts[0]] + [exchange(parts[s], s, bands) for s in range(1, bands)]
 
-    sent_terms = round_up(2 * keys + len(OFFSETS), SUBLANES)
+    sent_terms = 2 * keys + len(OFFSETS)
     grid = (lines, columns, width)
     terms, *grad_parts = vmem_call(
         functools.partial(attention_kernel, bands, sectors, width, keys),
-        [(devices, sent_terms, width)] + [(rows, columns, width)] * bands,
+        [(devices * sent_terms, width)] + [(rows, columns, width)] * bands,
         [grid, (lines + 2, columns + 2 * SUBLANES, width), grid, grid],
     )(*parts, row_blocks, conv_taps)
 
+    terms = terms.reshape(devices, sent_terms, 1, width)
     terms = lax.all_to_all(terms, ("lat", "lon"), 0, 0, tiled=True)
+    terms = terms.reshape(devices * sent_terms, width)
     grad_parts = [grad_parts[0]] + [exchange(grad_parts[s], s, bands) for s in range(1, bands)]
-    (query_grad,) = vmem_call(
-        functools.partial(join_kernel, bands, width), [(rows, columns, channels)]
-    )(*grad_parts)
-    key_grad, value_grad, tap_update = vmem_call(
-        functools.partial(sums_kernel, bands, sectors, width, keys),
-        [(keys, channels), (keys, channels), (len(OFFSETS), channels)],
-    )(terms)
+    query_grad, key_grad, value_grad, tap_update = pl.pallas_call(
+        functools.partial(finish_kernel, bands, sectors, width, keys),
+        out_shape=[
+            jax.ShapeDtypeStruct(s, jnp.float32)
+            for s in (queries.shape, key_rows.shape, value_rows.shape, conv_taps.shape)
+        ],
+        compiler_params=pltpu.CompilerParams(vmem_limit_bytes=VMEM_LIMIT),
+    )(*grad_parts, terms)
     return (query_grad, key_grad, value_grad, tap_update)
 
 

time: 38.6 us -> 37 us (0.959)
  waiting for transfers between devices: 13.5 us -> 12.7 us
  Pallas kernels: 5.76 us -> 5 us
    all_to_all x1, waiting for transfers between devices: 0.97 us -> 0.01 us  [split_heads_body(): terms = lax.all_to_all(terms, ('lat', 'lon'), 0, 0, tiled=True)]
    pallas_call x2 -> x1, Pallas kernels: 1.51 us -> 0.78 us  [split_heads_body(): pl.pallas_call(functools.partial(finish_kernel, bands, sectors, width, ke...]
  transfers between devices with their start and end apart: 8 -> 8, of which waited for: 6 -> 5; matrix products, arithmetic and copies ran while one was open for 0% -> 0% of each run, Pallas kernels for 2% -> 0%
where the time goes in v3:
time: 37 us; the launch traced here: 36.6 us
  starting transfers between devices  18.3 us (49%)
  waiting for transfers between devices  12.7 us (34%)
  Pallas kernels  5 us (14%)
  between operations  0.67 us (2%)
    ppermute x6, waiting for transfers between devices, exchange(): lax.ppermute(value, 'lat', [(i, partner(i, step, peers)) for i in range(p...  12.7 us
    all_to_all x1, starting transfers between devices, split_heads_body(): row_blocks = lax.all_to_all(row_blocks, ('lat', 'lon'), 0, 0, tiled=True)  7.3 us
    ppermute x6, starting transfers between devices, exchange(): lax.ppermute(value, 'lat', [(i, partner(i, step, peers)) for i in range(p...  7.11 us
    all_to_all x1, starting transfers between devices, split_heads_body(): terms = lax.all_to_all(terms, ('lat', 'lon'), 0, 0, tiled=True)  3.88 us
    pallas_call x1, Pallas kernels, split_heads_body(): vmem_call(functools.partial(attention_kernel, bands, sectors, width, keys...  2.31 us
    pallas_call x1, Pallas kernels, split_heads_body(): pl.pallas_call(functools.partial(pack_kernel, bands, sectors, width, keys...  1.91 us
    pallas_call x1, Pallas kernels, split_heads_body(): pl.pallas_call(functools.partial(finish_kernel, bands, sectors, width, ke...  0.78 us
  transfers between devices with their start and end apart: 8, of which 5 were waited for; matrix products, arithmetic and copies ran while one was open for 0% of the time, Pallas kernels for 0%

profile of v3, /device:TPU:0, one launch (start us, length us, event | category | flops | bytes accessed | tf_op | source)
XLA Modules:
  0.0 36.6 jit_solution(14082360063615459401)
XLA Ops:
  0.6 1.9 %shard_map.84 = (f32[32,8,128]{2,1,0:T(8,128)}, f32[2,4,32,128]{3,2,1,0:T(8,128)S(1)}, f32[2,4,32,128]{3,2,1,0:T(8,128)S(1)}, f32[2,4,32,128]{3,2,1,0:T(8,128)S(1)}, f32[2,4,32,128]{3,2,1,0:T(8,128)S(1)}) custom-call(f32[1,512]{1,0:T(1,128)} %refs_0_.1, f32[1,512]{1,0:T(1,128)} %refs_1_.1, f32[4,32,512]{2,1,0:T(8,128)} %refs_2_.1, f32[4,32,512]{2,1,0:T(8,128)} %refs_3_.1), custom_call_target="tpu_custom_call" | custom-call | tf_op jit(solution)/shard_map/pallas_call | solution.py:268
  2.5 0.0 copy-start
  2.6 7.3 %all-to-all-start = ((f32[32,8,128]{2,1,0:T(8,128)}), f32[32,8,128]{2,1,0:T(8,128)S(1)}, u32[]{:S(2)}, u32[]{:S(2)}) async-start(f32[32,8,128]{2,1,0:T(8,128)} %get-tuple-element.18), calls=%async_computation | async-start | bytes 262144 | tf_op jit(solution)/shard_map/all_to_all | solution.py:284
  9.9 1.8 %collective-permute-start = (f32[2,4,32,128]{3,2,1,0:T(8,128)S(1)}, f32[2,4,32,128]{3,2,1,0:T(8,128)S(1)}, u32[]{:S(2)}, u32[]{:S(2)}) collective-permute-start(f32[2,4,32,128]{3,2,1,0:T(8,128)S(1)} %get-tuple-element.15), channel_id=1, source_target_pairs={{0,8},{8,0},{16,24},{24,16},{1,9},{9,1},{17,25},{25,17},{2,10},{10... | collective-permute-start | bytes 393224 | tf_op jit(solution)/shard_map/ppermute | solution.py:33
  11.7 1.5 %collective-permute-start.1 = (f32[2,4,32,128]{3,2,1,0:T(8,128)S(1)}, f32[2,4,32,128]{3,2,1,0:T(8,128)S(1)}, u32[]{:S(2)}, u32[]{:S(2)}) collective-permute-start(f32[2,4,32,128]{3,2,1,0:T(8,128)S(1)} %get-tuple-element.16), channel_id=1, source_target_pairs={{0,16},{8,24},{16,0},{24,8},{1,17},{9,25},{17,1},{25,9},{2,18},{10... | collective-permute-start | bytes 393224 | tf_op jit(solution)/shard_map/ppermute | solution.py:33
  13.2 0.3 collective-permute-start.2
  13.4 3.9 %collective-permute-done.refs_1_ = f32[2,4,32,128]{3,2,1,0:T(8,128)S(1)} collective-permute-done((f32[2,4,32,128]{3,2,1,0:T(8,128)S(1)}, f32[2,4,32,128]{3,2,1,0:T(8,128)S(1)}, u32[]{:S(2)}, u32[]{:S(2)}) %collective-permute-start) | collective-permute-done | bytes 131104 | tf_op jit(solution)/shard_map/ppermute | solution.py:33
  17.3 3.5 %collective-permute-done.1.refs_2_ = f32[2,4,32,128]{3,2,1,0:T(8,128)S(1)} collective-permute-done((f32[2,4,32,128]{3,2,1,0:T(8,128)S(1)}, f32[2,4,32,128]{3,2,1,0:T(8,128)S(1)}, u32[]{:S(2)}, u32[]{:S(2)}) %collective-permute-start.1) | collective-permute-done | bytes 131104 | tf_op jit(solution)/shard_map/ppermute | solution.py:33
  20.8 0.0 collective-permute-done.2.refs_3_
  20.8 0.0 all-to-all-done.refs_4_
  20.8 0.0 copy-done
  20.9 2.3 %shard_map.85 = (f32[352,128]{1,0:T(8,128)}, f32[4,32,128]{2,1,0:T(8,128)S(1)}, f32[4,32,128]{2,1,0:T(8,128)S(1)}, f32[4,32,128]{2,1,0:T(8,128)S(1)}, f32[4,32,128]{2,1,0:T(8,128)S(1)}) custom-call(f32[2,4,32,128]{3,2,1,0:T(8,128)S(1)} %get-tuple-element.14.refs_0_, f32[2,4,32,128]{3,2,1,0:T(8,128)S(1)} %collective-permute-done.refs_1_, ...), custom_call_target="tpu_custom_call" | custom-call | tf_op jit(solution)/shard_map/pallas_call | solution.py:289
  23.2 3.9 %all-to-all-start.1 = ((f32[32,11,1,128]{3,2,1,0:T(1,128)}), f32[32,11,1,128]{3,2,1,0:T(1,128)S(1)}, u32[]{:S(2)}, u32[]{:S(2)}) async-start(f32[32,11,1,128]{3,2,1,0:T(1,128)} %bitcast), calls=%async_computation.1 | async-start | bytes 360448 | tf_op jit(solution)/shard_map/all_to_all | solution.py:296
  27.1 1.8 %collective-permute-start.3 = (f32[4,32,128]{2,1,0:T(8,128)S(1)}, f32[4,32,128]{2,1,0:T(8,128)S(1)}, u32[]{:S(2)}, u32[]{:S(2)}) collective-permute-start(f32[4,32,128]{2,1,0:T(8,128)S(1)} %get-tuple-element.20), channel_id=1, source_target_pairs={{0,8},{8,0},{16,24},{24,16},{1,9},{9,1},{17,25},{25,17},{2,10},{10... | collective-permute-start | bytes 196616 | tf_op jit(solution)/shard_map/ppermute | solution.py:33
  28.9 1.5 %collective-permute-start.4 = (f32[4,32,128]{2,1,0:T(8,128)S(1)}, f32[4,32,128]{2,1,0:T(8,128)S(1)}, u32[]{:S(2)}, u32[]{:S(2)}) collective-permute-start(f32[4,32,128]{2,1,0:T(8,128)S(1)} %get-tuple-element.21), channel_id=1, source_target_pairs={{0,16},{8,24},{16,0},{24,8},{1,17},{9,25},{17,1},{25,9},{2,18},{10... | collective-permute-start | bytes 196616 | tf_op jit(solution)/shard_map/ppermute | solution.py:33
  30.4 0.3 collective-permute-start.5
  30.6 1.8 %collective-permute-done.3.refs_1_ = f32[4,32,128]{2,1,0:T(8,128)S(1)} collective-permute-done((f32[4,32,128]{2,1,0:T(8,128)S(1)}, f32[4,32,128]{2,1,0:T(8,128)S(1)}, u32[]{:S(2)}, u32[]{:S(2)}) %collective-permute-start.3) | collective-permute-done | bytes 65568 | tf_op jit(solution)/shard_map/ppermute | solution.py:33
  32.4 2.1 %collective-permute-done.4.refs_2_ = f32[4,32,128]{2,1,0:T(8,128)S(1)} collective-permute-done((f32[4,32,128]{2,1,0:T(8,128)S(1)}, f32[4,32,128]{2,1,0:T(8,128)S(1)}, u32[]{:S(2)}, u32[]{:S(2)}) %collective-permute-start.4) | collective-permute-done | bytes 65568 | tf_op jit(solution)/shard_map/ppermute | solution.py:33
  34.5 1.4 %collective-permute-done.5.refs_3_ = f32[4,32,128]{2,1,0:T(8,128)S(1)} collective-permute-done((f32[4,32,128]{2,1,0:T(8,128)S(1)}, f32[4,32,128]{2,1,0:T(8,128)S(1)}, u32[]{:S(2)}, u32[]{:S(2)}) %collective-permute-start.5) | collective-permute-done | bytes 65568 | tf_op jit(solution)/shard_map/ppermute | solution.py:33
  35.9 0.0 all-to-all-done.1
  35.9 0.8 %shard_map.86 = (f32[4,32,512]{2,1,0:T(8,128)}, f32[1,512]{1,0:T(1,128)}, f32[1,512]{1,0:T(1,128)}, f32[9,512]{1,0:T(8,128)}) custom-call(f32[4,32,128]{2,1,0:T(8,128)S(1)} %get-tuple-element.19.refs_0_, f32[4,32,128]{2,1,0:T(8,128)S(1)} %collective-permute-done.3.refs_1_, f32[4,32,128]{2,1,0:T(8,128)S(1)} %collective-permute-done.4.refs_2_, ...), custom_call_target="tpu_custom_call" | custom-call | tf_op jit(solution)/shard_map/pallas_call | solution.py:299
Async XLA Ops:
  2.5 18.3 %copy-start = (f32[9,512]{1,0:T(8,128)S(1)}, f32[9,512]{1,0:T(8,128)}, u32[]{:S(2)}) copy-start(f32[9,512]{1,0:T(8,128)} %refs_5_.1) | copy-start | bytes 55300
  2.6 18.3 %all-to-all-start = ((f32[32,8,128]{2,1,0:T(8,128)}), f32[32,8,128]{2,1,0:T(8,128)S(1)}, u32[]{:S(2)}, u32[]{:S(2)}) async-start(f32[32,8,128]{2,1,0:T(8,128)} %get-tuple-element.18), calls=%async_computation | async-start | bytes 262144 | tf_op jit(solution)/shard_map/all_to_all | solution.py:284
  9.9 7.5 %collective-permute-start = (f32[2,4,32,128]{3,2,1,0:T(8,128)S(1)}, f32[2,4,32,128]{3,2,1,0:T(8,128)S(1)}, u32[]{:S(2)}, u32[]{:S(2)}) collective-permute-start(f32[2,4,32,128]{3,2,1,0:T(8,128)S(1)} %get-tuple-element.15), channel_id=1, source_target_pairs={{0,8},{8,0},{16,24},{24,16},{1,9},{9,1},{17,25},{25,17},{2,10},{10... | collective-permute-start | bytes 393224 | tf_op jit(solution)/shard_map/ppermute | solution.py:33
  11.7 9.1 %collective-permute-start.1 = (f32[2,4,32,128]{3,2,1,0:T(8,128)S(1)}, f32[2,4,32,128]{3,2,1,0:T(8,128)S(1)}, u32[]{:S(2)}, u32[]{:S(2)}) collective-permute-start(f32[2,4,32,128]{3,2,1,0:T(8,128)S(1)} %get-tuple-element.16), channel_id=1, source_target_pairs={{0,16},{8,24},{16,0},{24,8},{1,17},{9,25},{17,1},{25,9},{2,18},{10... | collective-permute-start | bytes 393224 | tf_op jit(solution)/shard_map/ppermute | solution.py:33
  13.2 7.7 %collective-permute-start.2 = (f32[2,4,32,128]{3,2,1,0:T(8,128)S(1)}, f32[2,4,32,128]{3,2,1,0:T(8,128)S(1)}, u32[]{:S(2)}, u32[]{:S(2)}) collective-permute-start(f32[2,4,32,128]{3,2,1,0:T(8,128)S(1)} %get-tuple-element.17), channel_id=1, source_target_pairs={{0,24},{8,16},{16,8},{24,0},{1,25},{9,17},{17,9},{25,1},{2,26},{10... | collective-permute-start | bytes 393224 | tf_op jit(solution)/shard_map/ppermute | solution.py:33
  23.2 12.7 %all-to-all-start.1 = ((f32[32,11,1,128]{3,2,1,0:T(1,128)}), f32[32,11,1,128]{3,2,1,0:T(1,128)S(1)}, u32[]{:S(2)}, u32[]{:S(2)}) async-start(f32[32,11,1,128]{3,2,1,0:T(1,128)} %bitcast), calls=%async_computation.1 | async-start | bytes 360448 | tf_op jit(solution)/shard_map/all_to_all | solution.py:296
  27.1 5.4 %collective-permute-start.3 = (f32[4,32,128]{2,1,0:T(8,128)S(1)}, f32[4,32,128]{2,1,0:T(8,128)S(1)}, u32[]{:S(2)}, u32[]{:S(2)}) collective-permute-start(f32[4,32,128]{2,1,0:T(8,128)S(1)} %get-tuple-element.20), channel_id=1, source_target_pairs={{0,8},{8,0},{16,24},{24,16},{1,9},{9,1},{17,25},{25,17},{2,10},{10... | collective-permute-start | bytes 196616 | tf_op jit(solution)/shard_map/ppermute | solution.py:33
  28.9 5.6 %collective-permute-start.4 = (f32[4,32,128]{2,1,0:T(8,128)S(1)}, f32[4,32,128]{2,1,0:T(8,128)S(1)}, u32[]{:S(2)}, u32[]{:S(2)}) collective-permute-start(f32[4,32,128]{2,1,0:T(8,128)S(1)} %get-tuple-element.21), channel_id=1, source_target_pairs={{0,16},{8,24},{16,0},{24,8},{1,17},{9,25},{17,1},{25,9},{2,18},{10... | collective-permute-start | bytes 196616 | tf_op jit(solution)/shard_map/ppermute | solution.py:33
  30.4 5.5 %collective-permute-start.5 = (f32[4,32,128]{2,1,0:T(8,128)S(1)}, f32[4,32,128]{2,1,0:T(8,128)S(1)}, u32[]{:S(2)}, u32[]{:S(2)}) collective-permute-start(f32[4,32,128]{2,1,0:T(8,128)S(1)} %get-tuple-element.22), channel_id=1, source_target_pairs={{0,24},{8,16},{16,8},{24,0},{1,25},{9,17},{17,9},{25,1},{2,26},{10... | collective-permute-start | bytes 196616 | tf_op jit(solution)/shard_map/ppermute | solution.py:33

commit v4 on v3

--- a/solution.py
+++ b/solution.py
@@ -24,17 +24,17 @@
 
 
 def source(index, step, peers):
-    if peers & (peers - 1) == 0:
-        return index ^ step
-    return lax.rem(index + (peers - step), peers)
+    return partner(index, step if peers & (peers - 1) == 0 else peers - step, peers)
 
 
 def exchange(value, step, peers):
     return lax.ppermute(value, "lat", [(i, partner(i, step, peers)) for i in range(peers)])
 
 
-def round_up(value, multiple):
-    return -(-value // multiple) * multiple
+def to_all(blocks, devices):
+    rows, width = blocks.shape
+    blocks = blocks.reshape(devices, rows // devices, 1, width)
+    return lax.all_to_all(blocks, ("lat", "lon"), 0, 0, tiled=True).reshape(rows, width)
 
 
 def row_weights(line_total):
@@ -51,17 +51,26 @@
     )
 
 
+def block_rows(bands, keys, rows):
+    return 2 * keys + rows
+
+
+def term_rows(keys):
+    return 2 * keys + len(OFFSETS)
+
+
 def in_hbm(array):
     return pltpu.with_memory_space_constraint(array, pltpu.HBM)
 
 
 def pack_kernel(bands, sectors, width, keys, *refs):
-    key_ref, value_ref, query_ref, cotangent_ref, block_ref = refs[:5]
+    key_ref, value_ref, query_ref, cotangent_ref, sent_ref = refs[:5]
     part_refs = refs[5 : 5 + bands]
-    key_own, value_own, first_own, last_own, sems = refs[5 + bands :]
+    key_own, value_own, first_own, last_own, block_ref, sems = refs[5 + bands :]
     band = lax.axis_index("lat")
     sector = lax.axis_index("lon")
     rows, columns = query_ref.shape[:2]
+    sent = block_rows(bands, keys, rows)
 
     small = [
         pltpu.make_async_copy(source_ref, target_ref, sems.at[i])
@@ -98,11 +107,20 @@
         for to_sector in range(sectors):
             device = to_band * sectors + to_sector
             is_next = lax.rem(to_sector - sector + sectors, sectors) == 1
-            block_ref[device, 0:keys, :] = key
-            block_ref[device, keys : 2 * keys, :] = value
-            block_ref[device, 2 * keys : 2 * keys + rows, :] = jnp.where(is_next, last, first)
+            start = device * sent
+            block_ref[start : start + keys, :] = key
+            start = start + keys
+            block_ref[start : start + keys, :] = value
+            block_ref[start + keys : start + keys + rows, :] = jnp.where(is_next, last, first)
+    send = pltpu.make_async_copy(block_ref, sent_ref, sems.at[len(small) + len(large)])
+    send.start()
     for copy in large:
         copy.wait()
+    send.wait()
+
+
+def arrival_kernel(part_ref, out_ref):
+    out_ref[...] = part_ref[...]
 
 
 def heads_of(matrix, width):
@@ -124,14 +142,75 @@
     return result
 
 
-def dot(left, right, left_dim, right_dim):
+def rows_from_all(rows_ref, first, keys, devices, sent):
+    return jnp.concatenate(
+        [rows_ref[pl.ds(first + k, devices, stride=sent), :] for k in range(keys)], 0
+    )
+
+
+def dot(left, right, left_dim, right_dim, precision=None):
     return lax.dot_general(
         left,
         right,
         (((left_dim,), (right_dim,)), ((), ())),
-        precision=HIGH,
+        precision=precision,
         preferred_element_type=jnp.float32,
     )
+
+
+def split(value, terms):
+    result = []
+    for _ in range(terms):
+        result.append(value.astype(jnp.bfloat16))
+        value = value - result[-1].astype(jnp.float32)
+    return result
+
+
+def rows_by_tokens(rows, tokens):
+    count = rows.shape[0]
+    large, middle, small = split(rows, 3)
+    token_large, token_middle, token_small = split(tokens, 3)
+    left = jnp.concatenate(
+        [
+            jnp.concatenate([large, large], 1),
+            jnp.concatenate([middle, middle], 1),
+            jnp.concatenate([small, jnp.zeros_like(small)], 1),
+        ],
+        0,
+    )
+    main = dot(left, jnp.concatenate([token_large, token_middle], 1), 1, 1)
+    rest = dot(large, token_small, 1, 1)
+    return main[0:count] + (main[count : 2 * count] + (main[2 * count :] + rest))
+
+
+def sum_over_tokens(left, right):
+    count, width = left.shape[0], right.shape[1]
+    every = dot(jnp.concatenate(split(left, 2), 0), jnp.concatenate(split(right, 2), 1), 1, 0)
+    top, bottom = every[0:count], every[count:]
+    return top[:, 0:width] + (top[:, width:] + bottom[:, 0:width] + bottom[:, width:])
+
+
+def mix_rows(weights, rows):
+    width = rows.shape[1]
+    right = jnp.concatenate(split(rows, 2), 1)
+    every = dot(jnp.concatenate(split(weights, 2), 0), jnp.concatenate([right, right], 0), 0, 0)
+    return every[:, 0:width] + every[:, width:]
+
+
+def mix_rows_exactly(weights, rows):
+    width = rows.shape[1]
+    large, middle, small = split(weights, 3)
+    row_large, row_middle, row_small = split(rows, 3)
+    zero = jnp.zeros_like(row_large)
+    right = jnp.concatenate(
+        [
+            jnp.concatenate([row_large, row_large, row_large, zero], 0),
+            jnp.concatenate([row_middle, row_middle, zero, row_small], 0),
+        ],
+        1,
+    )
+    every = dot(jnp.concatenate([large, middle, small, large], 0), right, 0, 0)
+    return every[:, 0:width] + every[:, width:]
 
 
 def attention_kernel(bands, sectors, width, keys, *refs):
@@ -148,7 +227,9 @@
     scale = HD ** (-0.5)
     weights = row_weights(lines)
     heads = width // HD
-    key_total = bands * sectors * keys
+    devices = bands * sectors
+    key_total = devices * keys
+    sent = block_rows(bands, keys, rows)
 
     for step, part_ref in enumerate(part_refs):
         start = source(band, step, bands) * rows
@@ -161,8 +242,8 @@
         r = 2 * keys + r
         inner = weighted_ref[1 + line, edge : edge + columns, :]
         weighted_ref[1 + line, edge : edge + columns, :] = inner * weights[line]
-        left = rows_ref[b * sectors + before, r : r + 1, :]
-        right = rows_ref[b * sectors + after, r : r + 1, :]
+        left = rows_ref[pl.ds((b * sectors + before) * sent + r, 1), :]
+        right = rows_ref[pl.ds((b * sectors + after) * sent + r, 1), :]
         weighted_ref[1 + line, edge - 1 : edge, :] = left * weights[line]
         weighted_ref[1 + line, edge + columns : edge + columns + 1, :] = right * weights[line]
     zeros = jnp.zeros(weighted_ref.shape[1:], jnp.float32)
@@ -182,22 +263,20 @@
             total = total + tap * shifted(line, offset)
         grad_ref[line] = total
 
-    key_all = rows_ref[:, 0:keys, :].reshape(key_total, width)
-    value_all = rows_ref[:, keys : 2 * keys, :].reshape(key_total, width)
-    key_heads = heads_of(key_all, width)
-    value_heads = heads_of(value_all, width)
+    key_heads = heads_of(rows_from_all(rows_ref, 0, keys, devices, sent), width)
+    value_heads = heads_of(rows_from_all(rows_ref, keys, keys, devices, sent), width)
     query = query_ref[...].reshape(tokens, width)
     grad = grad_ref[...].reshape(tokens, width)
 
-    logits = dot(key_heads, query, 1, 1) * scale
+    logits = rows_by_tokens(key_heads, query) * scale
     prob_list = []
     for h in range(heads):
         part = logits[h * key_total : (h + 1) * key_total]
         raised = jnp.exp(part - jnp.max(part, 0, keepdims=True))
         prob_list.append(raised / jnp.sum(raised, 0, keepdims=True))
     probs = jnp.concatenate(prob_list, 0)
-    out_ref[...] = dot(probs, value_heads, 0, 0).reshape(lines, columns, width)
-    prob_grad = dot(value_heads, grad, 1, 1)
+    out_ref[...] = mix_rows(probs, value_heads).reshape(lines, columns, width)
+    prob_grad = rows_by_tokens(value_heads, grad)
     logit_grad_list = []
     for h in range(heads):
         part = prob_grad[h * key_total : (h + 1) * key_total]
@@ -205,8 +284,8 @@
         logit_grad_list.append(prob_list[h] * (part - row_dot))
     logit_grad = jnp.concatenate(logit_grad_list, 0)
 
-    key_grad = own_heads(dot(logit_grad, query, 1, 0), width, key_total) * scale
-    value_grad = own_heads(dot(probs, grad, 1, 0), width, key_total)
+    key_grad = own_heads(sum_over_tokens(logit_grad, query), width, key_total) * scale
+    value_grad = own_heads(sum_over_tokens(probs, grad), width, key_total)
 
     sums = [jnp.zeros((SUBLANES, width), jnp.float32) for _ in OFFSETS]
     for line in range(lines):
@@ -216,28 +295,29 @@
             for c in range(0, columns, SUBLANES):
                 sums[t] = sums[t] + product[c : c + SUBLANES]
     tap_sum = jnp.concatenate([jnp.sum(s, 0, keepdims=True) for s in sums], 0)
-    used = 2 * keys + len(OFFSETS)
-    for device in range(bands * sectors):
-        mine = slice(device * keys, (device + 1) * keys)
-        start = device * used
-        terms_ref[start : start + keys, :] = key_grad[mine]
-        terms_ref[start + keys : start + 2 * keys, :] = value_grad[mine]
-        terms_ref[start + 2 * keys : start + used, :] = tap_sum
-
-    query_grad = (dot(logit_grad, key_heads, 0, 0) * scale).reshape(lines, columns, width)
-    out_ref[...] = query_grad
-    for step, query_grad_ref in enumerate(query_grad_refs):
-        query_grad_ref[...] = out_ref[pl.ds(partner(band, step, bands) * rows, rows)]
+    used = term_rows(keys)
+    for k in range(keys):
+        mine = slice(k * devices, (k + 1) * devices)
+        terms_ref[pl.ds(k, devices, stride=used), :] = key_grad[mine]
+        terms_ref[pl.ds(keys + k, devices, stride=used), :] = value_grad[mine]
+    for device in range(devices):
+        terms_ref[device * used + 2 * keys : (device + 1) * used, :] = tap_sum
+
+    out_ref[...] = (mix_rows_exactly(logit_grad, key_heads) * scale).reshape(out_ref.shape)
+    for step, part_ref in enumerate(query_grad_refs):
+        part_ref[...] = out_ref[pl.ds(partner(band, step, bands) * rows, rows)]
 
 
 def finish_kernel(bands, sectors, width, keys, *refs):
     part_refs = refs[:bands]
     terms_ref, query_ref, key_ref, value_ref, taps_ref = refs[bands:]
     band = lax.axis_index("lat")
+    devices = bands * sectors
+    rows, columns = query_ref.shape[:2]
     for step, part_ref in enumerate(part_refs):
         lanes = pl.ds(pl.multiple_of(source(band, step, bands) * width, width), width)
         query_ref[:, :, lanes] = part_ref[...]
-    used = 2 * keys + len(OFFSETS)
+    used = term_rows(keys)
     parts = []
     for to_band in range(bands):
         lanes = slice(to_band * width, (to_band + 1) * width)
@@ -262,40 +342,54 @@
     width = channels // bands
     lines = rows * bands
 
-    sent_rows = round_up(2 * keys + rows, SUBLANES)
+    sent_rows = block_rows(bands, keys, rows)
     part_shape = (2, rows, columns, width)
     anywhere = pl.BlockSpec(memory_space=pl.ANY)
+    here = pl.BlockSpec(memory_space=pltpu.VMEM)
     row_blocks, *parts = pl.pallas_call(
         functools.partial(pack_kernel, bands, sectors, width, keys),
         out_shape=[
             jax.ShapeDtypeStruct(s, jnp.float32)
-            for s in [(devices, sent_rows, width)] + [part_shape] * bands
+            for s in [(devices * sent_rows, width)] + [part_shape] * bands
         ],
         in_specs=[anywhere] * 4,
+        out_specs=[anywhere] + [here] * bands,
         scratch_shapes=[
             pltpu.VMEM((keys, channels), jnp.float32),
             pltpu.VMEM((keys, channels), jnp.float32),
             pltpu.VMEM((rows, SUBLANES, channels), jnp.float32),
             pltpu.VMEM((rows, SUBLANES, channels), jnp.float32),
-            pltpu.SemaphoreType.DMA((4 + 2 * bands,)),
+            pltpu.VMEM((devices * sent_rows, width), jnp.float32),
+            pltpu.SemaphoreType.DMA((5 + 2 * bands,)),
         ],
         compiler_params=pltpu.CompilerParams(vmem_limit_bytes=VMEM_LIMIT),
     )(*[in_hbm(x) for x in (key_rows, value_rows, queries, cotangent)])
-    row_blocks = lax.all_to_all(row_blocks, ("lat", "lon"), 0, 0, tiled=True)
-    parts = [parts[0]] + [exchange(parts[s], s, bands) for s in range(1, bands)]
-
-    sent_terms = 2 * keys + len(OFFSETS)
+    row_blocks = to_all(row_blocks, devices)
+    (first_part,) = pl.pallas_call(
+        arrival_kernel,
+        out_shape=[jax.ShapeDtypeStruct(part_shape, jnp.float32)],
+        cost_estimate=pl.CostEstimate(flops=10**9, bytes_accessed=10**6, transcendentals=0),
+        compiler_params=pltpu.CompilerParams(vmem_limit_bytes=VMEM_LIMIT),
+    )(exchange(parts[-1], bands - 1, bands))
+    parts = [parts[0]] + [exchange(parts[s], s, bands) for s in range(1, bands - 1)] + [first_part]
+
     grid = (lines, columns, width)
+    heads = width // HD
     terms, *grad_parts = vmem_call(
         functools.partial(attention_kernel, bands, sectors, width, keys),
-        [(devices * sent_terms, width)] + [(rows, columns, width)] * bands,
-        [grid, (lines + 2, columns + 2 * SUBLANES, width), grid, grid],
+        [(devices * term_rows(keys), width)] + [(rows, columns, width)] * bands,
+        [
+            grid,
+            (lines + 2, columns + 2 * SUBLANES, width),
+            grid,
+            grid,
+        ],
     )(*parts, row_blocks, conv_taps)
 
-    terms = terms.reshape(devices, sent_terms, 1, width)
-    terms = lax.all_to_all(terms, ("lat", "lon"), 0, 0, tiled=True)
-    terms = terms.reshape(devices * sent_terms, width)
-    grad_parts = [grad_parts[0]] + [exchange(grad_parts[s], s, bands) for s in range(1, bands)]
+    terms = to_all(terms, devices)
+    grad_parts = [grad_parts[0]] + [
+        exchange(grad_parts[s], s, bands) for s in range(1, bands)
+    ]
     query_grad, key_grad, value_grad, tap_update = pl.pallas_call(
         functools.partial(finish_kernel, bands, sectors, width, keys),
         out_shape=[
@@ -477,8 +571,10 @@
 def body(queries, key_rows, value_rows, cotangent, conv_taps):
     bands = lax.axis_size("lat")
     sectors = lax.axis_size("lon")
-    columns, channels = queries.shape[1:]
-    if channels % (bands * LANES) == 0 and sectors > 2 and columns % SUBLANES == 0:
+    rows, columns, channels = queries.shape
+    whole_heads = channels % (bands * LANES) == 0
+    whole_tiles = columns % SUBLANES == 0 and (rows * columns) % LANES == 0
+    if whole_heads and whole_tiles and sectors > 2:
         return split_heads_body(queries, key_rows, value_rows, cotangent, conv_taps)
     return whole_rows_body(queries, key_rows, value_rows, cotangent, conv_taps)
 

time: 37 us -> 33.7 us (0.911)
  waiting for transfers between devices: 12.7 us -> 9.8 us
  Pallas kernels: 5 us -> 4.18 us
  starting transfers between devices: 18.3 us -> 18.7 us
    ppermute x6, starting transfers between devices: 7.11 us -> 10.8 us  [exchange(): lax.ppermute(value, 'lat', [(i, partner(i, step, peers)) for i in range(p...]
    all_to_all x2, starting transfers between devices: 11.2 us -> 7.93 us  [to_all(): lax.all_to_all(blocks, ('lat', 'lon'), 0, 0, tiled=True)]
    ppermute x6, waiting for transfers between devices: 12.7 us -> 9.77 us  [exchange(): lax.ppermute(value, 'lat', [(i, partner(i, step, peers)) for i in range(p...]
    pallas_call x1, Pallas kernels: 2.31 us -> 1.69 us  [split_heads_body(): vmem_call(functools.partial(attention_kernel, bands, sectors, width, keys...]
where the time goes in v4:
time: 33.7 us; the launch traced here: 33.4 us
  starting transfers between devices  18.7 us (55%)
  waiting for transfers between devices  9.8 us (29%)
  Pallas kernels  4.18 us (12%)
  between operations  0.67 us (2%)
    ppermute x6, starting transfers between devices, exchange(): lax.ppermute(value, 'lat', [(i, partner(i, step, peers)) for i in range(p...  10.8 us
    ppermute x6, waiting for transfers between devices, exchange(): lax.ppermute(value, 'lat', [(i, partner(i, step, peers)) for i in range(p...  9.77 us
    all_to_all x2, starting transfers between devices, to_all(): lax.all_to_all(blocks, ('lat', 'lon'), 0, 0, tiled=True)  7.93 us
    pallas_call x1, Pallas kernels, split_heads_body(): pl.pallas_call(functools.partial(pack_kernel, bands, sectors, width, keys...  1.7 us
    pallas_call x1, Pallas kernels, split_heads_body(): vmem_call(functools.partial(attention_kernel, bands, sectors, width, keys...  1.69 us
    pallas_call x1, Pallas kernels, split_heads_body(): pl.pallas_call(functools.partial(finish_kernel, bands, sectors, width, ke...  0.78 us
  transfers between devices with their start and end apart: 8, of which 5 were waited for; matrix products, arithmetic and copies ran while one was open for 0% of the time, Pallas kernels for 0%

profile of v4, /device:TPU:0, one launch (start us, length us, event | category | flops | bytes accessed | tf_op | source)
XLA Modules:
  0.0 33.4 jit_solution(11660305634977525306)
XLA Ops:
  0.6 1.7 %shard_map.84 = (f32[192,128]{1,0:T(8,128)}, f32[2,4,32,128]{3,2,1,0:T(8,128)S(1)}, f32[2,4,32,128]{3,2,1,0:T(8,128)S(1)}, f32[2,4,32,128]{3,2,1,0:T(8,128)S(1)}, f32[2,4,32,128]{3,2,1,0:T(8,128)S(1)}) custom-call(f32[1,512]{1,0:T(1,128)} %refs_0_.1, f32[1,512]{1,0:T(1,128)} %refs_1_.1, f32[4,32,512]{2,1,0:T(8,128)} %refs_2_.1, f32[4,32,512]{2,1,0:T(8,128)} %refs_3_.1), custom_call_target="tpu_custom_call" | custom-call | tf_op jit(solution)/shard_map/pallas_call | solution.py:349
  2.3 4.0 %collective-permute-start.2 = (f32[2,4,32,128]{3,2,1,0:T(8,128)S(1)}, f32[2,4,32,128]{3,2,1,0:T(8,128)S(1)}, u32[]{:S(2)}, u32[]{:S(2)}) collective-permute-start(f32[2,4,32,128]{3,2,1,0:T(8,128)S(1)} %get-tuple-element.17), channel_id=1, source_target_pairs={{0,24},{8,16},{16,8},{24,0},{1,25},{9,17},{17,9},{25,1},{2,26},{10... | collective-permute-start | bytes 393224 | tf_op jit(solution)/shard_map/ppermute | solution.py:31
  6.3 4.0 %all-to-all-start = ((f32[32,6,1,128]{3,2,1,0:T(1,128)}), f32[32,6,1,128]{3,2,1,0:T(1,128)S(1)}, u32[]{:S(2)}, u32[]{:S(2)}) async-start(f32[32,6,1,128]{3,2,1,0:T(1,128)} %bitcast), calls=%async_computation | async-start | bytes 196608 | tf_op jit(solution)/shard_map/all_to_all | solution.py:37
  10.3 1.8 %collective-permute-start = (f32[2,4,32,128]{3,2,1,0:T(8,128)S(1)}, f32[2,4,32,128]{3,2,1,0:T(8,128)S(1)}, u32[]{:S(2)}, u32[]{:S(2)}) collective-permute-start(f32[2,4,32,128]{3,2,1,0:T(8,128)S(1)} %get-tuple-element.15), channel_id=1, source_target_pairs={{0,8},{8,0},{16,24},{24,16},{1,9},{9,1},{17,25},{25,17},{2,10},{10... | collective-permute-start | bytes 393224 | tf_op jit(solution)/shard_map/ppermute | solution.py:31
  12.1 0.0 copy-start
  12.1 1.5 %collective-permute-start.1 = (f32[2,4,32,128]{3,2,1,0:T(8,128)S(1)}, f32[2,4,32,128]{3,2,1,0:T(8,128)S(1)}, u32[]{:S(2)}, u32[]{:S(2)}) collective-permute-start(f32[2,4,32,128]{3,2,1,0:T(8,128)S(1)} %get-tuple-element.16), channel_id=1, source_target_pairs={{0,16},{8,24},{16,0},{24,8},{1,17},{9,25},{17,1},{25,9},{2,18},{10... | collective-permute-start | bytes 393224 | tf_op jit(solution)/shard_map/ppermute | solution.py:31
  13.6 0.0 collective-permute-done.2.part_ref
  13.6 3.3 %collective-permute-done.refs_1_ = f32[2,4,32,128]{3,2,1,0:T(8,128)S(1)} collective-permute-done((f32[2,4,32,128]{3,2,1,0:T(8,128)S(1)}, f32[2,4,32,128]{3,2,1,0:T(8,128)S(1)}, u32[]{:S(2)}, u32[]{:S(2)}) %collective-permute-start) | collective-permute-done | bytes 131104 | tf_op jit(solution)/shard_map/ppermute | solution.py:31
  16.9 1.2 %collective-permute-done.1.refs_2_ = f32[2,4,32,128]{3,2,1,0:T(8,128)S(1)} collective-permute-done((f32[2,4,32,128]{3,2,1,0:T(8,128)S(1)}, f32[2,4,32,128]{3,2,1,0:T(8,128)S(1)}, u32[]{:S(2)}, u32[]{:S(2)}) %collective-permute-start.1) | collective-permute-done | bytes 131104 | tf_op jit(solution)/shard_map/ppermute | solution.py:31
  18.1 0.0 all-to-all-done
  18.1 0.0 copy-done
  18.1 1.7 %shard_map.86 = (f32[352,128]{1,0:T(8,128)}, f32[4,32,128]{2,1,0:T(8,128)S(1)}, f32[4,32,128]{2,1,0:T(8,128)S(1)}, f32[4,32,128]{2,1,0:T(8,128)S(1)}, f32[4,32,128]{2,1,0:T(8,128)S(1)}) custom-call(f32[2,4,32,128]{3,2,1,0:T(8,128)S(1)} %get-tuple-element.14.refs_0_, f32[2,4,32,128]{3,2,1,0:T(8,128)S(1)} %collective-permute-done.refs_1_, ...), custom_call_target="tpu_custom_call" | custom-call | tf_op jit(solution)/shard_map/pallas_call | solution.py:378
  19.8 4.0 %all-to-all-start.1 = ((f32[32,11,1,128]{3,2,1,0:T(1,128)}), f32[32,11,1,128]{3,2,1,0:T(1,128)S(1)}, u32[]{:S(2)}, u32[]{:S(2)}) async-start(f32[32,11,1,128]{3,2,1,0:T(1,128)} %bitcast.2), calls=%async_computation.1 | async-start | bytes 360448 | tf_op jit(solution)/shard_map/all_to_all | solution.py:37
  23.8 1.8 %collective-permute-start.3 = (f32[4,32,128]{2,1,0:T(8,128)S(1)}, f32[4,32,128]{2,1,0:T(8,128)S(1)}, u32[]{:S(2)}, u32[]{:S(2)}) collective-permute-start(f32[4,32,128]{2,1,0:T(8,128)S(1)} %get-tuple-element.20), channel_id=1, source_target_pairs={{0,8},{8,0},{16,24},{24,16},{1,9},{9,1},{17,25},{25,17},{2,10},{10... | collective-permute-start | bytes 196616 | tf_op jit(solution)/shard_map/ppermute | solution.py:31
  25.6 1.5 %collective-permute-start.4 = (f32[4,32,128]{2,1,0:T(8,128)S(1)}, f32[4,32,128]{2,1,0:T(8,128)S(1)}, u32[]{:S(2)}, u32[]{:S(2)}) collective-permute-start(f32[4,32,128]{2,1,0:T(8,128)S(1)} %get-tuple-element.21), channel_id=1, source_target_pairs={{0,16},{8,24},{16,0},{24,8},{1,17},{9,25},{17,1},{25,9},{2,18},{10... | collective-permute-start | bytes 196616 | tf_op jit(solution)/shard_map/ppermute | solution.py:31
  27.1 0.3 collective-permute-start.5
  27.4 1.8 %collective-permute-done.3.refs_1_ = f32[4,32,128]{2,1,0:T(8,128)S(1)} collective-permute-done((f32[4,32,128]{2,1,0:T(8,128)S(1)}, f32[4,32,128]{2,1,0:T(8,128)S(1)}, u32[]{:S(2)}, u32[]{:S(2)}) %collective-permute-start.3) | collective-permute-done | bytes 65568 | tf_op jit(solution)/shard_map/ppermute | solution.py:31
  29.2 2.1 %collective-permute-done.4.refs_2_ = f32[4,32,128]{2,1,0:T(8,128)S(1)} collective-permute-done((f32[4,32,128]{2,1,0:T(8,128)S(1)}, f32[4,32,128]{2,1,0:T(8,128)S(1)}, u32[]{:S(2)}, u32[]{:S(2)}) %collective-permute-start.4) | collective-permute-done | bytes 65568 | tf_op jit(solution)/shard_map/ppermute | solution.py:31
  31.2 1.4 %collective-permute-done.5.refs_3_ = f32[4,32,128]{2,1,0:T(8,128)S(1)} collective-permute-done((f32[4,32,128]{2,1,0:T(8,128)S(1)}, f32[4,32,128]{2,1,0:T(8,128)S(1)}, u32[]{:S(2)}, u32[]{:S(2)}) %collective-permute-start.5) | collective-permute-done | bytes 65568 | tf_op jit(solution)/shard_map/ppermute | solution.py:31
  32.6 0.0 all-to-all-done.1
  32.6 0.8 %shard_map.87 = (f32[4,32,512]{2,1,0:T(8,128)}, f32[1,512]{1,0:T(1,128)}, f32[1,512]{1,0:T(1,128)}, f32[9,512]{1,0:T(8,128)}) custom-call(f32[4,32,128]{2,1,0:T(8,128)S(1)} %get-tuple-element.19.refs_0_, f32[4,32,128]{2,1,0:T(8,128)S(1)} %collective-permute-done.3.refs_1_, f32[4,32,128]{2,1,0:T(8,128)S(1)} %collective-permute-done.4.refs_2_, ...), custom_call_target="tpu_custom_call" | custom-call | tf_op jit(solution)/shard_map/pallas_call | solution.py:393
  (1 shorter events, 0.0 us)
Async XLA Ops:
  2.3 11.2 %collective-permute-start.2 = (f32[2,4,32,128]{3,2,1,0:T(8,128)S(1)}, f32[2,4,32,128]{3,2,1,0:T(8,128)S(1)}, u32[]{:S(2)}, u32[]{:S(2)}) collective-permute-start(f32[2,4,32,128]{3,2,1,0:T(8,128)S(1)} %get-tuple-element.17), channel_id=1, source_target_pairs={{0,24},{8,16},{16,8},{24,0},{1,25},{9,17},{17,9},{25,1},{2,26},{10... | collective-permute-start | bytes 393224 | tf_op jit(solution)/shard_map/ppermute | solution.py:31
  6.3 11.8 %all-to-all-start = ((f32[32,6,1,128]{3,2,1,0:T(1,128)}), f32[32,6,1,128]{3,2,1,0:T(1,128)S(1)}, u32[]{:S(2)}, u32[]{:S(2)}) async-start(f32[32,6,1,128]{3,2,1,0:T(1,128)} %bitcast), calls=%async_computation | async-start | bytes 196608 | tf_op jit(solution)/shard_map/all_to_all | solution.py:37
  10.3 6.6 %collective-permute-start = (f32[2,4,32,128]{3,2,1,0:T(8,128)S(1)}, f32[2,4,32,128]{3,2,1,0:T(8,128)S(1)}, u32[]{:S(2)}, u32[]{:S(2)}) collective-permute-start(f32[2,4,32,128]{3,2,1,0:T(8,128)S(1)} %get-tuple-element.15), channel_id=1, source_target_pairs={{0,8},{8,0},{16,24},{24,16},{1,9},{9,1},{17,25},{25,17},{2,10},{10... | collective-permute-start | bytes 393224 | tf_op jit(solution)/shard_map/ppermute | solution.py:31
  12.1 6.0 %copy-start = (f32[9,512]{1,0:T(8,128)S(1)}, f32[9,512]{1,0:T(8,128)}, u32[]{:S(2)}) copy-start(f32[9,512]{1,0:T(8,128)} %refs_5_.1) | copy-start | bytes 55300
  12.1 6.0 %collective-permute-start.1 = (f32[2,4,32,128]{3,2,1,0:T(8,128)S(1)}, f32[2,4,32,128]{3,2,1,0:T(8,128)S(1)}, u32[]{:S(2)}, u32[]{:S(2)}) collective-permute-start(f32[2,4,32,128]{3,2,1,0:T(8,128)S(1)} %get-tuple-element.16), channel_id=1, source_target_pairs={{0,16},{8,24},{16,0},{24,8},{1,17},{9,25},{17,1},{25,9},{2,18},{10... | collective-permute-start | bytes 393224 | tf_op jit(solution)/shard_map/ppermute | solution.py:31
  19.8 12.8 %all-to-all-start.1 = ((f32[32,11,1,128]{3,2,1,0:T(1,128)}), f32[32,11,1,128]{3,2,1,0:T(1,128)S(1)}, u32[]{:S(2)}, u32[]{:S(2)}) async-start(f32[32,11,1,128]{3,2,1,0:T(1,128)} %bitcast.2), calls=%async_computation.1 | async-start | bytes 360448 | tf_op jit(solution)/shard_map/all_to_all | solution.py:37
  23.8 5.4 %collective-permute-start.3 = (f32[4,32,128]{2,1,0:T(8,128)S(1)}, f32[4,32,128]{2,1,0:T(8,128)S(1)}, u32[]{:S(2)}, u32[]{:S(2)}) collective-permute-start(f32[4,32,128]{2,1,0:T(8,128)S(1)} %get-tuple-element.20), channel_id=1, source_target_pairs={{0,8},{8,0},{16,24},{24,16},{1,9},{9,1},{17,25},{25,17},{2,10},{10... | collective-permute-start | bytes 196616 | tf_op jit(solution)/shard_map/ppermute | solution.py:31
  25.6 5.6 %collective-permute-start.4 = (f32[4,32,128]{2,1,0:T(8,128)S(1)}, f32[4,32,128]{2,1,0:T(8,128)S(1)}, u32[]{:S(2)}, u32[]{:S(2)}) collective-permute-start(f32[4,32,128]{2,1,0:T(8,128)S(1)} %get-tuple-element.21), channel_id=1, source_target_pairs={{0,16},{8,24},{16,0},{24,8},{1,17},{9,25},{17,1},{25,9},{2,18},{10... | collective-permute-start | bytes 196616 | tf_op jit(solution)/shard_map/ppermute | solution.py:31
  27.1 5.5 %collective-permute-start.5 = (f32[4,32,128]{2,1,0:T(8,128)S(1)}, f32[4,32,128]{2,1,0:T(8,128)S(1)}, u32[]{:S(2)}, u32[]{:S(2)}) collective-permute-start(f32[4,32,128]{2,1,0:T(8,128)S(1)} %get-tuple-element.22), channel_id=1, source_target_pairs={{0,24},{8,16},{16,8},{24,0},{1,25},{9,17},{17,9},{25,1},{2,26},{10... | collective-permute-start | bytes 196616 | tf_op jit(solution)/shard_map/ppermute | solution.py:31

commit v5 on v4

--- a/solution.py
+++ b/solution.py
@@ -49,6 +49,22 @@
         scratch_shapes=[pltpu.VMEM(s, jnp.float32) for s in scratch],
         compiler_params=pltpu.CompilerParams(vmem_limit_bytes=VMEM_LIMIT),
     )
+
+
+def arrival_kernel(part_ref, out_ref):
+    out_ref[...] = part_ref[...]
+
+
+def exchange_all(parts, bands, ahead):
+    last = exchange(parts[-1], bands - 1, bands)
+    cost = pl.CostEstimate(flops=10**9, bytes_accessed=10**6, transcendentals=0)
+    (last,) = pl.pallas_call(
+        arrival_kernel,
+        out_shape=[jax.ShapeDtypeStruct(last.shape, jnp.float32)],
+        cost_estimate=cost if ahead else None,
+        compiler_params=pltpu.CompilerParams(vmem_limit_bytes=VMEM_LIMIT),
+    )(last)
+    return [parts[0]] + [exchange(parts[s], s, bands) for s in range(1, bands - 1)] + [last]
 
 
 def block_rows(bands, keys, rows):
@@ -78,8 +94,8 @@
             (
                 (key_ref, key_own),
                 (value_ref, value_own),
-                (cotangent_ref.at[:, 0:SUBLANES, :], first_own),
-                (cotangent_ref.at[:, columns - SUBLANES : columns, :], last_own),
+                (cotangent_ref.at[:, 0:1, :], first_own),
+                (cotangent_ref.at[:, columns - 1 : columns, :], last_own),
             )
         )
     ]
@@ -103,7 +119,7 @@
         key = key_own[:, lanes]
         value = value_own[:, lanes]
         first = first_own[:, 0, lanes]
-        last = last_own[:, SUBLANES - 1, lanes]
+        last = last_own[:, 0, lanes]
         for to_sector in range(sectors):
             device = to_band * sectors + to_sector
             is_next = lax.rem(to_sector - sector + sectors, sectors) == 1
@@ -117,10 +133,6 @@
     for copy in large:
         copy.wait()
     send.wait()
-
-
-def arrival_kernel(part_ref, out_ref):
-    out_ref[...] = part_ref[...]
 
 
 def heads_of(matrix, width):
@@ -357,21 +369,15 @@
         scratch_shapes=[
             pltpu.VMEM((keys, channels), jnp.float32),
             pltpu.VMEM((keys, channels), jnp.float32),
-            pltpu.VMEM((rows, SUBLANES, channels), jnp.float32),
-            pltpu.VMEM((rows, SUBLANES, channels), jnp.float32),
+            pltpu.VMEM((rows, 1, channels), jnp.float32),
+            pltpu.VMEM((rows, 1, channels), jnp.float32),
             pltpu.VMEM((devices * sent_rows, width), jnp.float32),
             pltpu.SemaphoreType.DMA((5 + 2 * bands,)),
         ],
         compiler_params=pltpu.CompilerParams(vmem_limit_bytes=VMEM_LIMIT),
     )(*[in_hbm(x) for x in (key_rows, value_rows, queries, cotangent)])
     row_blocks = to_all(row_blocks, devices)
-    (first_part,) = pl.pallas_call(
-        arrival_kernel,
-        out_shape=[jax.ShapeDtypeStruct(part_shape, jnp.float32)],
-        cost_estimate=pl.CostEstimate(flops=10**9, bytes_accessed=10**6, transcendentals=0),
-        compiler_params=pltpu.CompilerParams(vmem_limit_bytes=VMEM_LIMIT),
-    )(exchange(parts[-1], bands - 1, bands))
-    parts = [parts[0]] + [exchange(parts[s], s, bands) for s in range(1, bands - 1)] + [first_part]
+    parts = exchange_all(parts, bands, ahead=True)
 
     grid = (lines, columns, width)
     heads = width // HD
@@ -387,9 +393,7 @@
     )(*parts, row_blocks, conv_taps)
 
     terms = to_all(terms, devices)
-    grad_parts = [grad_parts[0]] + [
-        exchange(grad_parts[s], s, bands) for s in range(1, bands)
-    ]
+    grad_parts = exchange_all(grad_parts, bands, ahead=False)
     query_grad, key_grad, value_grad, tap_update = pl.pallas_call(
         functools.partial(finish_kernel, bands, sectors, width, keys),
         out_shape=[

time: 33.7 us -> 33.5 us (level)
    ppermute x6, waiting for transfers between devices: 9.77 us -> 9.11 us  [exchange(): lax.ppermute(value, 'lat', [(i, partner(i, step, peers)) for i in range(p...]
    all_to_all x2, waiting for transfers between devices: 0.02 us -> 0.48 us  [to_all(): lax.all_to_all(blocks, ('lat', 'lon'), 0, 0, tiled=True)]
  transfers between devices with their start and end apart: 8 -> 8, of which waited for: 5 -> 6; matrix products, arithmetic and copies ran while one was open for 0% -> 0% of each run, Pallas kernels for 0% -> 0%
where the time goes in v5:
time: 33.5 us; the launch traced here: 33 us
  starting transfers between devices  18.7 us (56%)
  waiting for transfers between devices  9.59 us (29%)
  Pallas kernels  4.03 us (12%)
  between operations  0.67 us (2%)
    ppermute x6, starting transfers between devices, exchange(): lax.ppermute(value, 'lat', [(i, partner(i, step, peers)) for i in range(p...  10.8 us
    ppermute x6, waiting for transfers between devices, exchange(): lax.ppermute(value, 'lat', [(i, partner(i, step, peers)) for i in range(p...  9.11 us
    all_to_all x2, starting transfers between devices, to_all(): lax.all_to_all(blocks, ('lat', 'lon'), 0, 0, tiled=True)  7.93 us
    pallas_call x1, Pallas kernels, split_heads_body(): vmem_call(functools.partial(attention_kernel, bands, sectors, width, keys...  1.69 us
    pallas_call x1, Pallas kernels, split_heads_body(): pl.pallas_call(functools.partial(pack_kernel, bands, sectors, width, keys...  1.56 us
    pallas_call x1, Pallas kernels, split_heads_body(): pl.pallas_call(functools.partial(finish_kernel, bands, sectors, width, ke...  0.78 us
  transfers between devices with their start and end apart: 8, of which 6 were waited for; matrix products, arithmetic and copies ran while one was open for 0% of the time, Pallas kernels for 0%

profile of v5, /device:TPU:0, one launch (start us, length us, event | category | flops | bytes accessed | tf_op | source)
XLA Modules:
  0.0 33.0 jit_solution(11851038348837973382)
XLA Ops:
  0.6 1.6 %shard_map.84 = (f32[192,128]{1,0:T(8,128)}, f32[2,4,32,128]{3,2,1,0:T(8,128)S(1)}, f32[2,4,32,128]{3,2,1,0:T(8,128)S(1)}, f32[2,4,32,128]{3,2,1,0:T(8,128)S(1)}, f32[2,4,32,128]{3,2,1,0:T(8,128)S(1)}) custom-call(f32[1,512]{1,0:T(1,128)} %refs_0_.1, f32[1,512]{1,0:T(1,128)} %refs_1_.1, f32[4,32,512]{2,1,0:T(8,128)} %refs_2_.1, f32[4,32,512]{2,1,0:T(8,128)} %refs_3_.1), custom_call_target="tpu_custom_call" | custom-call | tf_op jit(solution)/shard_map/pallas_call | solution.py:361
  2.2 4.0 %collective-permute-start.2 = (f32[2,4,32,128]{3,2,1,0:T(8,128)S(1)}, f32[2,4,32,128]{3,2,1,0:T(8,128)S(1)}, u32[]{:S(2)}, u32[]{:S(2)}) collective-permute-start(f32[2,4,32,128]{3,2,1,0:T(8,128)S(1)} %get-tuple-element.17), channel_id=1, source_target_pairs={{0,24},{8,16},{16,8},{24,0},{1,25},{9,17},{17,9},{25,1},{2,26},{10... | collective-permute-start | bytes 393224 | tf_op jit(solution)/shard_map/ppermute | solution.py:31
  6.2 4.0 %all-to-all-start = ((f32[32,6,1,128]{3,2,1,0:T(1,128)}), f32[32,6,1,128]{3,2,1,0:T(1,128)S(1)}, u32[]{:S(2)}, u32[]{:S(2)}) async-start(f32[32,6,1,128]{3,2,1,0:T(1,128)} %bitcast), calls=%async_computation | async-start | bytes 196608 | tf_op jit(solution)/shard_map/all_to_all | solution.py:37
  10.1 1.8 %collective-permute-start = (f32[2,4,32,128]{3,2,1,0:T(8,128)S(1)}, f32[2,4,32,128]{3,2,1,0:T(8,128)S(1)}, u32[]{:S(2)}, u32[]{:S(2)}) collective-permute-start(f32[2,4,32,128]{3,2,1,0:T(8,128)S(1)} %get-tuple-element.15), channel_id=1, source_target_pairs={{0,8},{8,0},{16,24},{24,16},{1,9},{9,1},{17,25},{25,17},{2,10},{10... | collective-permute-start | bytes 393224 | tf_op jit(solution)/shard_map/ppermute | solution.py:31
  12.0 0.0 copy-start
  12.0 1.5 %collective-permute-start.1 = (f32[2,4,32,128]{3,2,1,0:T(8,128)S(1)}, f32[2,4,32,128]{3,2,1,0:T(8,128)S(1)}, u32[]{:S(2)}, u32[]{:S(2)}) collective-permute-start(f32[2,4,32,128]{3,2,1,0:T(8,128)S(1)} %get-tuple-element.16), channel_id=1, source_target_pairs={{0,16},{8,24},{16,0},{24,8},{1,17},{9,25},{17,1},{25,9},{2,18},{10... | collective-permute-start | bytes 393224 | tf_op jit(solution)/shard_map/ppermute | solution.py:31
  13.4 0.0 collective-permute-done.2.part_ref
  13.4 3.3 %collective-permute-done.refs_1_ = f32[2,4,32,128]{3,2,1,0:T(8,128)S(1)} collective-permute-done((f32[2,4,32,128]{3,2,1,0:T(8,128)S(1)}, f32[2,4,32,128]{3,2,1,0:T(8,128)S(1)}, u32[]{:S(2)}, u32[]{:S(2)}) %collective-permute-start) | collective-permute-done | bytes 131104 | tf_op jit(solution)/shard_map/ppermute | solution.py:31
  16.8 1.2 %collective-permute-done.1.refs_2_ = f32[2,4,32,128]{3,2,1,0:T(8,128)S(1)} collective-permute-done((f32[2,4,32,128]{3,2,1,0:T(8,128)S(1)}, f32[2,4,32,128]{3,2,1,0:T(8,128)S(1)}, u32[]{:S(2)}, u32[]{:S(2)}) %collective-permute-start.1) | collective-permute-done | bytes 131104 | tf_op jit(solution)/shard_map/ppermute | solution.py:31
  18.0 0.0 all-to-all-done
  18.0 0.0 copy-done
  18.0 1.7 %shard_map.86 = (f32[352,128]{1,0:T(8,128)}, f32[4,32,128]{2,1,0:T(8,128)S(1)}, f32[4,32,128]{2,1,0:T(8,128)S(1)}, f32[4,32,128]{2,1,0:T(8,128)S(1)}, f32[4,32,128]{2,1,0:T(8,128)S(1)}) custom-call(f32[2,4,32,128]{3,2,1,0:T(8,128)S(1)} %get-tuple-element.14.refs_0_, f32[2,4,32,128]{3,2,1,0:T(8,128)S(1)} %collective-permute-done.refs_1_, ...), custom_call_target="tpu_custom_call" | custom-call | tf_op jit(solution)/shard_map/pallas_call | solution.py:384
  19.7 4.0 %all-to-all-start.1 = ((f32[32,11,1,128]{3,2,1,0:T(1,128)}), f32[32,11,1,128]{3,2,1,0:T(1,128)S(1)}, u32[]{:S(2)}, u32[]{:S(2)}) async-start(f32[32,11,1,128]{3,2,1,0:T(1,128)} %bitcast.2), calls=%async_computation.1 | async-start | bytes 360448 | tf_op jit(solution)/shard_map/all_to_all | solution.py:37
  23.7 2.7 %collective-permute-start.5 = (f32[4,32,128]{2,1,0:T(8,128)S(1)}, f32[4,32,128]{2,1,0:T(8,128)S(1)}, u32[]{:S(2)}, u32[]{:S(2)}) collective-permute-start(f32[4,32,128]{2,1,0:T(8,128)S(1)} %get-tuple-element.22), channel_id=1, source_target_pairs={{0,24},{8,16},{16,8},{24,0},{1,25},{9,17},{17,9},{25,1},{2,26},{10... | collective-permute-start | bytes 196616 | tf_op jit(solution)/shard_map/ppermute | solution.py:31
  26.4 0.6 %collective-permute-start.3 = (f32[4,32,128]{2,1,0:T(8,128)S(1)}, f32[4,32,128]{2,1,0:T(8,128)S(1)}, u32[]{:S(2)}, u32[]{:S(2)}) collective-permute-start(f32[4,32,128]{2,1,0:T(8,128)S(1)} %get-tuple-element.20), channel_id=1, source_target_pairs={{0,8},{8,0},{16,24},{24,16},{1,9},{9,1},{17,25},{25,17},{2,10},{10... | collective-permute-start | bytes 196616 | tf_op jit(solution)/shard_map/ppermute | solution.py:31
  27.0 0.3 collective-permute-start.4
  27.2 3.3 %collective-permute-done.5.part_ref = f32[4,32,128]{2,1,0:T(8,128)S(1)} collective-permute-done((f32[4,32,128]{2,1,0:T(8,128)S(1)}, f32[4,32,128]{2,1,0:T(8,128)S(1)}, u32[]{:S(2)}, u32[]{:S(2)}) %collective-permute-start.5) | collective-permute-done | bytes 65568 | tf_op jit(solution)/shard_map/ppermute | solution.py:31
  30.5 1.1 %collective-permute-done.3.refs_1_ = f32[4,32,128]{2,1,0:T(8,128)S(1)} collective-permute-done((f32[4,32,128]{2,1,0:T(8,128)S(1)}, f32[4,32,128]{2,1,0:T(8,128)S(1)}, u32[]{:S(2)}, u32[]{:S(2)}) %collective-permute-start.3) | collective-permute-done | bytes 65568 | tf_op jit(solution)/shard_map/ppermute | solution.py:31
  31.6 0.2 collective-permute-done.4.refs_2_
  31.8 0.5 %all-to-all-done.1 = f32[32,11,1,128]{3,2,1,0:T(1,128)S(1)} async-done(((f32[32,11,1,128]{3,2,1,0:T(1,128)}), f32[32,11,1,128]{3,2,1,0:T(1,128)S(1)}, u32[]{:S(2)}, u32[]{:S(2)}) %all-to-all-start.1) | async-done | bytes 180256 | tf_op jit(solution)/shard_map/all_to_all | solution.py:37
  32.3 0.8 %shard_map.88 = (f32[4,32,512]{2,1,0:T(8,128)}, f32[1,512]{1,0:T(1,128)}, f32[1,512]{1,0:T(1,128)}, f32[9,512]{1,0:T(8,128)}) custom-call(f32[4,32,128]{2,1,0:T(8,128)S(1)} %get-tuple-element.19.refs_0_, f32[4,32,128]{2,1,0:T(8,128)S(1)} %collective-permute-done.3.refs_1_, f32[4,32,128]{2,1,0:T(8,128)S(1)} %collective-permute-done.4.refs_2_, ...), custom_call_target="tpu_custom_call" | custom-call | tf_op jit(solution)/shard_map/pallas_call | solution.py:397
  (2 shorter events, 0.0 us)
Async XLA Ops:
  2.2 11.2 %collective-permute-start.2 = (f32[2,4,32,128]{3,2,1,0:T(8,128)S(1)}, f32[2,4,32,128]{3,2,1,0:T(8,128)S(1)}, u32[]{:S(2)}, u32[]{:S(2)}) collective-permute-start(f32[2,4,32,128]{3,2,1,0:T(8,128)S(1)} %get-tuple-element.17), channel_id=1, source_target_pairs={{0,24},{8,16},{16,8},{24,0},{1,25},{9,17},{17,9},{25,1},{2,26},{10... | collective-permute-start | bytes 393224 | tf_op jit(solution)/shard_map/ppermute | solution.py:31
  6.2 11.8 %all-to-all-start = ((f32[32,6,1,128]{3,2,1,0:T(1,128)}), f32[32,6,1,128]{3,2,1,0:T(1,128)S(1)}, u32[]{:S(2)}, u32[]{:S(2)}) async-start(f32[32,6,1,128]{3,2,1,0:T(1,128)} %bitcast), calls=%async_computation | async-start | bytes 196608 | tf_op jit(solution)/shard_map/all_to_all | solution.py:37
  10.1 6.6 %collective-permute-start = (f32[2,4,32,128]{3,2,1,0:T(8,128)S(1)}, f32[2,4,32,128]{3,2,1,0:T(8,128)S(1)}, u32[]{:S(2)}, u32[]{:S(2)}) collective-permute-start(f32[2,4,32,128]{3,2,1,0:T(8,128)S(1)} %get-tuple-element.15), channel_id=1, source_target_pairs={{0,8},{8,0},{16,24},{24,16},{1,9},{9,1},{17,25},{25,17},{2,10},{10... | collective-permute-start | bytes 393224 | tf_op jit(solution)/shard_map/ppermute | solution.py:31
  12.0 6.0 %copy-start = (f32[9,512]{1,0:T(8,128)S(1)}, f32[9,512]{1,0:T(8,128)}, u32[]{:S(2)}) copy-start(f32[9,512]{1,0:T(8,128)} %refs_5_.1) | copy-start | bytes 55300
  12.0 6.0 %collective-permute-start.1 = (f32[2,4,32,128]{3,2,1,0:T(8,128)S(1)}, f32[2,4,32,128]{3,2,1,0:T(8,128)S(1)}, u32[]{:S(2)}, u32[]{:S(2)}) collective-permute-start(f32[2,4,32,128]{3,2,1,0:T(8,128)S(1)} %get-tuple-element.16), channel_id=1, source_target_pairs={{0,16},{8,24},{16,0},{24,8},{1,17},{9,25},{17,1},{25,9},{2,18},{10... | collective-permute-start | bytes 393224 | tf_op jit(solution)/shard_map/ppermute | solution.py:31
  19.7 12.6 %all-to-all-start.1 = ((f32[32,11,1,128]{3,2,1,0:T(1,128)}), f32[32,11,1,128]{3,2,1,0:T(1,128)S(1)}, u32[]{:S(2)}, u32[]{:S(2)}) async-start(f32[32,11,1,128]{3,2,1,0:T(1,128)} %bitcast.2), calls=%async_computation.1 | async-start | bytes 360448 | tf_op jit(solution)/shard_map/all_to_all | solution.py:37
  23.7 6.8 %collective-permute-start.5 = (f32[4,32,128]{2,1,0:T(8,128)S(1)}, f32[4,32,128]{2,1,0:T(8,128)S(1)}, u32[]{:S(2)}, u32[]{:S(2)}) collective-permute-start(f32[4,32,128]{2,1,0:T(8,128)S(1)} %get-tuple-element.22), channel_id=1, source_target_pairs={{0,24},{8,16},{16,8},{24,0},{1,25},{9,17},{17,9},{25,1},{2,26},{10... | collective-permute-start | bytes 196616 | tf_op jit(solution)/shard_map/ppermute | solution.py:31
  26.4 5.2 %collective-permute-start.3 = (f32[4,32,128]{2,1,0:T(8,128)S(1)}, f32[4,32,128]{2,1,0:T(8,128)S(1)}, u32[]{:S(2)}, u32[]{:S(2)}) collective-permute-start(f32[4,32,128]{2,1,0:T(8,128)S(1)} %get-tuple-element.20), channel_id=1, source_target_pairs={{0,8},{8,0},{16,24},{24,16},{1,9},{9,1},{17,25},{25,17},{2,10},{10... | collective-permute-start | bytes 196616 | tf_op jit(solution)/shard_map/ppermute | solution.py:31
  27.0 4.9 %collective-permute-start.4 = (f32[4,32,128]{2,1,0:T(8,128)S(1)}, f32[4,32,128]{2,1,0:T(8,128)S(1)}, u32[]{:S(2)}, u32[]{:S(2)}) collective-permute-start(f32[4,32,128]{2,1,0:T(8,128)S(1)} %get-tuple-element.21), channel_id=1, source_target_pairs={{0,16},{8,24},{16,0},{24,8},{1,17},{9,25},{17,1},{25,9},{2,18},{10... | collective-permute-start | bytes 196616 | tf_op jit(solution)/shard_map/ppermute | solution.py:31

commit v6 on v5

--- a/solution.py
+++ b/solution.py
@@ -57,7 +57,7 @@
 
 def exchange_all(parts, bands, ahead):
     last = exchange(parts[-1], bands - 1, bands)
-    cost = pl.CostEstimate(flops=10**9, bytes_accessed=10**6, transcendentals=0)
+    cost = pl.CostEstimate(flops=10**10, bytes_accessed=10**6, transcendentals=0)
     (last,) = pl.pallas_call(
         arrival_kernel,
         out_shape=[jax.ShapeDtypeStruct(last.shape, jnp.float32)],
@@ -160,12 +160,11 @@
     )
 
 
-def dot(left, right, left_dim, right_dim, precision=None):
+def dot(left, right, left_dim, right_dim):
     return lax.dot_general(
         left,
         right,
         (((left_dim,), (right_dim,)), ((), ())),
-        precision=precision,
         preferred_element_type=jnp.float32,
     )
 

time: 33.5 us -> 33.5 us (level)
  no operation moved by 1% of the time
where the time goes in v6:
time: 33.5 us; the launch traced here: 33 us
  starting transfers between devices  18.7 us (56%)
  waiting for transfers between devices  9.59 us (29%)
  Pallas kernels  4.03 us (12%)
  between operations  0.67 us (2%)
    ppermute x6, starting transfers between devices, exchange(): lax.ppermute(value, 'lat', [(i, partner(i, step, peers)) for i in range(p...  10.8 us
    ppermute x6, waiting for transfers between devices, exchange(): lax.ppermute(value, 'lat', [(i, partner(i, step, peers)) for i in range(p...  9.11 us
    all_to_all x2, starting transfers between devices, to_all(): lax.all_to_all(blocks, ('lat', 'lon'), 0, 0, tiled=True)  7.93 us
    pallas_call x1, Pallas kernels, split_heads_body(): vmem_call(functools.partial(attention_kernel, bands, sectors, width, keys...  1.69 us
    pallas_call x1, Pallas kernels, split_heads_body(): pl.pallas_call(functools.partial(pack_kernel, bands, sectors, width, keys...  1.56 us
    pallas_call x1, Pallas kernels, split_heads_body(): pl.pallas_call(functools.partial(finish_kernel, bands, sectors, width, ke...  0.78 us
  transfers between devices with their start and end apart: 8, of which 6 were waited for; matrix products, arithmetic and copies ran while one was open for 0% of the time, Pallas kernels for 0%

profile of v6, /device:TPU:0, one launch (start us, length us, event | category | flops | bytes accessed | tf_op | source)
XLA Modules:
  0.0 33.0 jit_solution(11851038348837973382)
XLA Ops:
  0.6 1.6 %shard_map.84 = (f32[192,128]{1,0:T(8,128)}, f32[2,4,32,128]{3,2,1,0:T(8,128)S(1)}, f32[2,4,32,128]{3,2,1,0:T(8,128)S(1)}, f32[2,4,32,128]{3,2,1,0:T(8,128)S(1)}, f32[2,4,32,128]{3,2,1,0:T(8,128)S(1)}) custom-call(f32[1,512]{1,0:T(1,128)} %refs_0_.1, f32[1,512]{1,0:T(1,128)} %refs_1_.1, f32[4,32,512]{2,1,0:T(8,128)} %refs_2_.1, f32[4,32,512]{2,1,0:T(8,128)} %refs_3_.1), custom_call_target="tpu_custom_call" | custom-call | tf_op jit(solution)/shard_map/pallas_call | solution.py:360
  2.2 4.0 %collective-permute-start.2 = (f32[2,4,32,128]{3,2,1,0:T(8,128)S(1)}, f32[2,4,32,128]{3,2,1,0:T(8,128)S(1)}, u32[]{:S(2)}, u32[]{:S(2)}) collective-permute-start(f32[2,4,32,128]{3,2,1,0:T(8,128)S(1)} %get-tuple-element.17), channel_id=1, source_target_pairs={{0,24},{8,16},{16,8},{24,0},{1,25},{9,17},{17,9},{25,1},{2,26},{10... | collective-permute-start | bytes 393224 | tf_op jit(solution)/shard_map/ppermute | solution.py:31
  6.2 4.0 %all-to-all-start = ((f32[32,6,1,128]{3,2,1,0:T(1,128)}), f32[32,6,1,128]{3,2,1,0:T(1,128)S(1)}, u32[]{:S(2)}, u32[]{:S(2)}) async-start(f32[32,6,1,128]{3,2,1,0:T(1,128)} %bitcast), calls=%async_computation | async-start | bytes 196608 | tf_op jit(solution)/shard_map/all_to_all | solution.py:37
  10.1 1.8 %collective-permute-start = (f32[2,4,32,128]{3,2,1,0:T(8,128)S(1)}, f32[2,4,32,128]{3,2,1,0:T(8,128)S(1)}, u32[]{:S(2)}, u32[]{:S(2)}) collective-permute-start(f32[2,4,32,128]{3,2,1,0:T(8,128)S(1)} %get-tuple-element.15), channel_id=1, source_target_pairs={{0,8},{8,0},{16,24},{24,16},{1,9},{9,1},{17,25},{25,17},{2,10},{10... | collective-permute-start | bytes 393224 | tf_op jit(solution)/shard_map/ppermute | solution.py:31
  12.0 0.0 copy-start
  12.0 1.5 %collective-permute-start.1 = (f32[2,4,32,128]{3,2,1,0:T(8,128)S(1)}, f32[2,4,32,128]{3,2,1,0:T(8,128)S(1)}, u32[]{:S(2)}, u32[]{:S(2)}) collective-permute-start(f32[2,4,32,128]{3,2,1,0:T(8,128)S(1)} %get-tuple-element.16), channel_id=1, source_target_pairs={{0,16},{8,24},{16,0},{24,8},{1,17},{9,25},{17,1},{25,9},{2,18},{10... | collective-permute-start | bytes 393224 | tf_op jit(solution)/shard_map/ppermute | solution.py:31
  13.4 0.0 collective-permute-done.2.part_ref
  13.4 3.3 %collective-permute-done.refs_1_ = f32[2,4,32,128]{3,2,1,0:T(8,128)S(1)} collective-permute-done((f32[2,4,32,128]{3,2,1,0:T(8,128)S(1)}, f32[2,4,32,128]{3,2,1,0:T(8,128)S(1)}, u32[]{:S(2)}, u32[]{:S(2)}) %collective-permute-start) | collective-permute-done | bytes 131104 | tf_op jit(solution)/shard_map/ppermute | solution.py:31
  16.8 1.2 %collective-permute-done.1.refs_2_ = f32[2,4,32,128]{3,2,1,0:T(8,128)S(1)} collective-permute-done((f32[2,4,32,128]{3,2,1,0:T(8,128)S(1)}, f32[2,4,32,128]{3,2,1,0:T(8,128)S(1)}, u32[]{:S(2)}, u32[]{:S(2)}) %collective-permute-start.1) | collective-permute-done | bytes 131104 | tf_op jit(solution)/shard_map/ppermute | solution.py:31
  18.0 0.0 all-to-all-done
  18.0 0.0 copy-done
  18.0 1.7 %shard_map.86 = (f32[352,128]{1,0:T(8,128)}, f32[4,32,128]{2,1,0:T(8,128)S(1)}, f32[4,32,128]{2,1,0:T(8,128)S(1)}, f32[4,32,128]{2,1,0:T(8,128)S(1)}, f32[4,32,128]{2,1,0:T(8,128)S(1)}) custom-call(f32[2,4,32,128]{3,2,1,0:T(8,128)S(1)} %get-tuple-element.14.refs_0_, f32[2,4,32,128]{3,2,1,0:T(8,128)S(1)} %collective-permute-done.refs_1_, ...), custom_call_target="tpu_custom_call" | custom-call | tf_op jit(solution)/shard_map/pallas_call | solution.py:383
  19.7 4.0 %all-to-all-start.1 = ((f32[32,11,1,128]{3,2,1,0:T(1,128)}), f32[32,11,1,128]{3,2,1,0:T(1,128)S(1)}, u32[]{:S(2)}, u32[]{:S(2)}) async-start(f32[32,11,1,128]{3,2,1,0:T(1,128)} %bitcast.2), calls=%async_computation.1 | async-start | bytes 360448 | tf_op jit(solution)/shard_map/all_to_all | solution.py:37
  23.7 2.7 %collective-permute-start.5 = (f32[4,32,128]{2,1,0:T(8,128)S(1)}, f32[4,32,128]{2,1,0:T(8,128)S(1)}, u32[]{:S(2)}, u32[]{:S(2)}) collective-permute-start(f32[4,32,128]{2,1,0:T(8,128)S(1)} %get-tuple-element.22), channel_id=1, source_target_pairs={{0,24},{8,16},{16,8},{24,0},{1,25},{9,17},{17,9},{25,1},{2,26},{10... | collective-permute-start | bytes 196616 | tf_op jit(solution)/shard_map/ppermute | solution.py:31
  26.4 0.6 %collective-permute-start.3 = (f32[4,32,128]{2,1,0:T(8,128)S(1)}, f32[4,32,128]{2,1,0:T(8,128)S(1)}, u32[]{:S(2)}, u32[]{:S(2)}) collective-permute-start(f32[4,32,128]{2,1,0:T(8,128)S(1)} %get-tuple-element.20), channel_id=1, source_target_pairs={{0,8},{8,0},{16,24},{24,16},{1,9},{9,1},{17,25},{25,17},{2,10},{10... | collective-permute-start | bytes 196616 | tf_op jit(solution)/shard_map/ppermute | solution.py:31
  27.0 0.3 collective-permute-start.4
  27.2 3.3 %collective-permute-done.5.part_ref = f32[4,32,128]{2,1,0:T(8,128)S(1)} collective-permute-done((f32[4,32,128]{2,1,0:T(8,128)S(1)}, f32[4,32,128]{2,1,0:T(8,128)S(1)}, u32[]{:S(2)}, u32[]{:S(2)}) %collective-permute-start.5) | collective-permute-done | bytes 65568 | tf_op jit(solution)/shard_map/ppermute | solution.py:31
  30.5 1.1 %collective-permute-done.3.refs_1_ = f32[4,32,128]{2,1,0:T(8,128)S(1)} collective-permute-done((f32[4,32,128]{2,1,0:T(8,128)S(1)}, f32[4,32,128]{2,1,0:T(8,128)S(1)}, u32[]{:S(2)}, u32[]{:S(2)}) %collective-permute-start.3) | collective-permute-done | bytes 65568 | tf_op jit(solution)/shard_map/ppermute | solution.py:31
  31.6 0.2 collective-permute-done.4.refs_2_
  31.8 0.5 %all-to-all-done.1 = f32[32,11,1,128]{3,2,1,0:T(1,128)S(1)} async-done(((f32[32,11,1,128]{3,2,1,0:T(1,128)}), f32[32,11,1,128]{3,2,1,0:T(1,128)S(1)}, u32[]{:S(2)}, u32[]{:S(2)}) %all-to-all-start.1) | async-done | bytes 180256 | tf_op jit(solution)/shard_map/all_to_all | solution.py:37
  32.3 0.8 %shard_map.88 = (f32[4,32,512]{2,1,0:T(8,128)}, f32[1,512]{1,0:T(1,128)}, f32[1,512]{1,0:T(1,128)}, f32[9,512]{1,0:T(8,128)}) custom-call(f32[4,32,128]{2,1,0:T(8,128)S(1)} %get-tuple-element.19.refs_0_, f32[4,32,128]{2,1,0:T(8,128)S(1)} %collective-permute-done.3.refs_1_, f32[4,32,128]{2,1,0:T(8,128)S(1)} %collective-permute-done.4.refs_2_, ...), custom_call_target="tpu_custom_call" | custom-call | tf_op jit(solution)/shard_map/pallas_call | solution.py:396
  (2 shorter events, 0.0 us)
Async XLA Ops:
  2.2 11.2 %collective-permute-start.2 = (f32[2,4,32,128]{3,2,1,0:T(8,128)S(1)}, f32[2,4,32,128]{3,2,1,0:T(8,128)S(1)}, u32[]{:S(2)}, u32[]{:S(2)}) collective-permute-start(f32[2,4,32,128]{3,2,1,0:T(8,128)S(1)} %get-tuple-element.17), channel_id=1, source_target_pairs={{0,24},{8,16},{16,8},{24,0},{1,25},{9,17},{17,9},{25,1},{2,26},{10... | collective-permute-start | bytes 393224 | tf_op jit(solution)/shard_map/ppermute | solution.py:31
  6.2 11.8 %all-to-all-start = ((f32[32,6,1,128]{3,2,1,0:T(1,128)}), f32[32,6,1,128]{3,2,1,0:T(1,128)S(1)}, u32[]{:S(2)}, u32[]{:S(2)}) async-start(f32[32,6,1,128]{3,2,1,0:T(1,128)} %bitcast), calls=%async_computation | async-start | bytes 196608 | tf_op jit(solution)/shard_map/all_to_all | solution.py:37
  10.1 6.6 %collective-permute-start = (f32[2,4,32,128]{3,2,1,0:T(8,128)S(1)}, f32[2,4,32,128]{3,2,1,0:T(8,128)S(1)}, u32[]{:S(2)}, u32[]{:S(2)}) collective-permute-start(f32[2,4,32,128]{3,2,1,0:T(8,128)S(1)} %get-tuple-element.15), channel_id=1, source_target_pairs={{0,8},{8,0},{16,24},{24,16},{1,9},{9,1},{17,25},{25,17},{2,10},{10... | collective-permute-start | bytes 393224 | tf_op jit(solution)/shard_map/ppermute | solution.py:31
  12.0 6.0 %copy-start = (f32[9,512]{1,0:T(8,128)S(1)}, f32[9,512]{1,0:T(8,128)}, u32[]{:S(2)}) copy-start(f32[9,512]{1,0:T(8,128)} %refs_5_.1) | copy-start | bytes 55300
  12.0 6.0 %collective-permute-start.1 = (f32[2,4,32,128]{3,2,1,0:T(8,128)S(1)}, f32[2,4,32,128]{3,2,1,0:T(8,128)S(1)}, u32[]{:S(2)}, u32[]{:S(2)}) collective-permute-start(f32[2,4,32,128]{3,2,1,0:T(8,128)S(1)} %get-tuple-element.16), channel_id=1, source_target_pairs={{0,16},{8,24},{16,0},{24,8},{1,17},{9,25},{17,1},{25,9},{2,18},{10... | collective-permute-start | bytes 393224 | tf_op jit(solution)/shard_map/ppermute | solution.py:31
  19.7 12.6 %all-to-all-start.1 = ((f32[32,11,1,128]{3,2,1,0:T(1,128)}), f32[32,11,1,128]{3,2,1,0:T(1,128)S(1)}, u32[]{:S(2)}, u32[]{:S(2)}) async-start(f32[32,11,1,128]{3,2,1,0:T(1,128)} %bitcast.2), calls=%async_computation.1 | async-start | bytes 360448 | tf_op jit(solution)/shard_map/all_to_all | solution.py:37
  23.7 6.8 %collective-permute-start.5 = (f32[4,32,128]{2,1,0:T(8,128)S(1)}, f32[4,32,128]{2,1,0:T(8,128)S(1)}, u32[]{:S(2)}, u32[]{:S(2)}) collective-permute-start(f32[4,32,128]{2,1,0:T(8,128)S(1)} %get-tuple-element.22), channel_id=1, source_target_pairs={{0,24},{8,16},{16,8},{24,0},{1,25},{9,17},{17,9},{25,1},{2,26},{10... | collective-permute-start | bytes 196616 | tf_op jit(solution)/shard_map/ppermute | solution.py:31
  26.4 5.2 %collective-permute-start.3 = (f32[4,32,128]{2,1,0:T(8,128)S(1)}, f32[4,32,128]{2,1,0:T(8,128)S(1)}, u32[]{:S(2)}, u32[]{:S(2)}) collective-permute-start(f32[4,32,128]{2,1,0:T(8,128)S(1)} %get-tuple-element.20), channel_id=1, source_target_pairs={{0,8},{8,0},{16,24},{24,16},{1,9},{9,1},{17,25},{25,17},{2,10},{10... | collective-permute-start | bytes 196616 | tf_op jit(solution)/shard_map/ppermute | solution.py:31
  27.0 4.9 %collective-permute-start.4 = (f32[4,32,128]{2,1,0:T(8,128)S(1)}, f32[4,32,128]{2,1,0:T(8,128)S(1)}, u32[]{:S(2)}, u32[]{:S(2)}) collective-permute-start(f32[4,32,128]{2,1,0:T(8,128)S(1)} %get-tuple-element.21), channel_id=1, source_target_pairs={{0,16},{8,24},{16,0},{24,8},{1,17},{9,25},{17,1},{25,9},{2,18},{10... | collective-permute-start | bytes 196616 | tf_op jit(solution)/shard_map/ppermute | solution.py:31

commit v7 on v6

--- a/solution.py
+++ b/solution.py
@@ -114,6 +114,7 @@
         copy.start()
     for copy in small:
         copy.wait()
+    sends = []
     for to_band in range(bands):
         lanes = slice(to_band * width, (to_band + 1) * width)
         key = key_own[:, lanes]
@@ -128,11 +129,17 @@
             start = start + keys
             block_ref[start : start + keys, :] = value
             block_ref[start + keys : start + keys + rows, :] = jnp.where(is_next, last, first)
-    send = pltpu.make_async_copy(block_ref, sent_ref, sems.at[len(small) + len(large)])
-    send.start()
-    for copy in large:
+        group = pl.ds(to_band * sectors * sent, sectors * sent)
+        sends.append(
+            pltpu.make_async_copy(
+                block_ref.at[group],
+                sent_ref.at[group],
+                sems.at[len(small) + len(large) + to_band],
+            )
+        )
+        sends[-1].start()
+    for copy in large + sends:
         copy.wait()
-    send.wait()
 
 
 def heads_of(matrix, width):
@@ -371,7 +378,7 @@
             pltpu.VMEM((rows, 1, channels), jnp.float32),
             pltpu.VMEM((rows, 1, channels), jnp.float32),
             pltpu.VMEM((devices * sent_rows, width), jnp.float32),
-            pltpu.SemaphoreType.DMA((5 + 2 * bands,)),
+            pltpu.SemaphoreType.DMA((4 + 3 * bands,)),
         ],
         compiler_params=pltpu.CompilerParams(vmem_limit_bytes=VMEM_LIMIT),
     )(*[in_hbm(x) for x in (key_rows, value_rows, queries, cotangent)])

time: 33.5 us -> 33.5 us (level)
  no operation moved by 1% of the time
where the time goes in v7:
time: 33.5 us; the launch traced here: 33 us
  starting transfers between devices  18.7 us (56%)
  waiting for transfers between devices  9.59 us (29%)
  Pallas kernels  4.03 us (12%)
  between operations  0.67 us (2%)
    ppermute x6, starting transfers between devices, exchange(): lax.ppermute(value, 'lat', [(i, partner(i, step, peers)) for i in range(p...  10.8 us
    ppermute x6, waiting for transfers between devices, exchange(): lax.ppermute(value, 'lat', [(i, partner(i, step, peers)) for i in range(p...  9.11 us
    all_to_all x2, starting transfers between devices, to_all(): lax.all_to_all(blocks, ('lat', 'lon'), 0, 0, tiled=True)  7.93 us
    pallas_call x1, Pallas kernels, split_heads_body(): vmem_call(functools.partial(attention_kernel, bands, sectors, width, keys...  1.69 us
    pallas_call x1, Pallas kernels, split_heads_body(): pl.pallas_call(functools.partial(pack_kernel, bands, sectors, width, keys...  1.55 us
    pallas_call x1, Pallas kernels, split_heads_body(): pl.pallas_call(functools.partial(finish_kernel, bands, sectors, width, ke...  0.78 us
  transfers between devices with their start and end apart: 8, of which 6 were waited for; matrix products, arithmetic and copies ran while one was open for 0% of the time, Pallas kernels for 0%

profile of v7, /device:TPU:0, one launch (start us, length us, event | category | flops | bytes accessed | tf_op | source)
XLA Modules:
  0.0 33.0 jit_solution(15463334853062155179)
XLA Ops:
  0.6 1.6 %shard_map.84 = (f32[192,128]{1,0:T(8,128)}, f32[2,4,32,128]{3,2,1,0:T(8,128)S(1)}, f32[2,4,32,128]{3,2,1,0:T(8,128)S(1)}, f32[2,4,32,128]{3,2,1,0:T(8,128)S(1)}, f32[2,4,32,128]{3,2,1,0:T(8,128)S(1)}) custom-call(f32[1,512]{1,0:T(1,128)} %refs_0_.1, f32[1,512]{1,0:T(1,128)} %refs_1_.1, f32[4,32,512]{2,1,0:T(8,128)} %refs_2_.1, f32[4,32,512]{2,1,0:T(8,128)} %refs_3_.1), custom_call_target="tpu_custom_call" | custom-call | tf_op jit(solution)/shard_map/pallas_call | solution.py:367
  2.2 4.0 %collective-permute-start.2 = (f32[2,4,32,128]{3,2,1,0:T(8,128)S(1)}, f32[2,4,32,128]{3,2,1,0:T(8,128)S(1)}, u32[]{:S(2)}, u32[]{:S(2)}) collective-permute-start(f32[2,4,32,128]{3,2,1,0:T(8,128)S(1)} %get-tuple-element.17), channel_id=1, source_target_pairs={{0,24},{8,16},{16,8},{24,0},{1,25},{9,17},{17,9},{25,1},{2,26},{10... | collective-permute-start | bytes 393224 | tf_op jit(solution)/shard_map/ppermute | solution.py:31
  6.1 4.0 %all-to-all-start = ((f32[32,6,1,128]{3,2,1,0:T(1,128)}), f32[32,6,1,128]{3,2,1,0:T(1,128)S(1)}, u32[]{:S(2)}, u32[]{:S(2)}) async-start(f32[32,6,1,128]{3,2,1,0:T(1,128)} %bitcast), calls=%async_computation | async-start | bytes 196608 | tf_op jit(solution)/shard_map/all_to_all | solution.py:37
  10.1 1.8 %collective-permute-start = (f32[2,4,32,128]{3,2,1,0:T(8,128)S(1)}, f32[2,4,32,128]{3,2,1,0:T(8,128)S(1)}, u32[]{:S(2)}, u32[]{:S(2)}) collective-permute-start(f32[2,4,32,128]{3,2,1,0:T(8,128)S(1)} %get-tuple-element.15), channel_id=1, source_target_pairs={{0,8},{8,0},{16,24},{24,16},{1,9},{9,1},{17,25},{25,17},{2,10},{10... | collective-permute-start | bytes 393224 | tf_op jit(solution)/shard_map/ppermute | solution.py:31
  12.0 0.0 copy-start
  12.0 1.5 %collective-permute-start.1 = (f32[2,4,32,128]{3,2,1,0:T(8,128)S(1)}, f32[2,4,32,128]{3,2,1,0:T(8,128)S(1)}, u32[]{:S(2)}, u32[]{:S(2)}) collective-permute-start(f32[2,4,32,128]{3,2,1,0:T(8,128)S(1)} %get-tuple-element.16), channel_id=1, source_target_pairs={{0,16},{8,24},{16,0},{24,8},{1,17},{9,25},{17,1},{25,9},{2,18},{10... | collective-permute-start | bytes 393224 | tf_op jit(solution)/shard_map/ppermute | solution.py:31
  13.4 0.0 collective-permute-done.2.part_ref
  13.4 3.3 %collective-permute-done.refs_1_ = f32[2,4,32,128]{3,2,1,0:T(8,128)S(1)} collective-permute-done((f32[2,4,32,128]{3,2,1,0:T(8,128)S(1)}, f32[2,4,32,128]{3,2,1,0:T(8,128)S(1)}, u32[]{:S(2)}, u32[]{:S(2)}) %collective-permute-start) | collective-permute-done | bytes 131104 | tf_op jit(solution)/shard_map/ppermute | solution.py:31
  16.7 1.2 %collective-permute-done.1.refs_2_ = f32[2,4,32,128]{3,2,1,0:T(8,128)S(1)} collective-permute-done((f32[2,4,32,128]{3,2,1,0:T(8,128)S(1)}, f32[2,4,32,128]{3,2,1,0:T(8,128)S(1)}, u32[]{:S(2)}, u32[]{:S(2)}) %collective-permute-start.1) | collective-permute-done | bytes 131104 | tf_op jit(solution)/shard_map/ppermute | solution.py:31
  18.0 0.0 all-to-all-done
  18.0 0.0 copy-done
  18.0 1.7 %shard_map.86 = (f32[352,128]{1,0:T(8,128)}, f32[4,32,128]{2,1,0:T(8,128)S(1)}, f32[4,32,128]{2,1,0:T(8,128)S(1)}, f32[4,32,128]{2,1,0:T(8,128)S(1)}, f32[4,32,128]{2,1,0:T(8,128)S(1)}) custom-call(f32[2,4,32,128]{3,2,1,0:T(8,128)S(1)} %get-tuple-element.14.refs_0_, f32[2,4,32,128]{3,2,1,0:T(8,128)S(1)} %collective-permute-done.refs_1_, ...), custom_call_target="tpu_custom_call" | custom-call | tf_op jit(solution)/shard_map/pallas_call | solution.py:390
  19.7 4.0 %all-to-all-start.1 = ((f32[32,11,1,128]{3,2,1,0:T(1,128)}), f32[32,11,1,128]{3,2,1,0:T(1,128)S(1)}, u32[]{:S(2)}, u32[]{:S(2)}) async-start(f32[32,11,1,128]{3,2,1,0:T(1,128)} %bitcast.2), calls=%async_computation.1 | async-start | bytes 360448 | tf_op jit(solution)/shard_map/all_to_all | solution.py:37
  23.6 2.7 %collective-permute-start.5 = (f32[4,32,128]{2,1,0:T(8,128)S(1)}, f32[4,32,128]{2,1,0:T(8,128)S(1)}, u32[]{:S(2)}, u32[]{:S(2)}) collective-permute-start(f32[4,32,128]{2,1,0:T(8,128)S(1)} %get-tuple-element.22), channel_id=1, source_target_pairs={{0,24},{8,16},{16,8},{24,0},{1,25},{9,17},{17,9},{25,1},{2,26},{10... | collective-permute-start | bytes 196616 | tf_op jit(solution)/shard_map/ppermute | solution.py:31
  26.4 0.6 %collective-permute-start.3 = (f32[4,32,128]{2,1,0:T(8,128)S(1)}, f32[4,32,128]{2,1,0:T(8,128)S(1)}, u32[]{:S(2)}, u32[]{:S(2)}) collective-permute-start(f32[4,32,128]{2,1,0:T(8,128)S(1)} %get-tuple-element.20), channel_id=1, source_target_pairs={{0,8},{8,0},{16,24},{24,16},{1,9},{9,1},{17,25},{25,17},{2,10},{10... | collective-permute-start | bytes 196616 | tf_op jit(solution)/shard_map/ppermute | solution.py:31
  26.9 0.3 collective-permute-start.4
  27.2 3.3 %collective-permute-done.5.part_ref = f32[4,32,128]{2,1,0:T(8,128)S(1)} collective-permute-done((f32[4,32,128]{2,1,0:T(8,128)S(1)}, f32[4,32,128]{2,1,0:T(8,128)S(1)}, u32[]{:S(2)}, u32[]{:S(2)}) %collective-permute-start.5) | collective-permute-done | bytes 65568 | tf_op jit(solution)/shard_map/ppermute | solution.py:31
  30.5 1.1 %collective-permute-done.3.refs_1_ = f32[4,32,128]{2,1,0:T(8,128)S(1)} collective-permute-done((f32[4,32,128]{2,1,0:T(8,128)S(1)}, f32[4,32,128]{2,1,0:T(8,128)S(1)}, u32[]{:S(2)}, u32[]{:S(2)}) %collective-permute-start.3) | collective-permute-done | bytes 65568 | tf_op jit(solution)/shard_map/ppermute | solution.py:31
  31.6 0.2 collective-permute-done.4.refs_2_
  31.8 0.5 %all-to-all-done.1 = f32[32,11,1,128]{3,2,1,0:T(1,128)S(1)} async-done(((f32[32,11,1,128]{3,2,1,0:T(1,128)}), f32[32,11,1,128]{3,2,1,0:T(1,128)S(1)}, u32[]{:S(2)}, u32[]{:S(2)}) %all-to-all-start.1) | async-done | bytes 180256 | tf_op jit(solution)/shard_map/all_to_all | solution.py:37
  32.3 0.8 %shard_map.88 = (f32[4,32,512]{2,1,0:T(8,128)}, f32[1,512]{1,0:T(1,128)}, f32[1,512]{1,0:T(1,128)}, f32[9,512]{1,0:T(8,128)}) custom-call(f32[4,32,128]{2,1,0:T(8,128)S(1)} %get-tuple-element.19.refs_0_, f32[4,32,128]{2,1,0:T(8,128)S(1)} %collective-permute-done.3.refs_1_, f32[4,32,128]{2,1,0:T(8,128)S(1)} %collective-permute-done.4.refs_2_, ...), custom_call_target="tpu_custom_call" | custom-call | tf_op jit(solution)/shard_map/pallas_call | solution.py:403
  (2 shorter events, 0.0 us)
Async XLA Ops:
  2.2 11.2 %collective-permute-start.2 = (f32[2,4,32,128]{3,2,1,0:T(8,128)S(1)}, f32[2,4,32,128]{3,2,1,0:T(8,128)S(1)}, u32[]{:S(2)}, u32[]{:S(2)}) collective-permute-start(f32[2,4,32,128]{3,2,1,0:T(8,128)S(1)} %get-tuple-element.17), channel_id=1, source_target_pairs={{0,24},{8,16},{16,8},{24,0},{1,25},{9,17},{17,9},{25,1},{2,26},{10... | collective-permute-start | bytes 393224 | tf_op jit(solution)/shard_map/ppermute | solution.py:31
  6.1 11.8 %all-to-all-start = ((f32[32,6,1,128]{3,2,1,0:T(1,128)}), f32[32,6,1,128]{3,2,1,0:T(1,128)S(1)}, u32[]{:S(2)}, u32[]{:S(2)}) async-start(f32[32,6,1,128]{3,2,1,0:T(1,128)} %bitcast), calls=%async_computation | async-start | bytes 196608 | tf_op jit(solution)/shard_map/all_to_all | solution.py:37
  10.1 6.6 %collective-permute-start = (f32[2,4,32,128]{3,2,1,0:T(8,128)S(1)}, f32[2,4,32,128]{3,2,1,0:T(8,128)S(1)}, u32[]{:S(2)}, u32[]{:S(2)}) collective-permute-start(f32[2,4,32,128]{3,2,1,0:T(8,128)S(1)} %get-tuple-element.15), channel_id=1, source_target_pairs={{0,8},{8,0},{16,24},{24,16},{1,9},{9,1},{17,25},{25,17},{2,10},{10... | collective-permute-start | bytes 393224 | tf_op jit(solution)/shard_map/ppermute | solution.py:31
  12.0 6.0 %copy-start = (f32[9,512]{1,0:T(8,128)S(1)}, f32[9,512]{1,0:T(8,128)}, u32[]{:S(2)}) copy-start(f32[9,512]{1,0:T(8,128)} %refs_5_.1) | copy-start | bytes 55300
  12.0 6.0 %collective-permute-start.1 = (f32[2,4,32,128]{3,2,1,0:T(8,128)S(1)}, f32[2,4,32,128]{3,2,1,0:T(8,128)S(1)}, u32[]{:S(2)}, u32[]{:S(2)}) collective-permute-start(f32[2,4,32,128]{3,2,1,0:T(8,128)S(1)} %get-tuple-element.16), channel_id=1, source_target_pairs={{0,16},{8,24},{16,0},{24,8},{1,17},{9,25},{17,1},{25,9},{2,18},{10... | collective-permute-start | bytes 393224 | tf_op jit(solution)/shard_map/ppermute | solution.py:31
  19.7 12.6 %all-to-all-start.1 = ((f32[32,11,1,128]{3,2,1,0:T(1,128)}), f32[32,11,1,128]{3,2,1,0:T(1,128)S(1)}, u32[]{:S(2)}, u32[]{:S(2)}) async-start(f32[32,11,1,128]{3,2,1,0:T(1,128)} %bitcast.2), calls=%async_computation.1 | async-start | bytes 360448 | tf_op jit(solution)/shard_map/all_to_all | solution.py:37
  23.6 6.8 %collective-permute-start.5 = (f32[4,32,128]{2,1,0:T(8,128)S(1)}, f32[4,32,128]{2,1,0:T(8,128)S(1)}, u32[]{:S(2)}, u32[]{:S(2)}) collective-permute-start(f32[4,32,128]{2,1,0:T(8,128)S(1)} %get-tuple-element.22), channel_id=1, source_target_pairs={{0,24},{8,16},{16,8},{24,0},{1,25},{9,17},{17,9},{25,1},{2,26},{10... | collective-permute-start | bytes 196616 | tf_op jit(solution)/shard_map/ppermute | solution.py:31
  26.4 5.2 %collective-permute-start.3 = (f32[4,32,128]{2,1,0:T(8,128)S(1)}, f32[4,32,128]{2,1,0:T(8,128)S(1)}, u32[]{:S(2)}, u32[]{:S(2)}) collective-permute-start(f32[4,32,128]{2,1,0:T(8,128)S(1)} %get-tuple-element.20), channel_id=1, source_target_pairs={{0,8},{8,0},{16,24},{24,16},{1,9},{9,1},{17,25},{25,17},{2,10},{10... | collective-permute-start | bytes 196616 | tf_op jit(solution)/shard_map/ppermute | solution.py:31
  26.9 4.9 %collective-permute-start.4 = (f32[4,32,128]{2,1,0:T(8,128)S(1)}, f32[4,32,128]{2,1,0:T(8,128)S(1)}, u32[]{:S(2)}, u32[]{:S(2)}) collective-permute-start(f32[4,32,128]{2,1,0:T(8,128)S(1)} %get-tuple-element.21), channel_id=1, source_target_pairs={{0,16},{8,24},{16,0},{24,8},{1,17},{9,25},{17,1},{25,9},{2,18},{10... | collective-permute-start | bytes 196616 | tf_op jit(solution)/shard_map/ppermute | solution.py:31

commit v8 on v7

--- a/solution.py
+++ b/solution.py
@@ -234,8 +234,8 @@
 def attention_kernel(bands, sectors, width, keys, *refs):
     part_refs = refs[:bands]
     rows_ref, taps_ref, terms_ref = refs[bands : bands + 3]
-    query_grad_refs = refs[bands + 3 : 2 * bands + 3]
-    query_ref, weighted_ref, grad_ref, out_ref = refs[2 * bands + 3 :]
+    logit_grad_ref = refs[bands + 3]
+    query_ref, weighted_ref, grad_ref, out_ref = refs[bands + 4 :]
     band = lax.axis_index("lat")
     sector = lax.axis_index("lon")
     rows, columns = part_refs[0].shape[1:3]
@@ -321,8 +321,18 @@
     for device in range(devices):
         terms_ref[device * used + 2 * keys : (device + 1) * used, :] = tap_sum
 
-    out_ref[...] = (mix_rows_exactly(logit_grad, key_heads) * scale).reshape(out_ref.shape)
-    for step, part_ref in enumerate(query_grad_refs):
+    logit_grad_ref[...] = logit_grad
+
+
+def query_grad_kernel(bands, sectors, width, keys, rows, columns, logit_grad_ref, rows_ref, *refs):
+    part_refs, out_ref = refs[:-1], refs[-1]
+    band = lax.axis_index("lat")
+    devices = bands * sectors
+    sent = block_rows(bands, keys, rows)
+    key_heads = heads_of(rows_from_all(rows_ref, 0, keys, devices, sent), width)
+    query_grad = mix_rows_exactly(logit_grad_ref[...], key_heads) * HD ** (-0.5)
+    out_ref[...] = query_grad.reshape(out_ref.shape)
+    for step, part_ref in enumerate(part_refs):
         part_ref[...] = out_ref[pl.ds(partner(band, step, bands) * rows, rows)]
 
 
@@ -387,18 +397,18 @@
 
     grid = (lines, columns, width)
     heads = width // HD
-    terms, *grad_parts = vmem_call(
+    heads = width // HD
+    terms, logit_grad = vmem_call(
         functools.partial(attention_kernel, bands, sectors, width, keys),
-        [(devices * term_rows(keys), width)] + [(rows, columns, width)] * bands,
-        [
-            grid,
-            (lines + 2, columns + 2 * SUBLANES, width),
-            grid,
-            grid,
-        ],
+        [(devices * term_rows(keys), width), (heads * devices * keys, lines * columns)],
+        [grid, (lines + 2, columns + 2 * SUBLANES, width), grid, grid],
     )(*parts, row_blocks, conv_taps)
-
     terms = to_all(terms, devices)
+    grad_parts = vmem_call(
+        functools.partial(query_grad_kernel, bands, sectors, width, keys, rows, columns),
+        [(rows, columns, width)] * bands,
+        [grid],
+    )(logit_grad, row_blocks)
     grad_parts = exchange_all(grad_parts, bands, ahead=False)
     query_grad, key_grad, value_grad, tap_update = pl.pallas_call(
         functools.partial(finish_kernel, bands, sectors, width, keys),

time: 33.5 us -> 33.5 us (level)
  transfers between devices with their start and end apart: 8 -> 8, of which waited for: 6 -> 6; matrix products, arithmetic and copies ran while one was open for 0% -> 0% of each run, Pallas kernels for 0% -> 1%
where the time goes in v8:
time: 33.5 us; the launch traced here: 33 us
  starting transfers between devices  18.7 us (56%)
  waiting for transfers between devices  9.27 us (28%)
  Pallas kernels  4.3 us (13%)
  between operations  0.68 us (2%)
    ppermute x6, starting transfers between devices, exchange(): lax.ppermute(value, 'lat', [(i, partner(i, step, peers)) for i in range(p...  10.8 us
    ppermute x6, waiting for transfers between devices, exchange(): lax.ppermute(value, 'lat', [(i, partner(i, step, peers)) for i in range(p...  8.99 us
    all_to_all x2, starting transfers between devices, to_all(): lax.all_to_all(blocks, ('lat', 'lon'), 0, 0, tiled=True)  7.92 us
    pallas_call x1, Pallas kernels, split_heads_body(): vmem_call(functools.partial(attention_kernel, bands, sectors, width, keys...  1.64 us
    pallas_call x1, Pallas kernels, split_heads_body(): pl.pallas_call(functools.partial(pack_kernel, bands, sectors, width, keys...  1.55 us
    pallas_call x1, Pallas kernels, split_heads_body(): pl.pallas_call(functools.partial(finish_kernel, bands, sectors, width, ke...  0.78 us
  transfers between devices with their start and end apart: 8, of which 6 were waited for; matrix products, arithmetic and copies ran while one was open for 0% of the time, Pallas kernels for 1%

profile of v8, /device:TPU:0, one launch (start us, length us, event | category | flops | bytes accessed | tf_op | source)
XLA Modules:
  0.0 33.0 jit_solution(4998041485924681981)
XLA Ops:
  0.6 1.6 %shard_map.84 = (f32[192,128]{1,0:T(8,128)}, f32[2,4,32,128]{3,2,1,0:T(8,128)S(1)}, f32[2,4,32,128]{3,2,1,0:T(8,128)S(1)}, f32[2,4,32,128]{3,2,1,0:T(8,128)S(1)}, f32[2,4,32,128]{3,2,1,0:T(8,128)S(1)}) custom-call(f32[1,512]{1,0:T(1,128)} %refs_0_.1, f32[1,512]{1,0:T(1,128)} %refs_1_.1, f32[4,32,512]{2,1,0:T(8,128)} %refs_2_.1, f32[4,32,512]{2,1,0:T(8,128)} %refs_3_.1), custom_call_target="tpu_custom_call" | custom-call | tf_op jit(solution)/shard_map/pallas_call | solution.py:377
  2.2 4.0 %collective-permute-start.2 = (f32[2,4,32,128]{3,2,1,0:T(8,128)S(1)}, f32[2,4,32,128]{3,2,1,0:T(8,128)S(1)}, u32[]{:S(2)}, u32[]{:S(2)}) collective-permute-start(f32[2,4,32,128]{3,2,1,0:T(8,128)S(1)} %get-tuple-element.18), channel_id=1, source_target_pairs={{0,24},{8,16},{16,8},{24,0},{1,25},{9,17},{17,9},{25,1},{2,26},{10... | collective-permute-start | bytes 393224 | tf_op jit(solution)/shard_map/ppermute | solution.py:31
  6.1 4.0 %all-to-all-start = ((f32[32,6,1,128]{3,2,1,0:T(1,128)}), f32[32,6,1,128]{3,2,1,0:T(1,128)S(1)}, u32[]{:S(2)}, u32[]{:S(2)}) async-start(f32[32,6,1,128]{3,2,1,0:T(1,128)} %bitcast), calls=%async_computation | async-start | bytes 196608 | tf_op jit(solution)/shard_map/all_to_all | solution.py:37
  10.1 1.8 %collective-permute-start = (f32[2,4,32,128]{3,2,1,0:T(8,128)S(1)}, f32[2,4,32,128]{3,2,1,0:T(8,128)S(1)}, u32[]{:S(2)}, u32[]{:S(2)}) collective-permute-start(f32[2,4,32,128]{3,2,1,0:T(8,128)S(1)} %get-tuple-element.16), channel_id=1, source_target_pairs={{0,8},{8,0},{16,24},{24,16},{1,9},{9,1},{17,25},{25,17},{2,10},{10... | collective-permute-start | bytes 393224 | tf_op jit(solution)/shard_map/ppermute | solution.py:31
  12.0 0.0 copy-start
  12.0 1.5 %collective-permute-start.1 = (f32[2,4,32,128]{3,2,1,0:T(8,128)S(1)}, f32[2,4,32,128]{3,2,1,0:T(8,128)S(1)}, u32[]{:S(2)}, u32[]{:S(2)}) collective-permute-start(f32[2,4,32,128]{3,2,1,0:T(8,128)S(1)} %get-tuple-element.17), channel_id=1, source_target_pairs={{0,16},{8,24},{16,0},{24,8},{1,17},{9,25},{17,1},{25,9},{2,18},{10... | collective-permute-start | bytes 393224 | tf_op jit(solution)/shard_map/ppermute | solution.py:31
  13.4 0.0 collective-permute-done.2.part_ref
  13.4 3.3 %collective-permute-done.refs_1_ = f32[2,4,32,128]{3,2,1,0:T(8,128)S(1)} collective-permute-done((f32[2,4,32,128]{3,2,1,0:T(8,128)S(1)}, f32[2,4,32,128]{3,2,1,0:T(8,128)S(1)}, u32[]{:S(2)}, u32[]{:S(2)}) %collective-permute-start) | collective-permute-done | bytes 131104 | tf_op jit(solution)/shard_map/ppermute | solution.py:31
  16.7 1.2 %collective-permute-done.1.refs_2_ = f32[2,4,32,128]{3,2,1,0:T(8,128)S(1)} collective-permute-done((f32[2,4,32,128]{3,2,1,0:T(8,128)S(1)}, f32[2,4,32,128]{3,2,1,0:T(8,128)S(1)}, u32[]{:S(2)}, u32[]{:S(2)}) %collective-permute-start.1) | collective-permute-done | bytes 131104 | tf_op jit(solution)/shard_map/ppermute | solution.py:31
  18.0 0.0 all-to-all-done
  18.0 0.0 copy-done
  18.0 1.6 %shard_map.86 = (f32[352,128]{1,0:T(8,128)}, f32[64,512]{1,0:T(8,128)S(1)}) custom-call(f32[2,4,32,128]{3,2,1,0:T(8,128)S(1)} %get-tuple-element.15.refs_0_, f32[2,4,32,128]{3,2,1,0:T(8,128)S(1)} %collective-permute-done.refs_1_, f32[2,4,32,128]{3,2,1,0:T(8,128)S(1)} %collective-permute-done.1.refs_2_, f32[2,4,32,128]{3,2,1,0:T(8,128)S(1)} %shard_map.85.refs_3_, ...), custom_call_target="tpu_custom_call" | custom-call | tf_op jit(solution)/shard_map/pallas_call | solution.py:401
  19.6 4.0 %all-to-all-start.1 = ((f32[32,11,1,128]{3,2,1,0:T(1,128)}), f32[32,11,1,128]{3,2,1,0:T(1,128)S(1)}, u32[]{:S(2)}, u32[]{:S(2)}) async-start(f32[32,11,1,128]{3,2,1,0:T(1,128)} %bitcast.2), calls=%async_computation.1 | async-start | bytes 360448 | tf_op jit(solution)/shard_map/all_to_all | solution.py:37
  23.6 0.3 shard_map.87
  23.9 2.7 %collective-permute-start.5 = (f32[4,32,128]{2,1,0:T(8,128)S(1)}, f32[4,32,128]{2,1,0:T(8,128)S(1)}, u32[]{:S(2)}, u32[]{:S(2)}) collective-permute-start(f32[4,32,128]{2,1,0:T(8,128)S(1)} %get-tuple-element.24), channel_id=1, source_target_pairs={{0,24},{8,16},{16,8},{24,0},{1,25},{9,17},{17,9},{25,1},{2,26},{10... | collective-permute-start | bytes 196616 | tf_op jit(solution)/shard_map/ppermute | solution.py:31
  26.7 0.6 %collective-permute-start.3 = (f32[4,32,128]{2,1,0:T(8,128)S(1)}, f32[4,32,128]{2,1,0:T(8,128)S(1)}, u32[]{:S(2)}, u32[]{:S(2)}) collective-permute-start(f32[4,32,128]{2,1,0:T(8,128)S(1)} %get-tuple-element.22), channel_id=1, source_target_pairs={{0,8},{8,0},{16,24},{24,16},{1,9},{9,1},{17,25},{25,17},{2,10},{10... | collective-permute-start | bytes 196616 | tf_op jit(solution)/shard_map/ppermute | solution.py:31
  27.2 0.3 collective-permute-start.4
  27.5 3.1 %collective-permute-done.5.part_ref = f32[4,32,128]{2,1,0:T(8,128)S(1)} collective-permute-done((f32[4,32,128]{2,1,0:T(8,128)S(1)}, f32[4,32,128]{2,1,0:T(8,128)S(1)}, u32[]{:S(2)}, u32[]{:S(2)}) %collective-permute-start.5) | collective-permute-done | bytes 65568 | tf_op jit(solution)/shard_map/ppermute | solution.py:31
  30.6 1.2 %collective-permute-done.3.refs_1_ = f32[4,32,128]{2,1,0:T(8,128)S(1)} collective-permute-done((f32[4,32,128]{2,1,0:T(8,128)S(1)}, f32[4,32,128]{2,1,0:T(8,128)S(1)}, u32[]{:S(2)}, u32[]{:S(2)}) %collective-permute-start.3) | collective-permute-done | bytes 65568 | tf_op jit(solution)/shard_map/ppermute | solution.py:31
  31.7 0.2 collective-permute-done.4.refs_2_
  31.9 0.3 all-to-all-done.1
  32.2 0.8 %shard_map.89 = (f32[4,32,512]{2,1,0:T(8,128)}, f32[1,512]{1,0:T(1,128)}, f32[1,512]{1,0:T(1,128)}, f32[9,512]{1,0:T(8,128)}) custom-call(f32[4,32,128]{2,1,0:T(8,128)S(1)} %get-tuple-element.21.refs_0_, f32[4,32,128]{2,1,0:T(8,128)S(1)} %collective-permute-done.3.refs_1_, f32[4,32,128]{2,1,0:T(8,128)S(1)} %collective-permute-done.4.refs_2_, ...), custom_call_target="tpu_custom_call" | custom-call | tf_op jit(solution)/shard_map/pallas_call | solution.py:413
  (2 shorter events, 0.0 us)
Async XLA Ops:
  2.2 11.2 %collective-permute-start.2 = (f32[2,4,32,128]{3,2,1,0:T(8,128)S(1)}, f32[2,4,32,128]{3,2,1,0:T(8,128)S(1)}, u32[]{:S(2)}, u32[]{:S(2)}) collective-permute-start(f32[2,4,32,128]{3,2,1,0:T(8,128)S(1)} %get-tuple-element.18), channel_id=1, source_target_pairs={{0,24},{8,16},{16,8},{24,0},{1,25},{9,17},{17,9},{25,1},{2,26},{10... | collective-permute-start | bytes 393224 | tf_op jit(solution)/shard_map/ppermute | solution.py:31
  6.1 11.8 %all-to-all-start = ((f32[32,6,1,128]{3,2,1,0:T(1,128)}), f32[32,6,1,128]{3,2,1,0:T(1,128)S(1)}, u32[]{:S(2)}, u32[]{:S(2)}) async-start(f32[32,6,1,128]{3,2,1,0:T(1,128)} %bitcast), calls=%async_computation | async-start | bytes 196608 | tf_op jit(solution)/shard_map/all_to_all | solution.py:37
  10.1 6.6 %collective-permute-start = (f32[2,4,32,128]{3,2,1,0:T(8,128)S(1)}, f32[2,4,32,128]{3,2,1,0:T(8,128)S(1)}, u32[]{:S(2)}, u32[]{:S(2)}) collective-permute-start(f32[2,4,32,128]{3,2,1,0:T(8,128)S(1)} %get-tuple-element.16), channel_id=1, source_target_pairs={{0,8},{8,0},{16,24},{24,16},{1,9},{9,1},{17,25},{25,17},{2,10},{10... | collective-permute-start | bytes 393224 | tf_op jit(solution)/shard_map/ppermute | solution.py:31
  12.0 6.0 %copy-start = (f32[9,512]{1,0:T(8,128)S(1)}, f32[9,512]{1,0:T(8,128)}, u32[]{:S(2)}) copy-start(f32[9,512]{1,0:T(8,128)} %refs_5_.1) | copy-start | bytes 55300
  12.0 6.0 %collective-permute-start.1 = (f32[2,4,32,128]{3,2,1,0:T(8,128)S(1)}, f32[2,4,32,128]{3,2,1,0:T(8,128)S(1)}, u32[]{:S(2)}, u32[]{:S(2)}) collective-permute-start(f32[2,4,32,128]{3,2,1,0:T(8,128)S(1)} %get-tuple-element.17), channel_id=1, source_target_pairs={{0,16},{8,24},{16,0},{24,8},{1,17},{9,25},{17,1},{25,9},{2,18},{10... | collective-permute-start | bytes 393224 | tf_op jit(solution)/shard_map/ppermute | solution.py:31
  19.6 12.6 %all-to-all-start.1 = ((f32[32,11,1,128]{3,2,1,0:T(1,128)}), f32[32,11,1,128]{3,2,1,0:T(1,128)S(1)}, u32[]{:S(2)}, u32[]{:S(2)}) async-start(f32[32,11,1,128]{3,2,1,0:T(1,128)} %bitcast.2), calls=%async_computation.1 | async-start | bytes 360448 | tf_op jit(solution)/shard_map/all_to_all | solution.py:37
  23.9 6.6 %collective-permute-start.5 = (f32[4,32,128]{2,1,0:T(8,128)S(1)}, f32[4,32,128]{2,1,0:T(8,128)S(1)}, u32[]{:S(2)}, u32[]{:S(2)}) collective-permute-start(f32[4,32,128]{2,1,0:T(8,128)S(1)} %get-tuple-element.24), channel_id=1, source_target_pairs={{0,24},{8,16},{16,8},{24,0},{1,25},{9,17},{17,9},{25,1},{2,26},{10... | collective-permute-start | bytes 196616 | tf_op jit(solution)/shard_map/ppermute | solution.py:31
  26.7 5.1 %collective-permute-start.3 = (f32[4,32,128]{2,1,0:T(8,128)S(1)}, f32[4,32,128]{2,1,0:T(8,128)S(1)}, u32[]{:S(2)}, u32[]{:S(2)}) collective-permute-start(f32[4,32,128]{2,1,0:T(8,128)S(1)} %get-tuple-element.22), channel_id=1, source_target_pairs={{0,8},{8,0},{16,24},{24,16},{1,9},{9,1},{17,25},{25,17},{2,10},{10... | collective-permute-start | bytes 196616 | tf_op jit(solution)/shard_map/ppermute | solution.py:31
  27.2 4.7 %collective-permute-start.4 = (f32[4,32,128]{2,1,0:T(8,128)S(1)}, f32[4,32,128]{2,1,0:T(8,128)S(1)}, u32[]{:S(2)}, u32[]{:S(2)}) collective-permute-start(f32[4,32,128]{2,1,0:T(8,128)S(1)} %get-tuple-element.23), channel_id=1, source_target_pairs={{0,16},{8,24},{16,0},{24,8},{1,17},{9,25},{17,1},{25,9},{2,18},{10... | collective-permute-start | bytes 196616 | tf_op jit(solution)/shard_map/ppermute | solution.py:31

commit v9 on v7

--- a/solution.py
+++ b/solution.py
@@ -291,7 +291,7 @@
     for h in range(heads):
         part = logits[h * key_total : (h + 1) * key_total]
         raised = jnp.exp(part - jnp.max(part, 0, keepdims=True))
-        prob_list.append(raised / jnp.sum(raised, 0, keepdims=True))
+        prob_list.append(raised * (1.0 / jnp.sum(raised, 0, keepdims=True)))
     probs = jnp.concatenate(prob_list, 0)
     out_ref[...] = mix_rows(probs, value_heads).reshape(lines, columns, width)
     prob_grad = rows_by_tokens(value_heads, grad)
@@ -339,10 +339,13 @@
     parts = []
     for to_band in range(bands):
         lanes = slice(to_band * width, (to_band + 1) * width)
-        part = jnp.zeros((used, width), jnp.float32)
-        for sector in range(sectors):
-            start = (to_band * sectors + sector) * used
-            part = part + terms_ref[start : start + used, :]
+        rows_of = [
+            terms_ref[(to_band * sectors + sector) * used : (to_band * sectors + sector + 1) * used, :]
+            for sector in range(sectors)
+        ]
+        while len(rows_of) > 1:
+            rows_of = [sum(rows_of[i : i + 2]) for i in range(0, len(rows_of), 2)]
+        part = rows_of[0]
         key_ref[:, lanes] = part[0:keys]
         value_ref[:, lanes] = part[keys : 2 * keys]
         parts.append(part[2 * keys : used])

time: 33.5 us -> 33.5 us (level)
  no operation moved by 1% of the time
where the time goes in v9:
time: 33.5 us; the launch traced here: 33 us
  starting transfers between devices  18.7 us (56%)
  waiting for transfers between devices  9.59 us (29%)
  Pallas kernels  4.03 us (12%)
  between operations  0.67 us (2%)
    ppermute x6, starting transfers between devices, exchange(): lax.ppermute(value, 'lat', [(i, partner(i, step, peers)) for i in range(p...  10.8 us
    ppermute x6, waiting for transfers between devices, exchange(): lax.ppermute(value, 'lat', [(i, partner(i, step, peers)) for i in range(p...  9.11 us
    all_to_all x2, starting transfers between devices, to_all(): lax.all_to_all(blocks, ('lat', 'lon'), 0, 0, tiled=True)  7.93 us
    pallas_call x1, Pallas kernels, split_heads_body(): vmem_call(functools.partial(attention_kernel, bands, sectors, width, keys...  1.69 us
    pallas_call x1, Pallas kernels, split_heads_body(): pl.pallas_call(functools.partial(pack_kernel, bands, sectors, width, keys...  1.55 us
    pallas_call x1, Pallas kernels, split_heads_body(): pl.pallas_call(functools.partial(finish_kernel, bands, sectors, width, ke...  0.77 us
  transfers between devices with their start and end apart: 8, of which 6 were waited for; matrix products, arithmetic and copies ran while one was open for 0% of the time, Pallas kernels for 0%

profile of v9, /device:TPU:0, one launch (start us, length us, event | category | flops | bytes accessed | tf_op | source)
XLA Modules:
  0.0 33.0 jit_solution(362906824817835391)
XLA Ops:
  0.6 1.6 %shard_map.84 = (f32[192,128]{1,0:T(8,128)}, f32[2,4,32,128]{3,2,1,0:T(8,128)S(1)}, f32[2,4,32,128]{3,2,1,0:T(8,128)S(1)}, f32[2,4,32,128]{3,2,1,0:T(8,128)S(1)}, f32[2,4,32,128]{3,2,1,0:T(8,128)S(1)}) custom-call(f32[1,512]{1,0:T(1,128)} %refs_0_.1, f32[1,512]{1,0:T(1,128)} %refs_1_.1, f32[4,32,512]{2,1,0:T(8,128)} %refs_2_.1, f32[4,32,512]{2,1,0:T(8,128)} %refs_3_.1), custom_call_target="tpu_custom_call" | custom-call | tf_op jit(solution)/shard_map/pallas_call | solution.py:370
  2.2 4.0 %collective-permute-start.2 = (f32[2,4,32,128]{3,2,1,0:T(8,128)S(1)}, f32[2,4,32,128]{3,2,1,0:T(8,128)S(1)}, u32[]{:S(2)}, u32[]{:S(2)}) collective-permute-start(f32[2,4,32,128]{3,2,1,0:T(8,128)S(1)} %get-tuple-element.17), channel_id=1, source_target_pairs={{0,24},{8,16},{16,8},{24,0},{1,25},{9,17},{17,9},{25,1},{2,26},{10... | collective-permute-start | bytes 393224 | tf_op jit(solution)/shard_map/ppermute | solution.py:31
  6.1 4.0 %all-to-all-start = ((f32[32,6,1,128]{3,2,1,0:T(1,128)}), f32[32,6,1,128]{3,2,1,0:T(1,128)S(1)}, u32[]{:S(2)}, u32[]{:S(2)}) async-start(f32[32,6,1,128]{3,2,1,0:T(1,128)} %bitcast), calls=%async_computation | async-start | bytes 196608 | tf_op jit(solution)/shard_map/all_to_all | solution.py:37
  10.1 1.8 %collective-permute-start = (f32[2,4,32,128]{3,2,1,0:T(8,128)S(1)}, f32[2,4,32,128]{3,2,1,0:T(8,128)S(1)}, u32[]{:S(2)}, u32[]{:S(2)}) collective-permute-start(f32[2,4,32,128]{3,2,1,0:T(8,128)S(1)} %get-tuple-element.15), channel_id=1, source_target_pairs={{0,8},{8,0},{16,24},{24,16},{1,9},{9,1},{17,25},{25,17},{2,10},{10... | collective-permute-start | bytes 393224 | tf_op jit(solution)/shard_map/ppermute | solution.py:31
  12.0 0.0 copy-start
  12.0 1.5 %collective-permute-start.1 = (f32[2,4,32,128]{3,2,1,0:T(8,128)S(1)}, f32[2,4,32,128]{3,2,1,0:T(8,128)S(1)}, u32[]{:S(2)}, u32[]{:S(2)}) collective-permute-start(f32[2,4,32,128]{3,2,1,0:T(8,128)S(1)} %get-tuple-element.16), channel_id=1, source_target_pairs={{0,16},{8,24},{16,0},{24,8},{1,17},{9,25},{17,1},{25,9},{2,18},{10... | collective-permute-start | bytes 393224 | tf_op jit(solution)/shard_map/ppermute | solution.py:31
  13.4 0.0 collective-permute-done.2.part_ref
  13.4 3.3 %collective-permute-done.refs_1_ = f32[2,4,32,128]{3,2,1,0:T(8,128)S(1)} collective-permute-done((f32[2,4,32,128]{3,2,1,0:T(8,128)S(1)}, f32[2,4,32,128]{3,2,1,0:T(8,128)S(1)}, u32[]{:S(2)}, u32[]{:S(2)}) %collective-permute-start) | collective-permute-done | bytes 131104 | tf_op jit(solution)/shard_map/ppermute | solution.py:31
  16.7 1.2 %collective-permute-done.1.refs_2_ = f32[2,4,32,128]{3,2,1,0:T(8,128)S(1)} collective-permute-done((f32[2,4,32,128]{3,2,1,0:T(8,128)S(1)}, f32[2,4,32,128]{3,2,1,0:T(8,128)S(1)}, u32[]{:S(2)}, u32[]{:S(2)}) %collective-permute-start.1) | collective-permute-done | bytes 131104 | tf_op jit(solution)/shard_map/ppermute | solution.py:31
  18.0 0.0 all-to-all-done
  18.0 0.0 copy-done
  18.0 1.7 %shard_map.86 = (f32[352,128]{1,0:T(8,128)}, f32[4,32,128]{2,1,0:T(8,128)S(1)}, f32[4,32,128]{2,1,0:T(8,128)S(1)}, f32[4,32,128]{2,1,0:T(8,128)S(1)}, f32[4,32,128]{2,1,0:T(8,128)S(1)}) custom-call(f32[2,4,32,128]{3,2,1,0:T(8,128)S(1)} %get-tuple-element.14.refs_0_, f32[2,4,32,128]{3,2,1,0:T(8,128)S(1)} %collective-permute-done.refs_1_, ...), custom_call_target="tpu_custom_call" | custom-call | tf_op jit(solution)/shard_map/pallas_call | solution.py:393
  19.7 4.0 %all-to-all-start.1 = ((f32[32,11,1,128]{3,2,1,0:T(1,128)}), f32[32,11,1,128]{3,2,1,0:T(1,128)S(1)}, u32[]{:S(2)}, u32[]{:S(2)}) async-start(f32[32,11,1,128]{3,2,1,0:T(1,128)} %bitcast.2), calls=%async_computation.1 | async-start | bytes 360448 | tf_op jit(solution)/shard_map/all_to_all | solution.py:37
  23.6 2.7 %collective-permute-start.5 = (f32[4,32,128]{2,1,0:T(8,128)S(1)}, f32[4,32,128]{2,1,0:T(8,128)S(1)}, u32[]{:S(2)}, u32[]{:S(2)}) collective-permute-start(f32[4,32,128]{2,1,0:T(8,128)S(1)} %get-tuple-element.22), channel_id=1, source_target_pairs={{0,24},{8,16},{16,8},{24,0},{1,25},{9,17},{17,9},{25,1},{2,26},{10... | collective-permute-start | bytes 196616 | tf_op jit(solution)/shard_map/ppermute | solution.py:31
  26.4 0.6 %collective-permute-start.3 = (f32[4,32,128]{2,1,0:T(8,128)S(1)}, f32[4,32,128]{2,1,0:T(8,128)S(1)}, u32[]{:S(2)}, u32[]{:S(2)}) collective-permute-start(f32[4,32,128]{2,1,0:T(8,128)S(1)} %get-tuple-element.20), channel_id=1, source_target_pairs={{0,8},{8,0},{16,24},{24,16},{1,9},{9,1},{17,25},{25,17},{2,10},{10... | collective-permute-start | bytes 196616 | tf_op jit(solution)/shard_map/ppermute | solution.py:31
  26.9 0.3 collective-permute-start.4
  27.2 3.3 %collective-permute-done.5.part_ref = f32[4,32,128]{2,1,0:T(8,128)S(1)} collective-permute-done((f32[4,32,128]{2,1,0:T(8,128)S(1)}, f32[4,32,128]{2,1,0:T(8,128)S(1)}, u32[]{:S(2)}, u32[]{:S(2)}) %collective-permute-start.5) | collective-permute-done | bytes 65568 | tf_op jit(solution)/shard_map/ppermute | solution.py:31
  30.5 1.1 %collective-permute-done.3.refs_1_ = f32[4,32,128]{2,1,0:T(8,128)S(1)} collective-permute-done((f32[4,32,128]{2,1,0:T(8,128)S(1)}, f32[4,32,128]{2,1,0:T(8,128)S(1)}, u32[]{:S(2)}, u32[]{:S(2)}) %collective-permute-start.3) | collective-permute-done | bytes 65568 | tf_op jit(solution)/shard_map/ppermute | solution.py:31
  31.6 0.2 collective-permute-done.4.refs_2_
  31.8 0.5 %all-to-all-done.1 = f32[32,11,1,128]{3,2,1,0:T(1,128)S(1)} async-done(((f32[32,11,1,128]{3,2,1,0:T(1,128)}), f32[32,11,1,128]{3,2,1,0:T(1,128)S(1)}, u32[]{:S(2)}, u32[]{:S(2)}) %all-to-all-start.1) | async-done | bytes 180256 | tf_op jit(solution)/shard_map/all_to_all | solution.py:37
  32.3 0.8 %shard_map.88 = (f32[4,32,512]{2,1,0:T(8,128)}, f32[1,512]{1,0:T(1,128)}, f32[1,512]{1,0:T(1,128)}, f32[9,512]{1,0:T(8,128)}) custom-call(f32[4,32,128]{2,1,0:T(8,128)S(1)} %get-tuple-element.19.refs_0_, f32[4,32,128]{2,1,0:T(8,128)S(1)} %collective-permute-done.3.refs_1_, f32[4,32,128]{2,1,0:T(8,128)S(1)} %collective-permute-done.4.refs_2_, ...), custom_call_target="tpu_custom_call" | custom-call | tf_op jit(solution)/shard_map/pallas_call | solution.py:406
  (2 shorter events, 0.0 us)
Async XLA Ops:
  2.2 11.2 %collective-permute-start.2 = (f32[2,4,32,128]{3,2,1,0:T(8,128)S(1)}, f32[2,4,32,128]{3,2,1,0:T(8,128)S(1)}, u32[]{:S(2)}, u32[]{:S(2)}) collective-permute-start(f32[2,4,32,128]{3,2,1,0:T(8,128)S(1)} %get-tuple-element.17), channel_id=1, source_target_pairs={{0,24},{8,16},{16,8},{24,0},{1,25},{9,17},{17,9},{25,1},{2,26},{10... | collective-permute-start | bytes 393224 | tf_op jit(solution)/shard_map/ppermute | solution.py:31
  6.1 11.8 %all-to-all-start = ((f32[32,6,1,128]{3,2,1,0:T(1,128)}), f32[32,6,1,128]{3,2,1,0:T(1,128)S(1)}, u32[]{:S(2)}, u32[]{:S(2)}) async-start(f32[32,6,1,128]{3,2,1,0:T(1,128)} %bitcast), calls=%async_computation | async-start | bytes 196608 | tf_op jit(solution)/shard_map/all_to_all | solution.py:37
  10.1 6.6 %collective-permute-start = (f32[2,4,32,128]{3,2,1,0:T(8,128)S(1)}, f32[2,4,32,128]{3,2,1,0:T(8,128)S(1)}, u32[]{:S(2)}, u32[]{:S(2)}) collective-permute-start(f32[2,4,32,128]{3,2,1,0:T(8,128)S(1)} %get-tuple-element.15), channel_id=1, source_target_pairs={{0,8},{8,0},{16,24},{24,16},{1,9},{9,1},{17,25},{25,17},{2,10},{10... | collective-permute-start | bytes 393224 | tf_op jit(solution)/shard_map/ppermute | solution.py:31
  12.0 6.0 %copy-start = (f32[9,512]{1,0:T(8,128)S(1)}, f32[9,512]{1,0:T(8,128)}, u32[]{:S(2)}) copy-start(f32[9,512]{1,0:T(8,128)} %refs_5_.1) | copy-start | bytes 55300
  12.0 6.0 %collective-permute-start.1 = (f32[2,4,32,128]{3,2,1,0:T(8,128)S(1)}, f32[2,4,32,128]{3,2,1,0:T(8,128)S(1)}, u32[]{:S(2)}, u32[]{:S(2)}) collective-permute-start(f32[2,4,32,128]{3,2,1,0:T(8,128)S(1)} %get-tuple-element.16), channel_id=1, source_target_pairs={{0,16},{8,24},{16,0},{24,8},{1,17},{9,25},{17,1},{25,9},{2,18},{10... | collective-permute-start | bytes 393224 | tf_op jit(solution)/shard_map/ppermute | solution.py:31
  19.7 12.6 %all-to-all-start.1 = ((f32[32,11,1,128]{3,2,1,0:T(1,128)}), f32[32,11,1,128]{3,2,1,0:T(1,128)S(1)}, u32[]{:S(2)}, u32[]{:S(2)}) async-start(f32[32,11,1,128]{3,2,1,0:T(1,128)} %bitcast.2), calls=%async_computation.1 | async-start | bytes 360448 | tf_op jit(solution)/shard_map/all_to_all | solution.py:37
  23.6 6.8 %collective-permute-start.5 = (f32[4,32,128]{2,1,0:T(8,128)S(1)}, f32[4,32,128]{2,1,0:T(8,128)S(1)}, u32[]{:S(2)}, u32[]{:S(2)}) collective-permute-start(f32[4,32,128]{2,1,0:T(8,128)S(1)} %get-tuple-element.22), channel_id=1, source_target_pairs={{0,24},{8,16},{16,8},{24,0},{1,25},{9,17},{17,9},{25,1},{2,26},{10... | collective-permute-start | bytes 196616 | tf_op jit(solution)/shard_map/ppermute | solution.py:31
  26.4 5.2 %collective-permute-start.3 = (f32[4,32,128]{2,1,0:T(8,128)S(1)}, f32[4,32,128]{2,1,0:T(8,128)S(1)}, u32[]{:S(2)}, u32[]{:S(2)}) collective-permute-start(f32[4,32,128]{2,1,0:T(8,128)S(1)} %get-tuple-element.20), channel_id=1, source_target_pairs={{0,8},{8,0},{16,24},{24,16},{1,9},{9,1},{17,25},{25,17},{2,10},{10... | collective-permute-start | bytes 196616 | tf_op jit(solution)/shard_map/ppermute | solution.py:31
  26.9 4.9 %collective-permute-start.4 = (f32[4,32,128]{2,1,0:T(8,128)S(1)}, f32[4,32,128]{2,1,0:T(8,128)S(1)}, u32[]{:S(2)}, u32[]{:S(2)}) collective-permute-start(f32[4,32,128]{2,1,0:T(8,128)S(1)} %get-tuple-element.21), channel_id=1, source_target_pairs={{0,16},{8,24},{16,0},{24,8},{1,17},{9,25},{17,1},{25,9},{2,18},{10... | collective-permute-start | bytes 196616 | tf_op jit(solution)/shard_map/ppermute | solution.py:31

commit v10 on v7

--- a/solution.py
+++ b/solution.py
@@ -19,7 +19,7 @@
 
 def partner(index, step, peers):
     if peers & (peers - 1) == 0:
-        return index ^ step
+        return index ^ (peers - 1 - step if 0 < step < peers - 1 else step)
     return lax.rem(index + step, peers) if not isinstance(index, int) else (index + step) % peers
 
 

time: 33.5 us -> 33.5 us (level)
  transfers between devices with their start and end apart: 8 -> 8, of which waited for: 6 -> 5; matrix products, arithmetic and copies ran while one was open for 0% -> 0% of each run, Pallas kernels for 0% -> 0%
where the time goes in v10:
time: 33.5 us; the launch traced here: 33.1 us
  starting transfers between devices  18.8 us (56%)
  waiting for transfers between devices  9.51 us (28%)
  Pallas kernels  4.03 us (12%)
  between operations  0.67 us (2%)
    ppermute x6, starting transfers between devices, exchange(): lax.ppermute(value, 'lat', [(i, partner(i, step, peers)) for i in range(p...  10.8 us
    ppermute x6, waiting for transfers between devices, exchange(): lax.ppermute(value, 'lat', [(i, partner(i, step, peers)) for i in range(p...  9.03 us
    all_to_all x2, starting transfers between devices, to_all(): lax.all_to_all(blocks, ('lat', 'lon'), 0, 0, tiled=True)  8.03 us
    pallas_call x1, Pallas kernels, split_heads_body(): vmem_call(functools.partial(attention_kernel, bands, sectors, width, keys...  1.69 us
    pallas_call x1, Pallas kernels, split_heads_body(): pl.pallas_call(functools.partial(pack_kernel, bands, sectors, width, keys...  1.55 us
    pallas_call x1, Pallas kernels, split_heads_body(): pl.pallas_call(functools.partial(finish_kernel, bands, sectors, width, ke...  0.78 us
  transfers between devices with their start and end apart: 8, of which 5 were waited for; matrix products, arithmetic and copies ran while one was open for 0% of the time, Pallas kernels for 0%

profile of v10, /device:TPU:0, one launch (start us, length us, event | category | flops | bytes accessed | tf_op | source)
XLA Modules:
  0.0 33.1 jit_solution(372257197069944343)
XLA Ops:
  0.6 1.6 %shard_map.84 = (f32[192,128]{1,0:T(8,128)}, f32[2,4,32,128]{3,2,1,0:T(8,128)S(1)}, f32[2,4,32,128]{3,2,1,0:T(8,128)S(1)}, f32[2,4,32,128]{3,2,1,0:T(8,128)S(1)}, f32[2,4,32,128]{3,2,1,0:T(8,128)S(1)}) custom-call(f32[1,512]{1,0:T(1,128)} %refs_0_.1, f32[1,512]{1,0:T(1,128)} %refs_1_.1, f32[4,32,512]{2,1,0:T(8,128)} %refs_2_.1, f32[4,32,512]{2,1,0:T(8,128)} %refs_3_.1), custom_call_target="tpu_custom_call" | custom-call | tf_op jit(solution)/shard_map/pallas_call | solution.py:367
  2.2 4.0 %collective-permute-start.2 = (f32[2,4,32,128]{3,2,1,0:T(8,128)S(1)}, f32[2,4,32,128]{3,2,1,0:T(8,128)S(1)}, u32[]{:S(2)}, u32[]{:S(2)}) collective-permute-start(f32[2,4,32,128]{3,2,1,0:T(8,128)S(1)} %get-tuple-element.17), channel_id=1, source_target_pairs={{0,24},{8,16},{16,8},{24,0},{1,25},{9,17},{17,9},{25,1},{2,26},{10... | collective-permute-start | bytes 393224 | tf_op jit(solution)/shard_map/ppermute | solution.py:31
  6.1 4.0 %all-to-all-start = ((f32[32,6,1,128]{3,2,1,0:T(1,128)}), f32[32,6,1,128]{3,2,1,0:T(1,128)S(1)}, u32[]{:S(2)}, u32[]{:S(2)}) async-start(f32[32,6,1,128]{3,2,1,0:T(1,128)} %bitcast), calls=%async_computation | async-start | bytes 196608 | tf_op jit(solution)/shard_map/all_to_all | solution.py:37
  10.1 1.8 %collective-permute-start = (f32[2,4,32,128]{3,2,1,0:T(8,128)S(1)}, f32[2,4,32,128]{3,2,1,0:T(8,128)S(1)}, u32[]{:S(2)}, u32[]{:S(2)}) collective-permute-start(f32[2,4,32,128]{3,2,1,0:T(8,128)S(1)} %get-tuple-element.15), channel_id=1, source_target_pairs={{0,16},{8,24},{16,0},{24,8},{1,17},{9,25},{17,1},{25,9},{2,18},{10... | collective-permute-start | bytes 393224 | tf_op jit(solution)/shard_map/ppermute | solution.py:31
  12.0 0.0 copy-start
  12.0 1.5 %collective-permute-start.1 = (f32[2,4,32,128]{3,2,1,0:T(8,128)S(1)}, f32[2,4,32,128]{3,2,1,0:T(8,128)S(1)}, u32[]{:S(2)}, u32[]{:S(2)}) collective-permute-start(f32[2,4,32,128]{3,2,1,0:T(8,128)S(1)} %get-tuple-element.16), channel_id=1, source_target_pairs={{0,8},{8,0},{16,24},{24,16},{1,9},{9,1},{17,25},{25,17},{2,10},{10... | collective-permute-start | bytes 393224 | tf_op jit(solution)/shard_map/ppermute | solution.py:31
  13.4 0.0 collective-permute-done.2.part_ref
  13.4 3.3 %collective-permute-done.refs_1_ = f32[2,4,32,128]{3,2,1,0:T(8,128)S(1)} collective-permute-done((f32[2,4,32,128]{3,2,1,0:T(8,128)S(1)}, f32[2,4,32,128]{3,2,1,0:T(8,128)S(1)}, u32[]{:S(2)}, u32[]{:S(2)}) %collective-permute-start) | collective-permute-done | bytes 131104 | tf_op jit(solution)/shard_map/ppermute | solution.py:31
  16.8 1.1 %collective-permute-done.1.refs_2_ = f32[2,4,32,128]{3,2,1,0:T(8,128)S(1)} collective-permute-done((f32[2,4,32,128]{3,2,1,0:T(8,128)S(1)}, f32[2,4,32,128]{3,2,1,0:T(8,128)S(1)}, u32[]{:S(2)}, u32[]{:S(2)}) %collective-permute-start.1) | collective-permute-done | bytes 131104 | tf_op jit(solution)/shard_map/ppermute | solution.py:31
  17.9 0.0 all-to-all-done
  17.9 0.0 copy-done
  17.9 1.7 %shard_map.86 = (f32[352,128]{1,0:T(8,128)}, f32[4,32,128]{2,1,0:T(8,128)S(1)}, f32[4,32,128]{2,1,0:T(8,128)S(1)}, f32[4,32,128]{2,1,0:T(8,128)S(1)}, f32[4,32,128]{2,1,0:T(8,128)S(1)}) custom-call(f32[2,4,32,128]{3,2,1,0:T(8,128)S(1)} %get-tuple-element.14.refs_0_, f32[2,4,32,128]{3,2,1,0:T(8,128)S(1)} %collective-permute-done.refs_1_, ...), custom_call_target="tpu_custom_call" | custom-call | tf_op jit(solution)/shard_map/pallas_call | solution.py:390
  19.6 4.1 %all-to-all-start.1 = ((f32[32,11,1,128]{3,2,1,0:T(1,128)}), f32[32,11,1,128]{3,2,1,0:T(1,128)S(1)}, u32[]{:S(2)}, u32[]{:S(2)}) async-start(f32[32,11,1,128]{3,2,1,0:T(1,128)} %bitcast.2), calls=%async_computation.1 | async-start | bytes 360448 | tf_op jit(solution)/shard_map/all_to_all | solution.py:37
  23.7 2.7 %collective-permute-start.5 = (f32[4,32,128]{2,1,0:T(8,128)S(1)}, f32[4,32,128]{2,1,0:T(8,128)S(1)}, u32[]{:S(2)}, u32[]{:S(2)}) collective-permute-start(f32[4,32,128]{2,1,0:T(8,128)S(1)} %get-tuple-element.22), channel_id=1, source_target_pairs={{0,24},{8,16},{16,8},{24,0},{1,25},{9,17},{17,9},{25,1},{2,26},{10... | collective-permute-start | bytes 196616 | tf_op jit(solution)/shard_map/ppermute | solution.py:31
  26.4 0.6 %collective-permute-start.3 = (f32[4,32,128]{2,1,0:T(8,128)S(1)}, f32[4,32,128]{2,1,0:T(8,128)S(1)}, u32[]{:S(2)}, u32[]{:S(2)}) collective-permute-start(f32[4,32,128]{2,1,0:T(8,128)S(1)} %get-tuple-element.20), channel_id=1, source_target_pairs={{0,16},{8,24},{16,0},{24,8},{1,17},{9,25},{17,1},{25,9},{2,18},{10... | collective-permute-start | bytes 196616 | tf_op jit(solution)/shard_map/ppermute | solution.py:31
  27.0 0.3 collective-permute-start.4
  27.2 2.8 %collective-permute-done.5.part_ref = f32[4,32,128]{2,1,0:T(8,128)S(1)} collective-permute-done((f32[4,32,128]{2,1,0:T(8,128)S(1)}, f32[4,32,128]{2,1,0:T(8,128)S(1)}, u32[]{:S(2)}, u32[]{:S(2)}) %collective-permute-start.5) | collective-permute-done | bytes 65568 | tf_op jit(solution)/shard_map/ppermute | solution.py:31
  30.0 1.8 %collective-permute-done.3.refs_1_ = f32[4,32,128]{2,1,0:T(8,128)S(1)} collective-permute-done((f32[4,32,128]{2,1,0:T(8,128)S(1)}, f32[4,32,128]{2,1,0:T(8,128)S(1)}, u32[]{:S(2)}, u32[]{:S(2)}) %collective-permute-start.3) | collective-permute-done | bytes 65568 | tf_op jit(solution)/shard_map/ppermute | solution.py:31
  31.8 0.0 collective-permute-done.4.refs_2_
  31.8 0.5 %all-to-all-done.1 = f32[32,11,1,128]{3,2,1,0:T(1,128)S(1)} async-done(((f32[32,11,1,128]{3,2,1,0:T(1,128)}), f32[32,11,1,128]{3,2,1,0:T(1,128)S(1)}, u32[]{:S(2)}, u32[]{:S(2)}) %all-to-all-start.1) | async-done | bytes 180256 | tf_op jit(solution)/shard_map/all_to_all | solution.py:37
  32.3 0.8 %shard_map.88 = (f32[4,32,512]{2,1,0:T(8,128)}, f32[1,512]{1,0:T(1,128)}, f32[1,512]{1,0:T(1,128)}, f32[9,512]{1,0:T(8,128)}) custom-call(f32[4,32,128]{2,1,0:T(8,128)S(1)} %get-tuple-element.19.refs_0_, f32[4,32,128]{2,1,0:T(8,128)S(1)} %collective-permute-done.3.refs_1_, f32[4,32,128]{2,1,0:T(8,128)S(1)} %collective-permute-done.4.refs_2_, ...), custom_call_target="tpu_custom_call" | custom-call | tf_op jit(solution)/shard_map/pallas_call | solution.py:403
  (2 shorter events, 0.0 us)
Async XLA Ops:
  2.2 11.2 %collective-permute-start.2 = (f32[2,4,32,128]{3,2,1,0:T(8,128)S(1)}, f32[2,4,32,128]{3,2,1,0:T(8,128)S(1)}, u32[]{:S(2)}, u32[]{:S(2)}) collective-permute-start(f32[2,4,32,128]{3,2,1,0:T(8,128)S(1)} %get-tuple-element.17), channel_id=1, source_target_pairs={{0,24},{8,16},{16,8},{24,0},{1,25},{9,17},{17,9},{25,1},{2,26},{10... | collective-permute-start | bytes 393224 | tf_op jit(solution)/shard_map/ppermute | solution.py:31
  6.1 11.8 %all-to-all-start = ((f32[32,6,1,128]{3,2,1,0:T(1,128)}), f32[32,6,1,128]{3,2,1,0:T(1,128)S(1)}, u32[]{:S(2)}, u32[]{:S(2)}) async-start(f32[32,6,1,128]{3,2,1,0:T(1,128)} %bitcast), calls=%async_computation | async-start | bytes 196608 | tf_op jit(solution)/shard_map/all_to_all | solution.py:37
  10.1 6.6 %collective-permute-start = (f32[2,4,32,128]{3,2,1,0:T(8,128)S(1)}, f32[2,4,32,128]{3,2,1,0:T(8,128)S(1)}, u32[]{:S(2)}, u32[]{:S(2)}) collective-permute-start(f32[2,4,32,128]{3,2,1,0:T(8,128)S(1)} %get-tuple-element.15), channel_id=1, source_target_pairs={{0,16},{8,24},{16,0},{24,8},{1,17},{9,25},{17,1},{25,9},{2,18},{10... | collective-permute-start | bytes 393224 | tf_op jit(solution)/shard_map/ppermute | solution.py:31
  12.0 5.9 %copy-start = (f32[9,512]{1,0:T(8,128)S(1)}, f32[9,512]{1,0:T(8,128)}, u32[]{:S(2)}) copy-start(f32[9,512]{1,0:T(8,128)} %refs_5_.1) | copy-start | bytes 55300
  12.0 5.9 %collective-permute-start.1 = (f32[2,4,32,128]{3,2,1,0:T(8,128)S(1)}, f32[2,4,32,128]{3,2,1,0:T(8,128)S(1)}, u32[]{:S(2)}, u32[]{:S(2)}) collective-permute-start(f32[2,4,32,128]{3,2,1,0:T(8,128)S(1)} %get-tuple-element.16), channel_id=1, source_target_pairs={{0,8},{8,0},{16,24},{24,16},{1,9},{9,1},{17,25},{25,17},{2,10},{10... | collective-permute-start | bytes 393224 | tf_op jit(solution)/shard_map/ppermute | solution.py:31
  19.6 12.7 %all-to-all-start.1 = ((f32[32,11,1,128]{3,2,1,0:T(1,128)}), f32[32,11,1,128]{3,2,1,0:T(1,128)S(1)}, u32[]{:S(2)}, u32[]{:S(2)}) async-start(f32[32,11,1,128]{3,2,1,0:T(1,128)} %bitcast.2), calls=%async_computation.1 | async-start | bytes 360448 | tf_op jit(solution)/shard_map/all_to_all | solution.py:37
  23.7 6.3 %collective-permute-start.5 = (f32[4,32,128]{2,1,0:T(8,128)S(1)}, f32[4,32,128]{2,1,0:T(8,128)S(1)}, u32[]{:S(2)}, u32[]{:S(2)}) collective-permute-start(f32[4,32,128]{2,1,0:T(8,128)S(1)} %get-tuple-element.22), channel_id=1, source_target_pairs={{0,24},{8,16},{16,8},{24,0},{1,25},{9,17},{17,9},{25,1},{2,26},{10... | collective-permute-start | bytes 196616 | tf_op jit(solution)/shard_map/ppermute | solution.py:31
  26.4 5.4 %collective-permute-start.3 = (f32[4,32,128]{2,1,0:T(8,128)S(1)}, f32[4,32,128]{2,1,0:T(8,128)S(1)}, u32[]{:S(2)}, u32[]{:S(2)}) collective-permute-start(f32[4,32,128]{2,1,0:T(8,128)S(1)} %get-tuple-element.20), channel_id=1, source_target_pairs={{0,16},{8,24},{16,0},{24,8},{1,17},{9,25},{17,1},{25,9},{2,18},{10... | collective-permute-start | bytes 196616 | tf_op jit(solution)/shard_map/ppermute | solution.py:31
  27.0 4.8 %collective-permute-start.4 = (f32[4,32,128]{2,1,0:T(8,128)S(1)}, f32[4,32,128]{2,1,0:T(8,128)S(1)}, u32[]{:S(2)}, u32[]{:S(2)}) collective-permute-start(f32[4,32,128]{2,1,0:T(8,128)S(1)} %get-tuple-element.21), channel_id=1, source_target_pairs={{0,8},{8,0},{16,24},{24,16},{1,9},{9,1},{17,25},{25,17},{2,10},{10... | collective-permute-start | bytes 196616 | tf_op jit(solution)/shard_map/ppermute | solution.py:31

commit v11 on v9

--- a/solution.py
+++ b/solution.py
@@ -19,7 +19,7 @@
 
 def partner(index, step, peers):
     if peers & (peers - 1) == 0:
-        return index ^ step
+        return index ^ (peers - 1 - step if 0 < step < peers - 1 else step)
     return lax.rem(index + step, peers) if not isinstance(index, int) else (index + step) % peers
 
 

time: 33.5 us -> 33.5 us (level)
  transfers between devices with their start and end apart: 8 -> 8, of which waited for: 6 -> 5; matrix products, arithmetic and copies ran while one was open for 0% -> 0% of each run, Pallas kernels for 0% -> 0%
where the time goes in v11:
time: 33.5 us; the launch traced here: 33 us
  starting transfers between devices  18.8 us (56%)
  waiting for transfers between devices  9.51 us (28%)
  Pallas kernels  4.03 us (12%)
  between operations  0.67 us (2%)
    ppermute x6, starting transfers between devices, exchange(): lax.ppermute(value, 'lat', [(i, partner(i, step, peers)) for i in range(p...  10.8 us
    ppermute x6, waiting for transfers between devices, exchange(): lax.ppermute(value, 'lat', [(i, partner(i, step, peers)) for i in range(p...  9.03 us
    all_to_all x2, starting transfers between devices, to_all(): lax.all_to_all(blocks, ('lat', 'lon'), 0, 0, tiled=True)  8.03 us
    pallas_call x1, Pallas kernels, split_heads_body(): vmem_call(functools.partial(attention_kernel, bands, sectors, width, keys...  1.69 us
    pallas_call x1, Pallas kernels, split_heads_body(): pl.pallas_call(functools.partial(pack_kernel, bands, sectors, width, keys...  1.55 us
    pallas_call x1, Pallas kernels, split_heads_body(): pl.pallas_call(functools.partial(finish_kernel, bands, sectors, width, ke...  0.77 us
  transfers between devices with their start and end apart: 8, of which 5 were waited for; matrix products, arithmetic and copies ran while one was open for 0% of the time, Pallas kernels for 0%

profile of v11, /device:TPU:0, one launch (start us, length us, event | category | flops | bytes accessed | tf_op | source)
XLA Modules:
  0.0 33.0 jit_solution(2211304563826578852)
XLA Ops:
  0.6 1.6 %shard_map.84 = (f32[192,128]{1,0:T(8,128)}, f32[2,4,32,128]{3,2,1,0:T(8,128)S(1)}, f32[2,4,32,128]{3,2,1,0:T(8,128)S(1)}, f32[2,4,32,128]{3,2,1,0:T(8,128)S(1)}, f32[2,4,32,128]{3,2,1,0:T(8,128)S(1)}) custom-call(f32[1,512]{1,0:T(1,128)} %refs_0_.1, f32[1,512]{1,0:T(1,128)} %refs_1_.1, f32[4,32,512]{2,1,0:T(8,128)} %refs_2_.1, f32[4,32,512]{2,1,0:T(8,128)} %refs_3_.1), custom_call_target="tpu_custom_call" | custom-call | tf_op jit(solution)/shard_map/pallas_call | solution.py:370
  2.2 4.0 %collective-permute-start.2 = (f32[2,4,32,128]{3,2,1,0:T(8,128)S(1)}, f32[2,4,32,128]{3,2,1,0:T(8,128)S(1)}, u32[]{:S(2)}, u32[]{:S(2)}) collective-permute-start(f32[2,4,32,128]{3,2,1,0:T(8,128)S(1)} %get-tuple-element.17), channel_id=1, source_target_pairs={{0,24},{8,16},{16,8},{24,0},{1,25},{9,17},{17,9},{25,1},{2,26},{10... | collective-permute-start | bytes 393224 | tf_op jit(solution)/shard_map/ppermute | solution.py:31
  6.1 4.0 %all-to-all-start = ((f32[32,6,1,128]{3,2,1,0:T(1,128)}), f32[32,6,1,128]{3,2,1,0:T(1,128)S(1)}, u32[]{:S(2)}, u32[]{:S(2)}) async-start(f32[32,6,1,128]{3,2,1,0:T(1,128)} %bitcast), calls=%async_computation | async-start | bytes 196608 | tf_op jit(solution)/shard_map/all_to_all | solution.py:37
  10.1 1.8 %collective-permute-start = (f32[2,4,32,128]{3,2,1,0:T(8,128)S(1)}, f32[2,4,32,128]{3,2,1,0:T(8,128)S(1)}, u32[]{:S(2)}, u32[]{:S(2)}) collective-permute-start(f32[2,4,32,128]{3,2,1,0:T(8,128)S(1)} %get-tuple-element.15), channel_id=1, source_target_pairs={{0,16},{8,24},{16,0},{24,8},{1,17},{9,25},{17,1},{25,9},{2,18},{10... | collective-permute-start | bytes 393224 | tf_op jit(solution)/shard_map/ppermute | solution.py:31
  12.0 0.0 copy-start
  12.0 1.5 %collective-permute-start.1 = (f32[2,4,32,128]{3,2,1,0:T(8,128)S(1)}, f32[2,4,32,128]{3,2,1,0:T(8,128)S(1)}, u32[]{:S(2)}, u32[]{:S(2)}) collective-permute-start(f32[2,4,32,128]{3,2,1,0:T(8,128)S(1)} %get-tuple-element.16), channel_id=1, source_target_pairs={{0,8},{8,0},{16,24},{24,16},{1,9},{9,1},{17,25},{25,17},{2,10},{10... | collective-permute-start | bytes 393224 | tf_op jit(solution)/shard_map/ppermute | solution.py:31
  13.4 0.0 collective-permute-done.2.part_ref
  13.4 3.3 %collective-permute-done.refs_1_ = f32[2,4,32,128]{3,2,1,0:T(8,128)S(1)} collective-permute-done((f32[2,4,32,128]{3,2,1,0:T(8,128)S(1)}, f32[2,4,32,128]{3,2,1,0:T(8,128)S(1)}, u32[]{:S(2)}, u32[]{:S(2)}) %collective-permute-start) | collective-permute-done | bytes 131104 | tf_op jit(solution)/shard_map/ppermute | solution.py:31
  16.8 1.1 %collective-permute-done.1.refs_2_ = f32[2,4,32,128]{3,2,1,0:T(8,128)S(1)} collective-permute-done((f32[2,4,32,128]{3,2,1,0:T(8,128)S(1)}, f32[2,4,32,128]{3,2,1,0:T(8,128)S(1)}, u32[]{:S(2)}, u32[]{:S(2)}) %collective-permute-start.1) | collective-permute-done | bytes 131104 | tf_op jit(solution)/shard_map/ppermute | solution.py:31
  17.9 0.0 all-to-all-done
  17.9 0.0 copy-done
  17.9 1.7 %shard_map.86 = (f32[352,128]{1,0:T(8,128)}, f32[4,32,128]{2,1,0:T(8,128)S(1)}, f32[4,32,128]{2,1,0:T(8,128)S(1)}, f32[4,32,128]{2,1,0:T(8,128)S(1)}, f32[4,32,128]{2,1,0:T(8,128)S(1)}) custom-call(f32[2,4,32,128]{3,2,1,0:T(8,128)S(1)} %get-tuple-element.14.refs_0_, f32[2,4,32,128]{3,2,1,0:T(8,128)S(1)} %collective-permute-done.refs_1_, ...), custom_call_target="tpu_custom_call" | custom-call | tf_op jit(solution)/shard_map/pallas_call | solution.py:393
  19.6 4.1 %all-to-all-start.1 = ((f32[32,11,1,128]{3,2,1,0:T(1,128)}), f32[32,11,1,128]{3,2,1,0:T(1,128)S(1)}, u32[]{:S(2)}, u32[]{:S(2)}) async-start(f32[32,11,1,128]{3,2,1,0:T(1,128)} %bitcast.2), calls=%async_computation.1 | async-start | bytes 360448 | tf_op jit(solution)/shard_map/all_to_all | solution.py:37
  23.7 2.7 %collective-permute-start.5 = (f32[4,32,128]{2,1,0:T(8,128)S(1)}, f32[4,32,128]{2,1,0:T(8,128)S(1)}, u32[]{:S(2)}, u32[]{:S(2)}) collective-permute-start(f32[4,32,128]{2,1,0:T(8,128)S(1)} %get-tuple-element.22), channel_id=1, source_target_pairs={{0,24},{8,16},{16,8},{24,0},{1,25},{9,17},{17,9},{25,1},{2,26},{10... | collective-permute-start | bytes 196616 | tf_op jit(solution)/shard_map/ppermute | solution.py:31
  26.4 0.6 %collective-permute-start.3 = (f32[4,32,128]{2,1,0:T(8,128)S(1)}, f32[4,32,128]{2,1,0:T(8,128)S(1)}, u32[]{:S(2)}, u32[]{:S(2)}) collective-permute-start(f32[4,32,128]{2,1,0:T(8,128)S(1)} %get-tuple-element.20), channel_id=1, source_target_pairs={{0,16},{8,24},{16,0},{24,8},{1,17},{9,25},{17,1},{25,9},{2,18},{10... | collective-permute-start | bytes 196616 | tf_op jit(solution)/shard_map/ppermute | solution.py:31
  27.0 0.3 collective-permute-start.4
  27.2 2.8 %collective-permute-done.5.part_ref = f32[4,32,128]{2,1,0:T(8,128)S(1)} collective-permute-done((f32[4,32,128]{2,1,0:T(8,128)S(1)}, f32[4,32,128]{2,1,0:T(8,128)S(1)}, u32[]{:S(2)}, u32[]{:S(2)}) %collective-permute-start.5) | collective-permute-done | bytes 65568 | tf_op jit(solution)/shard_map/ppermute | solution.py:31
  30.0 1.8 %collective-permute-done.3.refs_1_ = f32[4,32,128]{2,1,0:T(8,128)S(1)} collective-permute-done((f32[4,32,128]{2,1,0:T(8,128)S(1)}, f32[4,32,128]{2,1,0:T(8,128)S(1)}, u32[]{:S(2)}, u32[]{:S(2)}) %collective-permute-start.3) | collective-permute-done | bytes 65568 | tf_op jit(solution)/shard_map/ppermute | solution.py:31
  31.8 0.0 collective-permute-done.4.refs_2_
  31.8 0.5 %all-to-all-done.1 = f32[32,11,1,128]{3,2,1,0:T(1,128)S(1)} async-done(((f32[32,11,1,128]{3,2,1,0:T(1,128)}), f32[32,11,1,128]{3,2,1,0:T(1,128)S(1)}, u32[]{:S(2)}, u32[]{:S(2)}) %all-to-all-start.1) | async-done | bytes 180256 | tf_op jit(solution)/shard_map/all_to_all | solution.py:37
  32.3 0.8 %shard_map.88 = (f32[4,32,512]{2,1,0:T(8,128)}, f32[1,512]{1,0:T(1,128)}, f32[1,512]{1,0:T(1,128)}, f32[9,512]{1,0:T(8,128)}) custom-call(f32[4,32,128]{2,1,0:T(8,128)S(1)} %get-tuple-element.19.refs_0_, f32[4,32,128]{2,1,0:T(8,128)S(1)} %collective-permute-done.3.refs_1_, f32[4,32,128]{2,1,0:T(8,128)S(1)} %collective-permute-done.4.refs_2_, ...), custom_call_target="tpu_custom_call" | custom-call | tf_op jit(solution)/shard_map/pallas_call | solution.py:406
  (2 shorter events, 0.0 us)
Async XLA Ops:
  2.2 11.2 %collective-permute-start.2 = (f32[2,4,32,128]{3,2,1,0:T(8,128)S(1)}, f32[2,4,32,128]{3,2,1,0:T(8,128)S(1)}, u32[]{:S(2)}, u32[]{:S(2)}) collective-permute-start(f32[2,4,32,128]{3,2,1,0:T(8,128)S(1)} %get-tuple-element.17), channel_id=1, source_target_pairs={{0,24},{8,16},{16,8},{24,0},{1,25},{9,17},{17,9},{25,1},{2,26},{10... | collective-permute-start | bytes 393224 | tf_op jit(solution)/shard_map/ppermute | solution.py:31
  6.1 11.8 %all-to-all-start = ((f32[32,6,1,128]{3,2,1,0:T(1,128)}), f32[32,6,1,128]{3,2,1,0:T(1,128)S(1)}, u32[]{:S(2)}, u32[]{:S(2)}) async-start(f32[32,6,1,128]{3,2,1,0:T(1,128)} %bitcast), calls=%async_computation | async-start | bytes 196608 | tf_op jit(solution)/shard_map/all_to_all | solution.py:37
  10.1 6.6 %collective-permute-start = (f32[2,4,32,128]{3,2,1,0:T(8,128)S(1)}, f32[2,4,32,128]{3,2,1,0:T(8,128)S(1)}, u32[]{:S(2)}, u32[]{:S(2)}) collective-permute-start(f32[2,4,32,128]{3,2,1,0:T(8,128)S(1)} %get-tuple-element.15), channel_id=1, source_target_pairs={{0,16},{8,24},{16,0},{24,8},{1,17},{9,25},{17,1},{25,9},{2,18},{10... | collective-permute-start | bytes 393224 | tf_op jit(solution)/shard_map/ppermute | solution.py:31
  12.0 5.9 %copy-start = (f32[9,512]{1,0:T(8,128)S(1)}, f32[9,512]{1,0:T(8,128)}, u32[]{:S(2)}) copy-start(f32[9,512]{1,0:T(8,128)} %refs_5_.1) | copy-start | bytes 55300
  12.0 5.9 %collective-permute-start.1 = (f32[2,4,32,128]{3,2,1,0:T(8,128)S(1)}, f32[2,4,32,128]{3,2,1,0:T(8,128)S(1)}, u32[]{:S(2)}, u32[]{:S(2)}) collective-permute-start(f32[2,4,32,128]{3,2,1,0:T(8,128)S(1)} %get-tuple-element.16), channel_id=1, source_target_pairs={{0,8},{8,0},{16,24},{24,16},{1,9},{9,1},{17,25},{25,17},{2,10},{10... | collective-permute-start | bytes 393224 | tf_op jit(solution)/shard_map/ppermute | solution.py:31
  19.6 12.7 %all-to-all-start.1 = ((f32[32,11,1,128]{3,2,1,0:T(1,128)}), f32[32,11,1,128]{3,2,1,0:T(1,128)S(1)}, u32[]{:S(2)}, u32[]{:S(2)}) async-start(f32[32,11,1,128]{3,2,1,0:T(1,128)} %bitcast.2), calls=%async_computation.1 | async-start | bytes 360448 | tf_op jit(solution)/shard_map/all_to_all | solution.py:37
  23.7 6.3 %collective-permute-start.5 = (f32[4,32,128]{2,1,0:T(8,128)S(1)}, f32[4,32,128]{2,1,0:T(8,128)S(1)}, u32[]{:S(2)}, u32[]{:S(2)}) collective-permute-start(f32[4,32,128]{2,1,0:T(8,128)S(1)} %get-tuple-element.22), channel_id=1, source_target_pairs={{0,24},{8,16},{16,8},{24,0},{1,25},{9,17},{17,9},{25,1},{2,26},{10... | collective-permute-start | bytes 196616 | tf_op jit(solution)/shard_map/ppermute | solution.py:31
  26.4 5.4 %collective-permute-start.3 = (f32[4,32,128]{2,1,0:T(8,128)S(1)}, f32[4,32,128]{2,1,0:T(8,128)S(1)}, u32[]{:S(2)}, u32[]{:S(2)}) collective-permute-start(f32[4,32,128]{2,1,0:T(8,128)S(1)} %get-tuple-element.20), channel_id=1, source_target_pairs={{0,16},{8,24},{16,0},{24,8},{1,17},{9,25},{17,1},{25,9},{2,18},{10... | collective-permute-start | bytes 196616 | tf_op jit(solution)/shard_map/ppermute | solution.py:31
  27.0 4.8 %collective-permute-start.4 = (f32[4,32,128]{2,1,0:T(8,128)S(1)}, f32[4,32,128]{2,1,0:T(8,128)S(1)}, u32[]{:S(2)}, u32[]{:S(2)}) collective-permute-start(f32[4,32,128]{2,1,0:T(8,128)S(1)} %get-tuple-element.21), channel_id=1, source_target_pairs={{0,8},{8,0},{16,24},{24,16},{1,9},{9,1},{17,25},{25,17},{2,10},{10... | collective-permute-start | bytes 196616 | tf_op jit(solution)/shard_map/ppermute | solution.py:31
